TPU v7x, 32 devices: a whole 2x2x4 slice. The times are simulated.
32 devices in a mesh: layer: 2 (over x), row: 4 (over y, core), col: 4 (over z).
Axes of the slice: x: 2, y: 2, z: 4, core: 2. Of those that a mesh axis runs over, the one named last changes fastest.
Arguments:
- reflect_fwd: float32 [2, 1024, 1024], P('layer', 'row', 'col'), may hold values from -1 to 1
- transmit_fwd: float32 [2, 1024, 1024], P('layer', 'row', 'col'), may hold values from -1 to 1
- reflect_bwd: float32 [2, 1024, 1024], P('layer', 'row', 'col'), may hold values from -1 to 1
- transmit_bwd: float32 [2, 1024, 1024], P('layer', 'row', 'col'), may hold values from -1 to 1
- material_ids: int32 [2], P('layer'), may hold values from 0 to 7
- interface_gain: float32 [8, 1024], replicated, may hold values from 0.5 to 1
Outputs:
- reflect_out: float32 [2, 1024, 1024], P('layer', 'row', 'col')
- transmit_out: float32 [2, 1024, 1024], P('layer', 'row', 'col')
All inputs are finite; a program needn't handle non-finite values.
Results may differ from a plain program's by a relative error of at most 0.00015.
Values sent between devices are 32-bit elements; how exact they have to be, the bound alone decides.
No kernel may reach another device: no remote copies, remote signals or barrier semaphores. Data moves between devices by JAX's collectives and lax.ppermute only.
A program may use at most 64 MiB of HBM per device.

v0:
```python
import jax
import jax.numpy as jnp
from jax import lax
from jax.sharding import PartitionSpec as P

NTERMS = 6


PRECISE = lax.Precision.HIGHEST


def partner(block, axis, stride):
    count = lax.axis_size(axis)
    route = []
    for low in range(count):
        high = low | 1 << stride
        if high != low and high < count:
            route += [(low, high), (high, low)]
    return lax.ppermute(block, axis, route)


def folder(panel, incoming):
    return jnp.dot(panel, incoming, precision=PRECISE, preferred_element_type=jnp.float32)


def folder_pair(first_panel, second_panel, incoming):
    return (
        jnp.dot(first_panel, incoming, precision=PRECISE, preferred_element_type=jnp.float32),
        jnp.dot(second_panel, incoming, precision=PRECISE, preferred_element_type=jnp.float32),
    )


def on_device(reflect_fwd, transmit_fwd, reflect_bwd, transmit_bwd, material_ids, interface_gain):
    reflect_own = reflect_fwd[0]
    transmit_own = transmit_fwd[0]
    reflect_back = reflect_bwd[0]
    transmit_back = transmit_bwd[0]
    rows_blk = reflect_own.shape[0]
    cols_blk = reflect_own.shape[1]
    materials = interface_gain.shape[0]
    selector = (material_ids[0] == jnp.arange(materials, dtype=jnp.int32)).astype(jnp.float32)
    own_gain = jnp.dot(selector[None, :], interface_gain, precision=PRECISE)[0]
    distance = lax.axis_size("layer") // 2
    partner_bit = distance.bit_length() - 1
    upper_side = lax.axis_index("layer") < distance
    other_reflect, other_transmit, other_back, other_tback, partner_gain = partner(
        (reflect_own, transmit_own, reflect_back, transmit_back, own_gain), "layer", partner_bit
    )
    reflect_a = jnp.where(upper_side, reflect_own, other_reflect)
    transmit_a = jnp.where(upper_side, transmit_own, other_transmit)
    back_a = jnp.where(upper_side, reflect_back, other_back)
    tback_a = jnp.where(upper_side, transmit_back, other_tback)
    reflect_b = jnp.where(upper_side, other_reflect, reflect_own)
    transmit_b = jnp.where(upper_side, other_transmit, transmit_own)
    weight = own_gain * partner_gain
    row_index = lax.axis_index("row")
    col_index = lax.axis_index("col")
    row_gain = lax.dynamic_slice_in_dim(weight, row_index * rows_blk, rows_blk)
    col_gain = lax.dynamic_slice_in_dim(weight, col_index * cols_blk, cols_blk)
    scaled_fwd = row_gain[:, None] * transmit_a
    scaled_bwd = tback_a * col_gain[None, :]
    global_rows = lax.broadcasted_iota(jnp.int32, (rows_blk, cols_blk), 0) + row_index * rows_blk
    global_cols = lax.broadcasted_iota(jnp.int32, (rows_blk, cols_blk), 1) + col_index * cols_blk
    eye_block = (global_rows == global_cols).astype(jnp.float32)
    back_rows, bwd_rows = (
        lax.all_gather(back_a, "col", axis=1, tiled=True),
        lax.all_gather(scaled_bwd, "col", axis=1, tiled=True),
    )
    power_term, side_term = folder_pair(
        back_rows, bwd_rows, lax.all_gather(reflect_b, "row", axis=0, tiled=True)
    )
    power_rows = lax.all_gather(power_term, "col", axis=1, tiled=True)
    series = eye_block + power_term
    for repeat in range(NTERMS - 2):
        series = eye_block + folder(power_rows, lax.all_gather(series, "row", axis=0, tiled=True))
    series_panel = lax.all_gather(series, "col", axis=1, tiled=True)
    middle = folder(series_panel, lax.all_gather(scaled_fwd, "row", axis=0, tiled=True))
    lower_rows, side_rows = (
        lax.all_gather(transmit_b, "col", axis=1, tiled=True),
        lax.all_gather(side_term, "col", axis=1, tiled=True),
    )
    trans_out, bounce = folder_pair(
        lower_rows, side_rows, lax.all_gather(middle, "row", axis=0, tiled=True)
    )
    refl_out = reflect_a + bounce
    return (refl_out[None], trans_out[None])


def solution(mesh):
    placed = (
        P("layer", "row", "col"),
        P("layer", "row", "col"),
        P("layer", "row", "col"),
        P("layer", "row", "col"),
        P("layer"),
        P(),
    )
    return jax.shard_map(
        on_device,
        mesh=mesh,
        in_specs=placed,
        out_specs=(P("layer", "row", "col"), P("layer", "row", "col")),
        check_vma=False,
    )
```

profile of v0, /device:TPU:0, one launch (start us, length us, event | category | flops | bytes accessed | tf_op | source)
XLA Modules:
  0.0 340.2 jit_solution(9179813378292550181)
XLA Ops:
  7.2 3.0 collective-permute-start
  10.2 6.5 %collective-permute-done = f32[256,256]{1,0:T(8,128)S(1)} collective-permute-done((f32[256,256]{1,0:T(8,128)}, f32[256,256]{1,0:T(8,128)S(1)}, u32[]{:S(2)}, u32[]{:S(2)}) %collective-permute-start) | collective-permute-done | bytes 262176 | tf_op jit(solution)/shard_map/ppermute | solution.py:19
  21.1 5.8 %collective-permute-done.3 = f32[256,256]{1,0:T(8,128)S(1)} collective-permute-done((f32[256,256]{1,0:T(8,128)S(1)}, f32[256,256]{1,0:T(8,128)S(1)}, u32[]{:S(2)}, u32[]{:S(2)}) %collective-permute-start.3) | collective-permute-done | bytes 262176 | tf_op jit(solution)/shard_map/ppermute | solution.py:19
  27.7 9.1 %all-gather.16.cloned.1.call-done = f32[1024,256]{1,0:T(8,128)} async-done(((f32[256,256]{1,0:T(8,128)}), f32[1024,256]{1,0:T(8,128)}) %all-gather.16.cloned.1.call-update) | async-done | bytes 1048592 | tf_op jit(solution)/shard_map/all_gather | solution.py:70
  36.8 30.1 %all-gather.20.cloned.1.call-done = f32[256,1024]{1,0:T(8,128)} async-done(((f32[256,256]{1,0:T(8,128)}), f32[256,1024]{1,0:T(8,128)}) %all-gather.20.cloned.1.call-update) | async-done | bytes 1048592 | tf_op jit(solution)/shard_map/all_gather | solution.py:66
  66.9 3.4 convert_add_fusion
  70.9 27.0 %all-gather.22.cloned.1.call-done = f32[256,1024]{1,0:T(8,128)} async-done(((f32[256,256]{1,0:T(8,128)}), f32[256,1024]{1,0:T(8,128)}) %all-gather.22.cloned.1.call-update) | async-done | bytes 1048592 | tf_op jit(solution)/shard_map/all_gather | solution.py:72
  97.9 18.2 %all-gather.24.cloned.1.call-done = f32[1024,256]{1,0:T(8,128)} async-done(((f32[256,256]{1,0:T(8,128)}), f32[1024,256]{1,0:T(8,128)}) %all-gather.24.cloned.1.call-update) | async-done | bytes 1048592 | tf_op jit(solution)/shard_map/all_gather | solution.py:75
  116.1 3.3 convolution_add_fusion.3
  119.5 16.8 %all-gather.26.cloned.1.call-done = f32[1024,256]{1,0:T(8,128)} async-done(((f32[256,256]{1,0:T(8,128)}), f32[1024,256]{1,0:T(8,128)}) %all-gather.26.cloned.1.call-update) | async-done | bytes 1048592 | tf_op jit(solution)/shard_map/all_gather | solution.py:75
  136.3 3.0 convolution_add_fusion.2
  139.3 16.8 %all-gather.28.cloned.1.call-done = f32[1024,256]{1,0:T(8,128)} async-done(((f32[256,256]{1,0:T(8,128)}), f32[1024,256]{1,0:T(8,128)}) %all-gather.28.cloned.1.call-update) | async-done | bytes 1048592 | tf_op jit(solution)/shard_map/all_gather | solution.py:75
  163.0 5.6 %collective-permute-done.2 = f32[1024]{0:T(1024)S(1)} collective-permute-done((f32[1024]{0:T(1024)S(1)}, f32[1024]{0:T(1024)S(1)}, u32[]{:S(2)}, u32[]{:S(2)}) %collective-permute-start.2) | collective-permute-done | bytes 4128 | tf_op jit(solution)/shard_map/ppermute | solution.py:19
  169.6 6.4 %all-gather.30.cloned.1.call-done = f32[1024,256]{1,0:T(8,128)} async-done(((f32[256,256]{1,0:T(8,128)}), f32[1024,256]{1,0:T(8,128)}) %all-gather.30.cloned.1.call-update) | async-done | bytes 1048592 | tf_op jit(solution)/shard_map/all_gather | solution.py:75
  181.4 7.0 %collective-permute-done.1 = f32[256,256]{1,0:T(8,128)S(1)} collective-permute-done((f32[256,256]{1,0:T(8,128)S(1)}, f32[256,256]{1,0:T(8,128)S(1)}, u32[]{:S(2)}, u32[]{:S(2)}) %collective-permute-start.1) | collective-permute-done | bytes 262176 | tf_op jit(solution)/shard_map/ppermute | solution.py:19
  189.9 4.4 %all-gather.34.cloned.1.call-done = f32[1024,256]{1,0:T(8,128)} async-done(((f32[256,256]{1,0:T(8,128)}), f32[1024,256]{1,0:T(8,128)}) %all-gather.34.cloned.1.call-update) | async-done | bytes 1048592 | tf_op jit(solution)/shard_map/all_gather | solution.py:77
  194.4 30.1 %all-gather.32.cloned.1.call-done = f32[256,1024]{1,0:T(8,128)} async-done(((f32[256,256]{1,0:T(8,128)}), f32[256,1024]{1,0:T(8,128)}) %all-gather.32.cloned.1.call-update) | async-done | bytes 1048592 | tf_op jit(solution)/shard_map/all_gather | solution.py:76
  224.5 3.3 fusion.7
  227.8 26.1 %all-gather.14.cloned.1.call-done = f32[256,1024]{1,0:T(8,128)} async-done(((f32[256,256]{1,0:T(8,128)}), f32[256,1024]{1,0:T(8,128)}) %all-gather.14.cloned.1.call-update) | async-done | bytes 1048592 | tf_op jit(solution)/shard_map/all_gather | solution.py:67
  256.9 26.0 %all-gather.38.cloned.1.call-done = f32[256,1024]{1,0:T(8,128)} async-done(((f32[256,256]{1,0:T(8,128)}), f32[256,1024]{1,0:T(8,128)}) %all-gather.38.cloned.1.call-update) | async-done | bytes 1048592 | tf_op jit(solution)/shard_map/all_gather | solution.py:79
  283.0 17.7 %all-gather.36.cloned.1.call-done = f32[1024,256]{1,0:T(8,128)} async-done(((f32[256,256]{1,0:T(8,128)}), f32[1024,256]{1,0:T(8,128)}) %all-gather.36.cloned.1.call-update) | async-done | bytes 1048592 | tf_op jit(solution)/shard_map/all_gather | solution.py:83
  300.6 3.4 convolution_bitcast_fusion
  304.0 26.8 %all-gather.18.cloned.1.call-done = f32[256,1024]{1,0:T(8,128)} async-done(((f32[256,256]{1,0:T(8,128)}), f32[256,1024]{1,0:T(8,128)}) %all-gather.18.cloned.1.call-update) | async-done | bytes 1048592 | tf_op jit(solution)/shard_map/all_gather | solution.py:80
  330.7 2.9 add_bitcast_fusion
  (58 shorter events, 22.9 us)
Async XLA Ops:
  7.2 155.0 %copy-start = (f32[8,1024]{1,0:T(8,128)S(1)}, f32[8,1024]{1,0:T(8,128)}, u32[]{:S(2)}) copy-start(f32[8,1024]{1,0:T(8,128)} %param.11) | copy-start | bytes 98308
  7.2 29.7 %all-gather.16.cloned.1.call-start = ((), (), s32[]{:S(2)}) async-start(), calls=%async_computation.1 | async-start | bytes 1310720 | tf_op jit(solution)/shard_map/all_gather | solution.py:70
  7.2 9.5 %collective-permute-start = (f32[256,256]{1,0:T(8,128)}, f32[256,256]{1,0:T(8,128)S(1)}, u32[]{:S(2)}, u32[]{:S(2)}) collective-permute-start(f32[256,256]{1,0:T(8,128)} %bitcast.39), channel_id=1, source_target_pairs={{0,16},{16,0},{1,17},{17,1},{2,18},{18,2},{3,19},{19,3},{4,20},{20... | collective-permute-start | bytes 786440 | tf_op jit(solution)/shard_map/ppermute | solution.py:19
  18.4 0.9 copy-start.7
  18.5 48.5 %all-gather.20.cloned.1.call-start = ((), (), s32[]{:S(2)}) async-start(), calls=%async_computation.3 | async-start | bytes 1310720 | tf_op jit(solution)/shard_map/all_gather | solution.py:66
  19.4 7.5 %collective-permute-start.3 = (f32[256,256]{1,0:T(8,128)S(1)}, f32[256,256]{1,0:T(8,128)S(1)}, u32[]{:S(2)}, u32[]{:S(2)}) collective-permute-start(f32[256,256]{1,0:T(8,128)S(1)} %bitcast.42), channel_id=1, source_target_pairs={{0,16},{16,0},{1,17},{17,1},{2,18},{18,2},{3,19},{19,3},{4,20},{20... | collective-permute-start | bytes 786440 | tf_op jit(solution)/shard_map/ppermute | solution.py:19
  27.6 70.3 %all-gather.22.cloned.1.call-start = ((), (), s32[]{:S(2)}) async-start(), calls=%async_computation.4 | async-start | bytes 1310720 | tf_op jit(solution)/shard_map/all_gather | solution.py:72
  70.3 45.8 %all-gather.24.cloned.1.call-start = ((), (), s32[]{:S(2)}) async-start(), calls=%async_computation.5 | async-start | bytes 1310720 | tf_op jit(solution)/shard_map/all_gather | solution.py:75
  70.9 65.4 %all-gather.26.cloned.1.call-start = ((), (), s32[]{:S(2)}) async-start(), calls=%async_computation.6 | async-start | bytes 1310720 | tf_op jit(solution)/shard_map/all_gather | solution.py:75
  97.9 38.4 %copy-start.1 = (f32[256,1024]{1,0:T(8,128)S(1)}, f32[256,1024]{1,0:T(8,128)}, u32[]{:S(2)}) copy-start(f32[256,1024]{1,0:T(8,128)} %all-gather.22.cloned.1.call-done) | copy-start | bytes 3145732
  119.4 36.7 %all-gather.28.cloned.1.call-start = ((), (), s32[]{:S(2)}) async-start(), calls=%async_computation.7 | async-start | bytes 1310720 | tf_op jit(solution)/shard_map/all_gather | solution.py:75
  139.3 36.7 %all-gather.30.cloned.1.call-start = ((), (), s32[]{:S(2)}) async-start(), calls=%async_computation.8 | async-start | bytes 1310720 | tf_op jit(solution)/shard_map/all_gather | solution.py:75
  159.2 35.2 %all-gather.34.cloned.1.call-start = ((), (), s32[]{:S(2)}) async-start(), calls=%async_computation.10 | async-start | bytes 1310720 | tf_op jit(solution)/shard_map/all_gather | solution.py:77
  160.1 8.6 %collective-permute-start.4 = (f32[256,256]{1,0:T(8,128)S(1)}, f32[256,256]{1,0:T(8,128)S(1)}, u32[]{:S(2)}, u32[]{:S(2)}) collective-permute-start(f32[256,256]{1,0:T(8,128)S(1)} %bitcast.40), channel_id=1, source_target_pairs={{0,16},{16,0},{1,17},{17,1},{2,18},{18,2},{3,19},{19,3},{4,20},{20... | collective-permute-start | bytes 786440 | tf_op jit(solution)/shard_map/ppermute | solution.py:19
  162.3 6.3 %collective-permute-start.2 = (f32[1024]{0:T(1024)S(1)}, f32[1024]{0:T(1024)S(1)}, u32[]{:S(2)}, u32[]{:S(2)}) collective-permute-start(f32[1024]{0:T(1024)S(1)} %bitcast.43), channel_id=1, source_target_pairs={{0,16},{16,0},{1,17},{17,1},{2,18},{18,2},{3,19},{19,3},{4,20},{20... | collective-permute-start | bytes 12296 | tf_op jit(solution)/shard_map/ppermute | solution.py:19
  169.6 54.9 %all-gather.32.cloned.1.call-start = ((), (), s32[]{:S(2)}) async-start(), calls=%async_computation.9 | async-start | bytes 1310720 | tf_op jit(solution)/shard_map/all_gather | solution.py:76
  179.0 74.9 %all-gather.14.cloned.1.call-start = ((), (), s32[]{:S(2)}) async-start(), calls=%async_computation | async-start | bytes 1310720 | tf_op jit(solution)/shard_map/all_gather | solution.py:67
  179.9 8.4 %collective-permute-start.1 = (f32[256,256]{1,0:T(8,128)S(1)}, f32[256,256]{1,0:T(8,128)S(1)}, u32[]{:S(2)}, u32[]{:S(2)}) collective-permute-start(f32[256,256]{1,0:T(8,128)S(1)} %bitcast.41), channel_id=1, source_target_pairs={{0,16},{16,0},{1,17},{17,1},{2,18},{18,2},{3,19},{19,3},{4,20},{20... | collective-permute-start | bytes 786440 | tf_op jit(solution)/shard_map/ppermute | solution.py:19
  189.1 93.8 %all-gather.38.cloned.1.call-start = ((), (), s32[]{:S(2)}) async-start(), calls=%async_computation.12 | async-start | bytes 1310720 | tf_op jit(solution)/shard_map/all_gather | solution.py:79
  189.9 64.0 %copy-start.3 = (f32[1024,256]{1,0:T(8,128)S(1)}, f32[1024,256]{1,0:T(8,128)}, u32[]{:S(2)}) copy-start(f32[1024,256]{1,0:T(8,128)} %all-gather.16.cloned.1.call-done) | copy-start | bytes 3145732
  189.9 110.7 %all-gather.36.cloned.1.call-start = ((), (), s32[]{:S(2)}) async-start(), calls=%async_computation.11 | async-start | bytes 1310720 | tf_op jit(solution)/shard_map/all_gather | solution.py:83
  227.7 103.0 %all-gather.18.cloned.1.call-start = ((), (), s32[]{:S(2)}) async-start(), calls=%async_computation.2 | async-start | bytes 1310720 | tf_op jit(solution)/shard_map/all_gather | solution.py:80
  256.9 73.8 %copy-start.4 = (f32[1,256,256]{2,1,0:T(8,128)S(1)}, f32[1,256,256]{2,1,0:T(8,128)}, u32[]{:S(2)}) copy-start(f32[1,256,256]{2,1,0:T(8,128)} %param.6) | copy-start | bytes 786436
  300.6 30.1 %copy-start.2 = (f32[1024,256]{1,0:T(8,128)S(1)}, f32[1024,256]{1,0:T(8,128)}, u32[]{:S(2)}) copy-start(f32[1024,256]{1,0:T(8,128)} %all-gather.36.cloned.1.call-done) | copy-start | bytes 3145732
  (2 other events, 1.9 us)
Sparse Core Ops, SparseCore 0:
  18.6 18.2 all-gather.15
  39.0 27.9 all-gather.19
  70.4 27.4 all-gather.21
  99.9 16.2 all-gather.23
  119.6 16.7 all-gather.25
  139.4 16.7 all-gather.27
  159.3 16.7 all-gather.29
  177.6 16.7 all-gather.33
  196.5 27.9 all-gather.31
  226.5 27.4 all-gather.13
  255.5 27.4 all-gather.37
  284.4 16.2 all-gather.35
  302.8 27.9 all-gather.17
where the time goes:
time: 341 us; the launch traced here: 340 us
  waiting for transfers between devices  282 us (83%)
  matrix products  28.1 us (8%)
  between operations  14.6 us (4%)
  starting transfers between devices  8.83 us (3%)
  other arithmetic  4.02 us (1%)
    all_gather x4, waiting for transfers between devices, on_device(): lax.all_gather(series, 'row', axis=0, tiled=True)  58.3 us
    all_gather x1, waiting for transfers between devices, on_device(): series_panel = lax.all_gather(series, 'col', axis=1, tiled=True)  30.1 us
    all_gather x1, waiting for transfers between devices, on_device(): lax.all_gather(back_a, 'col', axis=1, tiled=True)  30.1 us
    all_gather x1, waiting for transfers between devices, on_device(): power_rows = lax.all_gather(power_term, 'col', axis=1, tiled=True)  27 us
    all_gather x1, waiting for transfers between devices, on_device(): lax.all_gather(side_term, 'col', axis=1, tiled=True)  26.8 us
    all_gather x1, waiting for transfers between devices, on_device(): lax.all_gather(scaled_bwd, 'col', axis=1, tiled=True)  26.1 us
    all_gather x1, waiting for transfers between devices, on_device(): lax.all_gather(transmit_b, 'col', axis=1, tiled=True)  26 us
    ppermute x5, waiting for transfers between devices, partner(): return lax.ppermute(block, axis, route)  24.9 us
  transfers between devices with their start and end apart: 18, of which 17 were waited for; matrix products, arithmetic and copies ran while one was open for 4% of the time, Pallas kernels for 0%

commit v1 on v0

v1 whole, which is shorter than its diff:
```python
import functools

import jax
import jax.numpy as jnp
from jax import lax
from jax.experimental import pallas as pl
from jax.experimental.pallas import tpu as pltpu
from jax.sharding import PartitionSpec as P

NTERMS = 6
VMEM_LIMIT = 48 * 2**20


def split(value):
    high = value.astype(jnp.bfloat16)
    return high, (value - high.astype(jnp.float32)).astype(jnp.bfloat16)


def dot(left, right):
    return jnp.dot(left, right, preferred_element_type=jnp.float32)


def dot3(left_high, left_low, right_high, right_low):
    return dot(left_high, right_high) + (dot(left_high, right_low) + dot(left_low, right_high))


def span(index, size):
    return pl.ds(pl.multiple_of(index * size, size), size)


def step_kernel(step, n_pieces, pos, *refs):
    pieces = refs[:n_pieces]
    refs = refs[n_pieces:]
    highs, lows, sums = refs[:step], refs[step : 2 * step], refs[2 * step : 3 * step]
    high, low = refs[3 * step], refs[3 * step + 1]
    out_sums = refs[3 * step + 2 :]
    rows, cols = pieces[0].shape
    for i, piece in enumerate(pieces):
        side, row = pos[2 * i], pos[2 * i + 1]
        high[side, span(row, rows), :], low[side, span(row, rows), :] = split(piece[...])
    place = pos[2 * n_pieces + step]
    for n in range(step):
        out_sums[n][...] = sums[n][...] + dot3(
            high[0], low[0], highs[n][1, span(place, cols), :], lows[n][1, span(place, cols), :]
        )
    total = dot3(high[0], low[0], high[1, span(place, cols), :], low[1, span(place, cols), :])
    for n in range(step):
        k = pos[2 * n_pieces + n]
        total += dot3(highs[n][0], lows[n][0], high[1, span(k, cols), :], low[1, span(k, cols), :])
    out_sums[step][...] = total


def last_kernel(blocks, row_pieces, pos, *refs):
    highs, lows, sums = refs[:blocks], refs[blocks : 2 * blocks], refs[2 * blocks : 3 * blocks]
    left = refs[3 * blocks : 4 * blocks]
    refs = refs[4 * blocks :]
    panels = refs[:row_pieces]
    weight, reflect, out, power_high, power_low, left_high, left_low, base, state, z_high, z_low = refs[row_pieces:]
    rows, cols = left[0].shape
    upper = pos[0] == 0
    for i, panel in enumerate(panels):
        base[span(pos[1 + i], rows), :] = panel[...]
    places = [pos[1 + row_pieces + j] for j in range(blocks)]

    def take(source):
        for j in range(blocks):
            here = pl.ds(j * cols, cols)
            z_high[here, :], z_low[here, :] = split(source[span(places[j], cols), :])

    for j in range(blocks):
        here = pl.ds(j * cols, cols)
        power_high[:, here], power_low[:, here] = split(sums[j][...])

    @pl.when(upper)
    def _():
        for n in range(blocks):
            total = None
            for j in range(blocks):
                scaled = left[j][...] * weight[pl.ds(places[j], 1), :]
                term = dot3(*split(scaled), highs[n][1, span(places[j], cols), :], lows[n][1, span(places[j], cols), :])
                total = term if total is None else total + term
            here = pl.ds(n * cols, cols)
            left_high[:, here], left_low[:, here] = split(total)

    @pl.when(jnp.logical_not(upper))
    def _():
        for n in range(blocks):
            here = pl.ds(n * cols, cols)
            left_high[:, here], left_low[:, here] = split(left[n][...])

    take(base)

    @pl.loop(0, NTERMS - 1)
    def _(_):
        state[...] = base[...] + dot3(power_high[...], power_low[...], z_high[...], z_low[...])
        take(state)

    result = dot3(left_high[...], left_low[...], z_high[...], z_low[...])

    @pl.when(upper)
    def _():
        out[...] = reflect[...] + result

    @pl.when(jnp.logical_not(upper))
    def _():
        out[...] = result


def vmem(count):
    return [pl.BlockSpec(memory_space=pltpu.VMEM)] * count


def call(kernel, pos, operands, outs, scratch, aliases, flops):
    moved = sum(a.size * a.dtype.itemsize for a in operands)
    return pl.pallas_call(
        kernel,
        out_shape=outs,
        in_specs=[pl.BlockSpec(memory_space=pltpu.SMEM)] + vmem(len(operands)),
        out_specs=jax.tree.map(lambda _: vmem(1)[0], outs),
        scratch_shapes=scratch,
        input_output_aliases=aliases,
        compiler_params=pltpu.CompilerParams(vmem_limit_bytes=VMEM_LIMIT),
        cost_estimate=pl.CostEstimate(flops=flops, bytes_accessed=moved, transcendentals=0),
    )(pos, *operands)


def on_device(reflect_fwd, transmit_fwd, reflect_bwd, transmit_bwd, material_ids, interface_gain):
    reflect_fwd, transmit_fwd, reflect_bwd, transmit_bwd = (
        a[0] for a in (reflect_fwd, transmit_fwd, reflect_bwd, transmit_bwd)
    )
    rows, cols = reflect_fwd.shape
    layers, row_count, blocks = (lax.axis_size(a) for a in ("layer", "row", "col"))
    order = rows * row_count
    distance = layers // 2
    cores = 2 if row_count % 2 == 0 else 1
    chips = row_count // cores
    layer, row, col = (lax.axis_index(a) for a in ("layer", "row", "col"))
    upper = layer < distance
    side, chip, core = jnp.where(upper, 0, 1), row // cores, row % cores

    def plane(value, even, odd):
        route = []
        for here in range(layers):
            for there in range(row_count):
                flip, hop = (even, odd)[there % cores]
                target = (here + distance) % layers if flip else here
                route.append((here * row_count + there, target * row_count + (there + hop * cores) % row_count))
        return lax.ppermute(value, ("layer", "row"), route)

    def sibling(value):
        return lax.ppermute(value, "row", [(i, i ^ 1) for i in range(row_count)])

    def onward(value):
        return lax.ppermute(value, "col", [(i, (i + 1) % blocks) for i in range(blocks)])

    own = jnp.where(upper, reflect_bwd, reflect_fwd)
    left_own = jnp.where(upper, transmit_bwd, transmit_fwd)
    own_gain = lax.dynamic_index_in_dim(interface_gain, material_ids[0], 0, keepdims=False)
    extended = jnp.concatenate([transmit_fwd, own_gain.reshape(-1, cols)], axis=0)
    across = plane(extended, (1, 0), (1, 0))
    weight = own_gain * across[rows:].reshape(-1)
    row_gain = lax.dynamic_slice_in_dim(weight, row * rows, rows)
    panel = row_gain[:, None] * jnp.where(upper, transmit_fwd, across[:rows])

    hops = [((0, 0), (0, 0))]
    if chips == 2:
        hops += [((1, 0), (0, 1)), ((0, 1), (1, 0)), ((1, 1), (1, 1))]
    else:
        hops += [((1, 0), (1, 0))]
        hops += [((f, h), (f, h)) for f in (0, 1) for h in range(1, chips)]

    def gather(piece):
        found = [piece]
        if chips == 2:
            first = plane(piece, *hops[1])
            found += [first, plane(piece, *hops[2]), plane(first, *hops[2])]
        else:
            first = plane(piece, (1, 0), (1, 0))
            found += [first]
            found += [plane(v, (0, h), (0, h)) for v in (piece, first) for h in range(1, chips)]
        if cores == 2:
            found += [sibling(v) for v in found]
        return found

    origins = []
    for other in range(cores):
        for even, odd in hops:
            on = core if other == 0 else 1 - core
            flip = jnp.where(on == 0, even[0], odd[0])
            hop = jnp.where(on == 0, even[1], odd[1])
            origins += [jnp.where(flip == 1, 1 - side, side), (chip - hop) % chips * cores + on]
    places = [(col - j) % blocks for j in range(blocks)]
    n_pieces = cores * len(hops)
    pos = jnp.stack([jnp.asarray(v, jnp.int32) for v in origins + places])

    highs, lows, sums = [], [], []
    piece = own
    both = jax.ShapeDtypeStruct((2, order, cols), jnp.bfloat16)
    total = jax.ShapeDtypeStruct((order, cols), jnp.float32)
    for step in range(blocks):
        pieces = gather(piece)
        if step + 1 < blocks:
            piece = onward(piece)
        results = call(
            functools.partial(step_kernel, step, n_pieces),
            pos,
            pieces + highs + lows + sums,
            [both, both] + [total] * (step + 1),
            [],
            {1 + n_pieces + 2 * step + n: 2 + n for n in range(step)},
            6 * (2 * step + 1) * order * cols * cols,
        )
        highs, lows, sums = highs + [results[0]], lows + [results[1]], list(results[2:])

    left = [left_own]
    for step in range(blocks - 1):
        left.append(onward(left[-1]))

    panels, starts = [panel], [row]
    for hop in range(1, chips):
        panels.append(plane(panel, (0, hop), (0, hop)))
        starts.append((row - hop * cores) % row_count)
    if cores == 2:
        panels += [sibling(v) for v in panels]
        starts += [v ^ 1 for v in starts]

    last_pos = jnp.stack([jnp.asarray(v, jnp.int32) for v in [side] + starts + places])
    result = call(
        functools.partial(last_kernel, blocks, len(panels)),
        last_pos,
        highs + lows + sums + left + panels + [weight.reshape(-1, cols), reflect_fwd],
        jax.ShapeDtypeStruct((rows, cols), jnp.float32),
        [pltpu.VMEM((order, order), jnp.bfloat16)] * 2
        + [pltpu.VMEM((rows, order), jnp.bfloat16)] * 2
        + [pltpu.VMEM((order, cols), jnp.float32)] * 2
        + [pltpu.VMEM((order, cols), jnp.bfloat16)] * 2,
        {},
        6 * NTERMS * order * order * cols,
    )
    swapped = plane(result, (1, 0), (1, 0))
    return jnp.where(upper, result, swapped)[None], jnp.where(upper, swapped, result)[None]


def solution(mesh):
    block = P("layer", "row", "col")
    return jax.shard_map(
        on_device,
        mesh=mesh,
        in_specs=(block, block, block, block, P("layer"), P()),
        out_specs=(block, block),
        check_vma=False,
    )
```

time: 341 us -> 128 us (0.38)
  waiting for transfers between devices: 282 us -> 34.7 us
  Pallas kernels: 0 us -> 38.2 us
  matrix products: 28.1 us -> 0 us
  starting transfers between devices: 8.83 us -> 29.6 us
  local copies, waits for them, and re-layouts: 2.73 us -> 19.2 us
  between operations: 14.6 us -> 1.93 us
    all_gather x13 -> x0, waiting for transfers between devices: 256 us -> none  [the longest x4 58.3 us: on_device(): lax.all_gather(series, 'row', axis=0, tiled=True)]
    pallas_call x0 -> x5, Pallas kernels: none -> 38.2 us  [call(): pl.pallas_call(kernel, out_shape=outs, in_specs=[pl.BlockSpec(memory_spac...]
    dot_general x10 -> x0, matrix products: 28.1 us -> none  [the longest x5 15.4 us: folder(): jnp.dot(panel, incoming, precision=PRECISE, preferred_element_type=jnp.fl...]
    ppermute x5 -> x39, starting transfers between devices: 8.3 us -> 29.6 us  [the longest x15 22.2 us: plane(): return lax.ppermute(value, ('layer', 'row'), route)]
    unnamed x16 -> x85, local copies, waits for them, and re-layouts: 2.65 us -> 17 us
    ppermute x5 -> x39, waiting for transfers between devices: 24.9 us -> 34.7 us  [the longest x15 24.6 us: plane(): return lax.ppermute(value, ('layer', 'row'), route)]
  transfers between devices with their start and end apart: 18 -> 39, of which waited for: 17 -> 8; matrix products, arithmetic and copies ran while one was open for 4% -> 2% of each run, Pallas kernels for 0% -> 17%
where the time goes in v1:
time: 128 us; the launch traced here: 127 us
  Pallas kernels  38.2 us (30%)
  waiting for transfers between devices  34.7 us (27%)
  starting transfers between devices  29.6 us (23%)
  local copies, waits for them, and re-layouts  19.2 us (15%)
  other arithmetic  3.75 us (3%)
  between operations  1.93 us (2%)
    pallas_call x5, Pallas kernels, call(): pl.pallas_call(kernel, out_shape=outs, in_specs=[pl.BlockSpec(memory_spac...  38.2 us
    ppermute x15, waiting for transfers between devices, plane(): return lax.ppermute(value, ('layer', 'row'), route)  24.6 us
    ppermute x15, starting transfers between devices, plane(): return lax.ppermute(value, ('layer', 'row'), route)  22.2 us
    unnamed x85, local copies, waits for them, and re-layouts  17 us
    ppermute x6, waiting for transfers between devices, onward(): lax.ppermute(value, 'col', [(i, (i + 1) % blocks) for i in range(blocks)])  10 us
    ppermute x6, starting transfers between devices, onward(): lax.ppermute(value, 'col', [(i, (i + 1) % blocks) for i in range(blocks)])  5.06 us
  transfers between devices with their start and end apart: 39, of which 8 were waited for; matrix products, arithmetic and copies ran while one was open for 2% of the time, Pallas kernels for 17%

profile of v1, /device:TPU:0, one launch (start us, length us, event | category | flops | bytes accessed | tf_op | source)
XLA Modules:
  0.0 127.4 jit_solution(7922411615612539054)
XLA Ops:
  4.3 3.0 %collective-permute-start.34 = (f32[260,256]{1,0:T(8,128)S(1)}, f32[260,256]{1,0:T(8,128)}, u32[]{:S(2)}, u32[]{:S(2)}) collective-permute-start(f32[260,256]{1,0:T(8,128)S(1)} %pad_maximum_fusion), channel_id=1, source_target_pairs={{0,16},{4,20},{8,24},{12,28},{16,0},{20,4},{24,8},{28,12},{1,17},{... | collective-permute-start | bytes 798728 | tf_op jit(solution)/shard_map/ppermute | solution.py:148
  7.4 2.0 %collective-permute-start.1 = (f32[256,256]{1,0:T(8,128)S(1)}, f32[256,256]{1,0:T(8,128)S(1)}, u32[]{:S(2)}, u32[]{:S(2)}) collective-permute-start(f32[256,256]{1,0:T(8,128)S(1)} %bitcast_select_fusion.1.refs_0_), channel_id=1, source_target_pairs={{0,8},{4,20},{8,0},{12,28},{16,24},{20,4},{24,16},{28,12},{1,9},{5... | collective-permute-start | bytes 786440 | tf_op jit(solution)/shard_map/ppermute | solution.py:148
  9.5 1.6 %collective-permute-start.7 = (f32[256,256]{1,0:T(8,128)S(1)}, f32[256,256]{1,0:T(8,128)S(1)}, u32[]{:S(2)}, u32[]{:S(2)}) collective-permute-start(f32[256,256]{1,0:T(8,128)S(1)} %bitcast_select_fusion.1.refs_0_), channel_id=1, source_target_pairs={{0,1},{1,2},{2,3},{3,0},{4,5},{5,6},{6,7},{7,4},{8,9},{9,10},{10,1... | collective-permute-start | bytes 786440 | tf_op jit(solution)/shard_map/ppermute | solution.py:154
  11.0 9.2 %collective-permute-done.refs_1_ = f32[256,256]{1,0:T(8,128)S(1)} collective-permute-done((f32[256,256]{1,0:T(8,128)S(1)}, f32[256,256]{1,0:T(8,128)S(1)}, u32[]{:S(2)}, u32[]{:S(2)}) %collective-permute-start) | collective-permute-done | bytes 262176 | tf_op jit(solution)/shard_map/ppermute | solution.py:148
  20.2 2.1 %collective-permute-start.2 = (f32[256,256]{1,0:T(8,128)S(1)}, f32[256,256]{1,0:T(8,128)S(1)}, u32[]{:S(2)}, u32[]{:S(2)}) collective-permute-start(f32[256,256]{1,0:T(8,128)S(1)} %collective-permute-done.refs_1_), channel_id=1, source_target_pairs={{0,8},{4,20},{8,0},{12,28},{16,24},{20,4},{24,16},{28,12},{1,9},{5... | collective-permute-start | bytes 786440 | tf_op jit(solution)/shard_map/ppermute | solution.py:148
  22.3 1.6 %collective-permute-start.8 = (f32[256,256]{1,0:T(8,128)S(1)}, f32[256,256]{1,0:T(8,128)S(1)}, u32[]{:S(2)}, u32[]{:S(2)}) collective-permute-start(f32[256,256]{1,0:T(8,128)S(1)} %collective-permute-done.7.refs_0_), channel_id=1, source_target_pairs={{0,16},{4,12},{8,24},{12,4},{16,0},{20,28},{24,8},{28,20},{1,17},{... | collective-permute-start | bytes 786440 | tf_op jit(solution)/shard_map/ppermute | solution.py:148
  26.4 2.5 %collective-permute-done.2.refs_3_ = f32[256,256]{1,0:T(8,128)S(1)} collective-permute-done((f32[256,256]{1,0:T(8,128)S(1)}, f32[256,256]{1,0:T(8,128)S(1)}, u32[]{:S(2)}, u32[]{:S(2)}) %collective-permute-start.2) | collective-permute-done | bytes 262176 | tf_op jit(solution)/shard_map/ppermute | solution.py:148
  28.8 1.7 %collective-permute-start.15 = (f32[256,256]{1,0:T(8,128)S(1)}, f32[256,256]{1,0:T(8,128)S(1)}, u32[]{:S(2)}, u32[]{:S(2)}) collective-permute-start(f32[256,256]{1,0:T(8,128)S(1)} %collective-permute-done.7.refs_0_), channel_id=1, source_target_pairs={{0,1},{1,2},{2,3},{3,0},{4,5},{5,6},{6,7},{7,4},{8,9},{9,10},{10,1... | collective-permute-start | bytes 786440 | tf_op jit(solution)/shard_map/ppermute | solution.py:154
  30.6 1.6 %collective-permute-start.31 = (f32[256,256]{1,0:T(8,128)S(1)}, f32[256,256]{1,0:T(8,128)}, u32[]{:S(2)}, u32[]{:S(2)}) collective-permute-start(f32[256,256]{1,0:T(8,128)S(1)} %get-tuple-element.45.refs_12_), channel_id=1, source_target_pairs={{0,1},{1,2},{2,3},{3,0},{4,5},{5,6},{6,7},{7,4},{8,9},{9,10},{10,1... | collective-permute-start | bytes 786440 | tf_op jit(solution)/shard_map/ppermute | solution.py:154
  32.9 2.5 %collective-permute-start.35 = (f32[256,256]{1,0:T(8,128)S(1)}, f32[256,256]{1,0:T(8,128)S(1)}, u32[]{:S(2)}, u32[]{:S(2)}) collective-permute-start(f32[256,256]{1,0:T(8,128)S(1)} %get-tuple-element.44.refs_16_), channel_id=1, source_target_pairs={{0,8},{4,12},{8,0},{12,4},{16,24},{20,28},{24,16},{28,20},{1,9},{5... | collective-permute-start | bytes 786440 | tf_op jit(solution)/shard_map/ppermute | solution.py:148
  36.1 3.7 %collective-permute-done.15.refs_0_ = f32[256,256]{1,0:T(8,128)S(1)} collective-permute-done((f32[256,256]{1,0:T(8,128)S(1)}, f32[256,256]{1,0:T(8,128)S(1)}, u32[]{:S(2)}, u32[]{:S(2)}) %collective-permute-start.15) | collective-permute-done | bytes 262176 | tf_op jit(solution)/shard_map/ppermute | solution.py:154
  40.5 4.8 %collective-permute-done.31.refs_13_ = f32[256,256]{1,0:T(8,128)} collective-permute-done((f32[256,256]{1,0:T(8,128)S(1)}, f32[256,256]{1,0:T(8,128)}, u32[]{:S(2)}, u32[]{:S(2)}) %collective-permute-start.31) | collective-permute-done | bytes 262176 | tf_op jit(solution)/shard_map/ppermute | solution.py:154
  46.0 1.5 %collective-permute-start.16 = (f32[256,256]{1,0:T(8,128)S(1)}, f32[256,256]{1,0:T(8,128)S(1)}, u32[]{:S(2)}, u32[]{:S(2)}) collective-permute-start(f32[256,256]{1,0:T(8,128)S(1)} %collective-permute-done.15.refs_0_), channel_id=1, source_target_pairs={{0,16},{4,12},{8,24},{12,4},{16,0},{20,28},{24,8},{28,20},{1,17},{... | collective-permute-start | bytes 786440 | tf_op jit(solution)/shard_map/ppermute | solution.py:148
  48.2 2.5 %collective-permute-start.17 = (f32[256,256]{1,0:T(8,128)S(1)}, f32[256,256]{1,0:T(8,128)S(1)}, u32[]{:S(2)}, u32[]{:S(2)}) collective-permute-start(f32[256,256]{1,0:T(8,128)S(1)} %collective-permute-done.15.refs_0_), channel_id=1, source_target_pairs={{0,8},{4,20},{8,0},{12,28},{16,24},{20,4},{24,16},{28,12},{1,9},{5... | collective-permute-start | bytes 786440 | tf_op jit(solution)/shard_map/ppermute | solution.py:148
  53.3 4.0 %collective-permute-start.18 = (f32[256,256]{1,0:T(8,128)S(1)}, f32[256,256]{1,0:T(8,128)}, u32[]{:S(2)}, u32[]{:S(2)}) collective-permute-start(f32[256,256]{1,0:T(8,128)S(1)} %collective-permute-done.16.refs_1_), channel_id=1, source_target_pairs={{0,8},{4,20},{8,0},{12,28},{16,24},{20,4},{24,16},{28,12},{1,9},{5... | collective-permute-start | bytes 786440 | tf_op jit(solution)/shard_map/ppermute | solution.py:148
  57.3 1.6 %collective-permute-done.23.refs_0_ = f32[256,256]{1,0:T(8,128)S(1)} collective-permute-done((f32[256,256]{1,0:T(8,128)S(1)}, f32[256,256]{1,0:T(8,128)S(1)}, u32[]{:S(2)}, u32[]{:S(2)}) %collective-permute-start.23) | collective-permute-done | bytes 262176 | tf_op jit(solution)/shard_map/ppermute | solution.py:154
  60.9 2.3 %collective-permute-start.25 = (f32[256,256]{1,0:T(8,128)S(1)}, f32[256,256]{1,0:T(8,128)S(1)}, u32[]{:S(2)}, u32[]{:S(2)}) collective-permute-start(f32[256,256]{1,0:T(8,128)S(1)} %collective-permute-done.23.refs_0_), channel_id=1, source_target_pairs={{0,8},{4,20},{8,0},{12,28},{16,24},{20,4},{24,16},{28,12},{1,9},{5... | collective-permute-start | bytes 786440 | tf_op jit(solution)/shard_map/ppermute | solution.py:148
  63.2 3.6 %collective-permute-done.24.refs_1_ = f32[256,256]{1,0:T(8,128)S(1)} collective-permute-done((f32[256,256]{1,0:T(8,128)S(1)}, f32[256,256]{1,0:T(8,128)S(1)}, u32[]{:S(2)}, u32[]{:S(2)}) %collective-permute-start.24) | collective-permute-done | bytes 262176 | tf_op jit(solution)/shard_map/ppermute | solution.py:148
  68.3 1.5 %shard_map.77 = (bf16[2,1024,256]{2,1,0:T(8,128)(2,1)S(1)}, bf16[2,1024,256]{2,1,0:T(8,128)(2,1)S(1)}, f32[1024,256]{1,0:T(8,128)S(1)}) custom-call(s32[20]{0:T(128)S(1)} %stack.102.pos, f32[256,256]{1,0:T(8,128)S(1)} %bitcast_select_fusion.1.refs_0_, f32[256,256]{1,0:T(8,128)S(1)} %collective-permute-done.refs_1_, ...), custom_call_target="tpu_custom_call" | custom-call | flops 402653184 | bytes 2097152 | tf_op jit(solution)/shard_map/pallas_call | solution.py:115
  73.3 4.4 %shard_map.78 = (bf16[2,1024,256]{2,1,0:T(8,128)(2,1)S(1)}, bf16[2,1024,256]{2,1,0:T(8,128)(2,1)S(1)}, f32[1024,256]{1,0:T(8,128)S(1)}, f32[1024,256]{1,0:T(8,128)}) custom-call(s32[20]{0:T(128)S(1)} %stack.102.pos, f32[256,256]{1,0:T(8,128)S(1)} %copy-done.21, f32[256,256]{1,0:T(8,128)S(1)} %copy-done.23, ...), custom_call_target="tpu_custom_call", output_to_operand_aliasing={{2}: (11, {})} | custom-call | flops 1207959552 | bytes 5242880 | tf_op jit(solution)/shard_map/pallas_call | solution.py:115
  79.8 6.8 %shard_map.79 = (bf16[2,1024,256]{2,1,0:T(8,128)(2,1)S(1)}, bf16[2,1024,256]{2,1,0:T(8,128)(2,1)S(1)}, f32[1024,256]{1,0:T(8,128)S(1)}, f32[1024,256]{1,0:T(8,128)}, f32[1024,256]{1,0:T(8,128)}) custom-call(s32[20]{0:T(128)S(1)} %stack.102.pos, f32[256,256]{1,0:T(8,128)S(1)} %collective-permute-done.15.refs_0_, ...), custom_call_target="tpu_custom_call", output_to_operand_aliasing={{2}: (13, {}), {3}: (14, {})} | custom-call | flops 2013265920 | bytes 8388608 | tf_op jit(solution)/shard_map/pallas_call | solution.py:115
  89.5 8.3 %shard_map.80 = (bf16[2,1024,256]{2,1,0:T(8,128)(2,1)S(1)}, bf16[2,1024,256]{2,1,0:T(8,128)(2,1)S(1)}, f32[1024,256]{1,0:T(8,128)S(1)}, f32[1024,256]{1,0:T(8,12...) custom-call(s32[20]{0:T(128)S(1)} %stack.102.pos, ...), custom_call_target="tpu_custom_call", output_to_operand_aliasing={{2}: (15, {}), {3}: (16, {}), {4}: (17, {})} | custom-call | flops 2818572288 | bytes 11534336 | tf_op jit(solution)/shard_map/pallas_call | solution.py:115
  100.8 17.2 %shard_map.81 = f32[256,256]{1,0:T(8,128)S(1)} custom-call(s32[9]{0:T(128)S(1)} %stack.88.pos, bf16[2,1024,256]{2,1,0:T(8,128)(2,1)S(1)} %copy-done.1, bf16[2,1024,256]{2,1,0:T(8,128)(2,1)S(1)} %copy-done.5, bf16[2,1024,256]{2,1,0:T(8,128)(2,1)S(1)} %copy-done.8, bf16[2,1024,256]{2,1,0:T(8,128)(2,1)} %copy-done.36, bf16[2,1024,256]{2,1,0:T(8,128)(2,1)} %copy-done.2, ...), custom_call_target="tpu_custom_call" | custom-call | flops 9663676416 | bytes 14946304 | tf_op jit(solution)/shard_map/pallas_call | solution.py:115
  118.1 8.4 %collective-permute-done.38 = f32[256,256]{1,0:T(8,128)S(1)} collective-permute-done((f32[256,256]{1,0:T(8,128)S(1)}, f32[256,256]{1,0:T(8,128)S(1)}, u32[]{:S(2)}, u32[]{:S(2)}) %collective-permute-start.38) | collective-permute-done | bytes 262176 | tf_op jit(solution)/shard_map/ppermute | solution.py:148
  (156 shorter events, 27.1 us)
Async XLA Ops:
  4.3 20.1 %collective-permute-start.34 = (f32[260,256]{1,0:T(8,128)S(1)}, f32[260,256]{1,0:T(8,128)}, u32[]{:S(2)}, u32[]{:S(2)}) collective-permute-start(f32[260,256]{1,0:T(8,128)S(1)} %pad_maximum_fusion), channel_id=1, source_target_pairs={{0,16},{4,20},{8,24},{12,28},{16,0},{20,4},{24,8},{28,12},{1,17},{... | collective-permute-start | bytes 798728 | tf_op jit(solution)/shard_map/ppermute | solution.py:148
  7.3 12.9 %collective-permute-start = (f32[256,256]{1,0:T(8,128)S(1)}, f32[256,256]{1,0:T(8,128)S(1)}, u32[]{:S(2)}, u32[]{:S(2)}) collective-permute-start(f32[256,256]{1,0:T(8,128)S(1)} %bitcast_select_fusion.1.refs_0_), channel_id=1, source_target_pairs={{0,16},{4,12},{8,24},{12,4},{16,0},{20,28},{24,8},{28,20},{1,17},{... | collective-permute-start | bytes 786440 | tf_op jit(solution)/shard_map/ppermute | solution.py:148
  7.4 14.9 %collective-permute-start.1 = (f32[256,256]{1,0:T(8,128)S(1)}, f32[256,256]{1,0:T(8,128)S(1)}, u32[]{:S(2)}, u32[]{:S(2)}) collective-permute-start(f32[256,256]{1,0:T(8,128)S(1)} %bitcast_select_fusion.1.refs_0_), channel_id=1, source_target_pairs={{0,8},{4,20},{8,0},{12,28},{16,24},{20,4},{24,16},{28,12},{1,9},{5... | collective-permute-start | bytes 786440 | tf_op jit(solution)/shard_map/ppermute | solution.py:148
  9.5 12.9 %collective-permute-start.7 = (f32[256,256]{1,0:T(8,128)S(1)}, f32[256,256]{1,0:T(8,128)S(1)}, u32[]{:S(2)}, u32[]{:S(2)}) collective-permute-start(f32[256,256]{1,0:T(8,128)S(1)} %bitcast_select_fusion.1.refs_0_), channel_id=1, source_target_pairs={{0,1},{1,2},{2,3},{3,0},{4,5},{5,6},{6,7},{7,4},{8,9},{9,10},{10,1... | collective-permute-start | bytes 786440 | tf_op jit(solution)/shard_map/ppermute | solution.py:154
  11.0 12.9 %collective-permute-start.3 = (f32[256,256]{1,0:T(8,128)S(1)}, f32[256,256]{1,0:T(8,128)S(1)}, u32[]{:S(2)}, u32[]{:S(2)}) collective-permute-start(f32[256,256]{1,0:T(8,128)S(1)} %bitcast_select_fusion.1.refs_0_), channel_id=1, source_target_pairs={{0,4},{4,0},{8,12},{12,8},{1,5},{5,1},{9,13},{13,9},{2,6},{6,2},{1... | collective-permute-start | bytes 786440 | tf_op jit(solution)/shard_map/ppermute | solution.py:151
  23.9 11.5 %collective-permute-start.9 = (f32[256,256]{1,0:T(8,128)S(1)}, f32[256,256]{1,0:T(8,128)S(1)}, u32[]{:S(2)}, u32[]{:S(2)}) collective-permute-start(f32[256,256]{1,0:T(8,128)S(1)} %collective-permute-done.7.refs_0_), channel_id=1, source_target_pairs={{0,8},{4,20},{8,0},{12,28},{16,24},{20,4},{24,16},{28,12},{1,9},{5... | collective-permute-start | bytes 786440 | tf_op jit(solution)/shard_map/ppermute | solution.py:148
  28.8 10.9 %collective-permute-start.15 = (f32[256,256]{1,0:T(8,128)S(1)}, f32[256,256]{1,0:T(8,128)S(1)}, u32[]{:S(2)}, u32[]{:S(2)}) collective-permute-start(f32[256,256]{1,0:T(8,128)S(1)} %collective-permute-done.7.refs_0_), channel_id=1, source_target_pairs={{0,1},{1,2},{2,3},{3,0},{4,5},{5,6},{6,7},{7,4},{8,9},{9,10},{10,1... | collective-permute-start | bytes 786440 | tf_op jit(solution)/shard_map/ppermute | solution.py:154
  30.6 14.7 %collective-permute-start.31 = (f32[256,256]{1,0:T(8,128)S(1)}, f32[256,256]{1,0:T(8,128)}, u32[]{:S(2)}, u32[]{:S(2)}) collective-permute-start(f32[256,256]{1,0:T(8,128)S(1)} %get-tuple-element.45.refs_12_), channel_id=1, source_target_pairs={{0,1},{1,2},{2,3},{3,0},{4,5},{5,6},{6,7},{7,4},{8,9},{9,10},{10,1... | collective-permute-start | bytes 786440 | tf_op jit(solution)/shard_map/ppermute | solution.py:154
  32.9 13.1 %collective-permute-start.35 = (f32[256,256]{1,0:T(8,128)S(1)}, f32[256,256]{1,0:T(8,128)S(1)}, u32[]{:S(2)}, u32[]{:S(2)}) collective-permute-start(f32[256,256]{1,0:T(8,128)S(1)} %get-tuple-element.44.refs_16_), channel_id=1, source_target_pairs={{0,8},{4,12},{8,0},{12,4},{16,24},{20,28},{24,16},{28,20},{1,9},{5... | collective-permute-start | bytes 786440 | tf_op jit(solution)/shard_map/ppermute | solution.py:148
  35.3 12.1 %collective-permute-start.6 = (f32[256,256]{1,0:T(8,128)S(1)}, f32[256,256]{1,0:T(8,128)S(1)}, u32[]{:S(2)}, u32[]{:S(2)}) collective-permute-start(f32[256,256]{1,0:T(8,128)S(1)} %collective-permute-done.2.refs_3_), channel_id=1, source_target_pairs={{0,4},{4,0},{8,12},{12,8},{1,5},{5,1},{9,13},{13,9},{2,6},{6,2},{1... | collective-permute-start | bytes 786440 | tf_op jit(solution)/shard_map/ppermute | solution.py:151
  36.0 12.1 %collective-permute-start.10 = (f32[256,256]{1,0:T(8,128)S(1)}, f32[256,256]{1,0:T(8,128)S(1)}, u32[]{:S(2)}, u32[]{:S(2)}) collective-permute-start(f32[256,256]{1,0:T(8,128)S(1)} %collective-permute-done.8.refs_1_), channel_id=1, source_target_pairs={{0,8},{4,20},{8,0},{12,28},{16,24},{20,4},{24,16},{28,12},{1,9},{5... | collective-permute-start | bytes 786440 | tf_op jit(solution)/shard_map/ppermute | solution.py:148
  39.8 10.9 %collective-permute-start.12 = (f32[256,256]{1,0:T(8,128)S(1)}, f32[256,256]{1,0:T(8,128)S(1)}, u32[]{:S(2)}, u32[]{:S(2)}) collective-permute-start(f32[256,256]{1,0:T(8,128)S(1)} %collective-permute-done.8.refs_1_), channel_id=1, source_target_pairs={{0,4},{4,0},{8,12},{12,8},{1,5},{5,1},{9,13},{13,9},{2,6},{6,2},{1... | collective-permute-start | bytes 786440 | tf_op jit(solution)/shard_map/ppermute | solution.py:151
  48.2 10.7 %collective-permute-start.17 = (f32[256,256]{1,0:T(8,128)S(1)}, f32[256,256]{1,0:T(8,128)S(1)}, u32[]{:S(2)}, u32[]{:S(2)}) collective-permute-start(f32[256,256]{1,0:T(8,128)S(1)} %collective-permute-done.15.refs_0_), channel_id=1, source_target_pairs={{0,8},{4,20},{8,0},{12,28},{16,24},{20,4},{24,16},{28,12},{1,9},{5... | collective-permute-start | bytes 786440 | tf_op jit(solution)/shard_map/ppermute | solution.py:148
  58.9 12.8 %collective-permute-start.20 = (f32[256,256]{1,0:T(8,128)S(1)}, f32[256,256]{1,0:T(8,128)}, u32[]{:S(2)}, u32[]{:S(2)}) collective-permute-start(f32[256,256]{1,0:T(8,128)S(1)} %collective-permute-done.16.refs_1_), channel_id=1, source_target_pairs={{0,4},{4,0},{8,12},{12,8},{1,5},{5,1},{9,13},{13,9},{2,6},{6,2},{1... | collective-permute-start | bytes 786440 | tf_op jit(solution)/shard_map/ppermute | solution.py:151
  59.7 12.0 %collective-permute-start.21 = (f32[256,256]{1,0:T(8,128)S(1)}, f32[256,256]{1,0:T(8,128)}, u32[]{:S(2)}, u32[]{:S(2)}) collective-permute-start(f32[256,256]{1,0:T(8,128)S(1)} %collective-permute-done.17.refs_2_), channel_id=1, source_target_pairs={{0,4},{4,0},{8,12},{12,8},{1,5},{5,1},{9,13},{13,9},{2,6},{6,2},{1... | collective-permute-start | bytes 786440 | tf_op jit(solution)/shard_map/ppermute | solution.py:151
  60.9 10.9 %collective-permute-start.25 = (f32[256,256]{1,0:T(8,128)S(1)}, f32[256,256]{1,0:T(8,128)S(1)}, u32[]{:S(2)}, u32[]{:S(2)}) collective-permute-start(f32[256,256]{1,0:T(8,128)S(1)} %collective-permute-done.23.refs_0_), channel_id=1, source_target_pairs={{0,8},{4,20},{8,0},{12,28},{16,24},{20,4},{24,16},{28,12},{1,9},{5... | collective-permute-start | bytes 786440 | tf_op jit(solution)/shard_map/ppermute | solution.py:148
  71.7 16.9 %collective-permute-start.32 = (f32[256,256]{1,0:T(8,128)}, f32[256,256]{1,0:T(8,128)S(1)}, u32[]{:S(2)}, u32[]{:S(2)}) collective-permute-start(f32[256,256]{1,0:T(8,128)} %collective-permute-done.31.refs_13_), channel_id=1, source_target_pairs={{0,1},{1,2},{2,3},{3,0},{4,5},{5,6},{6,7},{7,4},{8,9},{9,10},{10,1... | collective-permute-start | bytes 786440 | tf_op jit(solution)/shard_map/ppermute | solution.py:154
  71.7 17.4 %collective-permute-start.27 = (f32[256,256]{1,0:T(8,128)S(1)}, f32[256,256]{1,0:T(8,128)S(1)}, u32[]{:S(2)}, u32[]{:S(2)}) collective-permute-start(f32[256,256]{1,0:T(8,128)S(1)} %collective-permute-done.23.refs_0_), channel_id=1, source_target_pairs={{0,4},{4,0},{8,12},{12,8},{1,5},{5,1},{9,13},{13,9},{2,6},{6,2},{1... | collective-permute-start | bytes 786440 | tf_op jit(solution)/shard_map/ppermute | solution.py:151
  71.8 17.4 %collective-permute-start.28 = (f32[256,256]{1,0:T(8,128)S(1)}, f32[256,256]{1,0:T(8,128)S(1)}, u32[]{:S(2)}, u32[]{:S(2)}) collective-permute-start(f32[256,256]{1,0:T(8,128)S(1)} %collective-permute-done.24.refs_1_), channel_id=1, source_target_pairs={{0,4},{4,0},{8,12},{12,8},{1,5},{5,1},{9,13},{13,9},{2,6},{6,2},{1... | collective-permute-start | bytes 786440 | tf_op jit(solution)/shard_map/ppermute | solution.py:151
  72.3 17.1 %collective-permute-start.29 = (f32[256,256]{1,0:T(8,128)S(1)}, f32[256,256]{1,0:T(8,128)S(1)}, u32[]{:S(2)}, u32[]{:S(2)}) collective-permute-start(f32[256,256]{1,0:T(8,128)S(1)} %collective-permute-done.25.refs_2_), channel_id=1, source_target_pairs={{0,4},{4,0},{8,12},{12,8},{1,5},{5,1},{9,13},{13,9},{2,6},{6,2},{1... | collective-permute-start | bytes 786440 | tf_op jit(solution)/shard_map/ppermute | solution.py:151
  73.3 16.1 %collective-permute-start.30 = (f32[256,256]{1,0:T(8,128)}, f32[256,256]{1,0:T(8,128)S(1)}, u32[]{:S(2)}, u32[]{:S(2)}) collective-permute-start(f32[256,256]{1,0:T(8,128)} %collective-permute-done.26.refs_3_), channel_id=1, source_target_pairs={{0,4},{4,0},{8,12},{12,8},{1,5},{5,1},{9,13},{13,9},{2,6},{6,2},{1... | collective-permute-start | bytes 786440 | tf_op jit(solution)/shard_map/ppermute | solution.py:151
  88.6 12.1 %collective-permute-start.36 = (f32[256,256]{1,0:T(8,128)S(1)}, f32[256,256]{1,0:T(8,128)S(1)}, u32[]{:S(2)}, u32[]{:S(2)}) collective-permute-start(f32[256,256]{1,0:T(8,128)S(1)} %copy-done.17), channel_id=1, source_target_pairs={{0,4},{4,0},{8,12},{12,8},{1,5},{5,1},{9,13},{13,9},{2,6},{6,2},{1... | collective-permute-start | bytes 786440 | tf_op jit(solution)/shard_map/ppermute | solution.py:151
  89.1 11.6 %collective-permute-start.37 = (f32[256,256]{1,0:T(8,128)S(1)}, f32[256,256]{1,0:T(8,128)S(1)}, u32[]{:S(2)}, u32[]{:S(2)}) collective-permute-start(f32[256,256]{1,0:T(8,128)S(1)} %copy-done.39), channel_id=1, source_target_pairs={{0,4},{4,0},{8,12},{12,8},{1,5},{5,1},{9,13},{13,9},{2,6},{6,2},{1... | collective-permute-start | bytes 786440 | tf_op jit(solution)/shard_map/ppermute | solution.py:151
  89.2 11.5 %collective-permute-start.33 = (f32[256,256]{1,0:T(8,128)S(1)}, f32[256,256]{1,0:T(8,128)S(1)}, u32[]{:S(2)}, u32[]{:S(2)}) collective-permute-start(f32[256,256]{1,0:T(8,128)S(1)} %collective-permute-done.32.refs_14_), channel_id=1, source_target_pairs={{0,1},{1,2},{2,3},{3,0},{4,5},{5,6},{6,7},{7,4},{8,9},{9,10},{10,1... | collective-permute-start | bytes 786440 | tf_op jit(solution)/shard_map/ppermute | solution.py:154
  (57 other events, 352.9 us)

commit v2 on v1

v2 whole, which is shorter than its diff:
```python
import functools

import jax
import jax.numpy as jnp
from jax import lax
from jax.experimental import pallas as pl
from jax.experimental.pallas import tpu as pltpu
from jax.sharding import PartitionSpec as P

NTERMS = 6
MIB = 2**20
TILE = 8
GATE = 10**11


class Grid:
    def __init__(self, shape, layers, row_count, blocks):
        self.shape = shape
        self.layers, self.row_count, self.blocks = layers, row_count, blocks
        self.distance = layers // 2
        self.cores = 2 if row_count % 2 == 0 else 1
        self.chips = row_count // self.cores
        self.hops = [((0, 0), (0, 0))]
        if self.chips == 2:
            self.hops += [((1, 0), (0, 1)), ((0, 1), (1, 0)), ((1, 1), (1, 1))]
        else:
            self.hops += [((1, 0), (1, 0))]
            self.hops += [((f, h), (f, h)) for f in (0, 1) for h in range(1, self.chips)]

    def upper(self):
        return lax.axis_index("layer") < self.distance

    def row(self):
        return lax.axis_index("row")

    def place(self, k):
        hop = k // 2 if k % 2 == 0 else self.blocks - k // 2 - 1
        return lax.rem(lax.axis_index("col") + hop, self.blocks)

    def row_of(self, hop, other):
        row = self.row()
        core = lax.rem(row, self.cores)
        chip = lax.rem(lax.div(row, self.cores) + self.chips - hop, self.chips)
        return chip * self.cores + (self.cores - 1 - core if other else core)

    def origins(self):
        side = jnp.where(self.upper(), 0, 1)
        odd = lax.rem(self.row(), self.cores)
        found = []
        for other in range(self.cores):
            for even_hop, odd_hop in self.hops:
                on_odd = (1 - odd if other else odd) == 1
                flip = jnp.where(on_odd, odd_hop[0], even_hop[0])
                hop = jnp.where(on_odd, odd_hop[1], even_hop[1])
                found.append((jnp.where(flip == 1, 1 - side, side), self.row_of(hop, other)))
        return found


def split(value):
    high = value.astype(jnp.bfloat16)
    return high, (value - high.astype(jnp.float32)).astype(jnp.bfloat16)


def dot(left, right):
    return jnp.dot(left, right, preferred_element_type=jnp.float32)


def dot3(left_high, left_low, right_high, right_low):
    return dot(left_high, right_high) + (dot(left_high, right_low) + dot(left_low, right_high))


def span(index, size):
    return pl.ds(pl.multiple_of(index * size, size), size)


def fetch(grid, first, second, out, sem):
    @pl.when(grid.upper())
    def _():
        pltpu.make_async_copy(first.at[0], out, sem).start()

    @pl.when(jnp.logical_not(grid.upper()))
    def _():
        pltpu.make_async_copy(second.at[0], out, sem).start()

    return pltpu.make_async_copy(first.at[0], out, sem)


def choose_kernel(grid, first, second, *refs):
    out, sem = refs[-2:]
    fetch(grid, first, second, out, sem).wait()


def panel_kernel(grid, start, gains, *refs):
    rows, cols = grid.shape
    panel, weight = refs[-2:]
    height = start + rows + TILE
    pieces = [ref.at[pl.ds(i, height), :] for ref in refs[:-2] for i in range(0, ref.shape[0], height)]
    for piece, (side, row) in zip(pieces, grid.origins()):
        @pl.when(side == 0)
        def _(piece=piece, row=row):
            panel[span(row, rows), :] = piece[start : start + rows, :]

    def gain(piece, i):
        number = piece[start + rows : start + rows + 1, :]
        here = pl.ds(i * cols, cols)
        return sum(jnp.where(number == m, gains[m : m + 1, here], 0.0) for m in range(gains.shape[0]))

    for i in range(gains.shape[1] // cols):
        weight[i : i + 1, :] = gain(pieces[0], i) * gain(pieces[len(grid.hops) - 1], i)
    for row in range(grid.row_count):
        here = weight[row * rows // cols : row * rows // cols + 1, :]
        column = jnp.concatenate([here] * 8, axis=0).T[:, :1]
        panel[row * rows : (row + 1) * rows, :] = panel[row * rows : (row + 1) * rows, :] * column


def gate_kernel(count, *refs):
    for value, out in zip(refs[:count], refs[-count:]):
        out[...] = value[...]


def unpack_kernel(whole, *outs):
    rows = outs[0].shape[0]
    for i, out in enumerate(outs):
        out[...] = whole[i * rows : (i + 1) * rows, :]


def pack_kernel(parts, *refs):
    here = 0
    for ref, (start, stop) in zip(refs, parts):
        refs[-1][here : here + stop - start, :] = ref[start:stop, :]
        here += stop - start


def absorb_kernel(grid, done, new, height, *refs):
    rows, cols = grid.shape
    n_pieces = grid.cores * len(grid.hops)
    pieces = []
    while len(pieces) < n_pieces:
        pieces += [refs[0].at[pl.ds(i, height), :] for i in range(0, refs[0].shape[0], height)]
        refs = refs[1:]
    old, sums, refs = refs[: 2 * done], refs[2 * done : 3 * done], refs[3 * done :]
    refs = refs[-(3 * new + done) :]
    fresh, out_sums = refs[: 2 * new], refs[2 * new :]
    highs, lows = old[:done] + fresh[:new], old[done:] + fresh[new:]
    for piece, (side, row) in zip(pieces, grid.origins()):
        for j in range(new):
            high, low = split(piece[j * rows : (j + 1) * rows, :])
            highs[done + j][side, span(row, rows), :] = high
            lows[done + j][side, span(row, rows), :] = low
    for n in range(done + new):
        total = sums[n][...] if n < done else None
        for k in range(done if n < done else 0, done + new):
            here = span(grid.place(k), cols)
            term = dot3(highs[k][0], lows[k][0], highs[n][1, here, :], lows[n][1, here, :])
            total = term if total is None else total + term
        out_sums[n][...] = total


def last_kernel(grid, *refs):
    blocks = grid.blocks
    highs, lows, sums = refs[:blocks], refs[blocks : 2 * blocks], refs[2 * blocks : 3 * blocks]
    left, refs = refs[3 * blocks : 4 * blocks], refs[4 * blocks :]
    base, weight, reflect, out, power_high, power_low, left_high, left_low, state, z_high, z_low = refs
    rows, cols = left[0].shape
    upper = grid.upper()
    places = [grid.place(j) for j in range(blocks)]

    def take(source):
        for j in range(blocks):
            here = pl.ds(j * cols, cols)
            z_high[here, :], z_low[here, :] = split(source[span(places[j], cols), :])

    for j in range(blocks):
        here = pl.ds(j * cols, cols)
        power_high[:, here], power_low[:, here] = split(sums[j][...])

    @pl.when(upper)
    def _():
        for n in range(blocks):
            total = None
            for j in range(blocks):
                scaled = left[j][...] * weight[pl.ds(places[j], 1), :]
                term = dot3(*split(scaled), highs[n][1, span(places[j], cols), :], lows[n][1, span(places[j], cols), :])
                total = term if total is None else total + term
            here = pl.ds(n * cols, cols)
            left_high[:, here], left_low[:, here] = split(total)

    @pl.when(jnp.logical_not(upper))
    def _():
        for n in range(blocks):
            here = pl.ds(n * cols, cols)
            left_high[:, here], left_low[:, here] = split(left[n][...])

    take(base)

    @pl.loop(0, NTERMS - 1)
    def _(_):
        state[...] = base[...] + dot3(power_high[...], power_low[...], z_high[...], z_low[...])
        take(state)

    result = dot3(left_high[...], left_low[...], z_high[...], z_low[...])

    @pl.when(upper)
    def _():
        out[...] = reflect[0] + result

    @pl.when(jnp.logical_not(upper))
    def _():
        out[...] = result


def finish_kernel(grid, own, across, reflect, transmit):
    upper = grid.upper()
    reflect[0] = jnp.where(upper, own[...], across[...])
    transmit[0] = jnp.where(upper, across[...], own[...])


def call(kernel, outs, operands, scalars=(), loose=(), far=(), scratch=(), aliases=None, flops=0, limit=4 * MIB):
    spaces = [pltpu.VMEM] * len(operands)
    for numbers, space in ((scalars, pltpu.SMEM), (far, pltpu.HBM), (loose, pl.ANY)):
        for i in numbers:
            spaces[i] = space
    specs = [pl.BlockSpec(memory_space=space) for space in spaces]
    return pl.pallas_call(
        kernel,
        out_shape=outs,
        in_specs=specs,
        out_specs=jax.tree.map(lambda _: pl.BlockSpec(memory_space=pltpu.VMEM), outs),
        scratch_shapes=list(scratch),
        input_output_aliases=aliases or {},
        compiler_params=pltpu.CompilerParams(vmem_limit_bytes=limit),
        cost_estimate=pl.CostEstimate(flops=flops, bytes_accessed=0, transcendentals=0),
    )(*operands)


def single(*shape):
    return jax.ShapeDtypeStruct(shape, jnp.float32)


def gate(values, *needs):
    count = len(values)
    kernel = functools.partial(gate_kernel, count)
    return call(kernel, [single(*v.shape) for v in values], [*values, *needs], loose=range(count, count + len(needs)), flops=GATE)


def pack(blocks, *needs):
    blocks = [b if isinstance(b, tuple) else (b, 0, b.shape[0]) for b in blocks]
    parts = [b[1:] for b in blocks]
    arrays = [b[0] for b in blocks]
    shape = (sum(stop - start for start, stop in parts), arrays[0].shape[1])
    loose = range(len(arrays), len(arrays) + len(needs))
    return call(functools.partial(pack_kernel, parts), single(*shape), [*arrays, *needs], loose=loose)


def unpack(whole, count):
    rows, cols = whole.shape
    return call(unpack_kernel, [single(rows // count, cols)] * count, [whole])


def on_device(reflect_fwd, transmit_fwd, reflect_bwd, transmit_bwd, material_ids, interface_gain):
    rows, cols = reflect_fwd.shape[1:]
    grid = Grid((rows, cols), *(lax.axis_size(a) for a in ("layer", "row", "col")))
    blocks, hops, cores, chips = grid.blocks, grid.hops, grid.cores, grid.chips
    order = rows * grid.row_count

    def plane(value, hop):
        route = []
        for layer in range(grid.layers):
            for row in range(grid.row_count):
                flip, on = hop[row % cores]
                target = (layer + grid.distance) % grid.layers if flip else layer
                route.append((layer * grid.row_count + row, target * grid.row_count + (row + on * cores) % grid.row_count))
        return lax.ppermute(value, ("layer", "row"), route)

    def both_cores(hop):
        return (hop, hop)

    def sibling(value):
        return lax.ppermute(value, "row", [(i, i ^ 1) for i in range(grid.row_count)])

    def ring(found, top=None):
        k = len(found)
        source = found[max(k - 2, 0)] if top is None else top
        shift = 1 if k % 2 else -1
        found.append(lax.ppermute(source, "col", [(i, (i + shift) % blocks) for i in range(blocks)]))

    def choose(first, second, *late):
        return call(
            functools.partial(choose_kernel, grid),
            single(rows, cols),
            [first, second, *late],
            far=(0, 1),
            loose=range(2, 2 + len(late)),
            scratch=[pltpu.SemaphoreType.DMA],
        )

    highs, lows, sums = [], [], []
    half = jax.ShapeDtypeStruct((2, order, cols), jnp.bfloat16)

    def absorb(pieces, new, height, weight, needs):
        nonlocal highs, lows, sums
        done = len(highs)
        operands = pieces + highs + lows + sums
        results = call(
            functools.partial(absorb_kernel, grid, done, new, height),
            [half] * (2 * new) + [single(order, cols)] * (done + new),
            operands + list(needs),
            loose=range(len(operands), len(operands) + len(needs)),
            aliases={len(operands) - done + n: 2 * new + n for n in range(done)},
            flops=int(weight * 6 * new * (2 * done + new) * order * cols * cols),
        )
        results = list(results)
        highs, lows, sums = highs + results[:new], lows + results[new : 2 * new], results[2 * new :]

    def along(value, shift):
        return lax.ppermute(value, "col", [(i, (i + shift) % blocks) for i in range(blocks)])

    def a_hop(value):
        return plane(value, hops[1])

    def b_hop(value):
        return plane(value, hops[2])

    p0 = jnp.where(grid.upper(), reflect_bwd[0], reflect_fwd[0])
    number = jnp.broadcast_to(material_ids.astype(jnp.float32), (TILE, cols))
    e0 = jnp.concatenate([p0, transmit_fwd[0], number], axis=0)

    token = number

    def step(*values):
        nonlocal token
        token, *rest = gate([token, *values])
        return rest

    p0, e0 = step(p0, e0)
    p1, a0 = along(p0, 1), a_hop(e0)
    p0, e0 = step(p0, e0)
    p2, b0 = along(p0, -1), b_hop(e0)
    p1, a0 = step(p1, a0)
    p3, a1, d0 = along(p1, 1), a_hop(p1), b_hop(a0)
    p1, p2, b0 = step(p1, p2, b0)
    b1, a2 = b_hop(p1), a_hop(p2)
    l0 = choose(transmit_bwd, transmit_fwd, p1)
    p2, p3, a1, d0, l0 = step(p2, p3, a1, d0, l0)
    d1, a3, b2 = b_hop(a1), a_hop(p3), b_hop(p2)
    b1, a2, l0 = step(b1, a2, l0)
    d2, l1 = b_hop(a2), along(l0, 1)
    d1, a3, b2, p3 = step(d1, a3, b2, p3)
    d3, b3 = b_hop(a3), b_hop(p3)
    mine01 = []
    for zero, one in ((e0, p1), (a0, a1), (b0, b1), (d0, d1)):
        mine01 += [(zero, 0, rows), one, (zero, rows, zero.shape[0])]
    mine01 = pack(mine01)
    theirs01 = sibling(mine01)
    d2, l1, l0 = step(d2, l1, l0)
    l2 = along(l0, -1)
    mine2 = pack([p2, a2, b2, d2])
    theirs2 = sibling(mine2)
    d3, b3, theirs01 = step(d3, b3, theirs01)
    l3 = along(l1, 1)
    mine3 = pack([p3, a3, b3, d3])
    theirs3 = sibling(mine3)
    absorb([mine01, theirs01], 2, 3 * rows + TILE, 1, [])
    theirs2, l2 = step(theirs2, l2)
    panel, weight = call(
        functools.partial(panel_kernel, grid, 2 * rows),
        [single(order, cols), single(-(-order // cols // TILE) * TILE, cols)],
        [interface_gain, mine01, theirs01],
    )
    absorb([mine2, theirs2], 1, rows, 1, [])
    absorb([mine3, theirs3], 1, rows, 1, [])
    left = [l0, l1, l2, l3]

    result = call(
        functools.partial(last_kernel, grid),
        single(rows, cols),
        highs + lows + sums + left + [panel, weight, reflect_fwd],
        scratch=[pltpu.VMEM((order, order), jnp.bfloat16)] * 2
        + [pltpu.VMEM((rows, order), jnp.bfloat16)] * 2
        + [pltpu.VMEM((order, cols), jnp.float32)]
        + [pltpu.VMEM((order, cols), jnp.bfloat16)] * 2,
        flops=6 * NTERMS * order * order * cols,
        limit=16 * MIB,
    )
    across = plane(result, both_cores((1, 0)))
    outs = [single(1, rows, cols)] * 2
    return tuple(call(functools.partial(finish_kernel, grid), outs, [result, across]))


def solution(mesh):
    block = P("layer", "row", "col")
    return jax.shard_map(
        on_device,
        mesh=mesh,
        in_specs=(block, block, block, block, P("layer"), P()),
        out_specs=(block, block),
        check_vma=False,
    )
```

time: 128 us -> 91.2 us (0.71)
  local copies, waits for them, and re-layouts: 19.2 us -> 1.82 us
  Pallas kernels: 38.2 us -> 26.8 us
  starting transfers between devices: 29.6 us -> 26.4 us
  waiting for transfers between devices: 34.7 us -> 32.3 us
  other arithmetic: 3.75 us -> 1.98 us
    unnamed x85 -> x28, local copies, waits for them, and re-layouts: 17 us -> 1.82 us
    pallas_call x5 -> x20, Pallas kernels: 38.2 us -> 26.8 us  [call(): pl.pallas_call(kernel, out_shape=outs, in_specs=specs, out_specs=jax.tree...]
    ppermute x15 -> x13, starting transfers between devices: 22.2 us -> 14.8 us  [plane(): return lax.ppermute(value, ('layer', 'row'), route)]
    ppermute x24 -> x9, starting transfers between devices: 7.33 us -> 11.6 us  [the longest x6 11.5 us: along(): lax.ppermute(value, 'col', [(i, (i + shift) % blocks) for i in range(bloc...]
    ppermute x24 -> x9, waiting for transfers between devices: 10.1 us -> 7.22 us  [the longest x6 7.21 us: along(): lax.ppermute(value, 'col', [(i, (i + shift) % blocks) for i in range(bloc...]
    dynamic_slice x3 -> x0, local copies, waits for them, and re-layouts: 2.01 us -> none  [the longest x2 1.93 us: on_device(): lax.dynamic_index_in_dim(interface_gain, material_ids[0], 0, keepdims=False)]
    mul x3 -> x0, other arithmetic: 1.87 us -> none  [the longest x1 1.16 us: on_device(): panel = row_gain[:, None] * jnp.where(upper, transmit_fwd, across[:rows])]
    ppermute x15 -> x13, waiting for transfers between devices: 24.6 us -> 25.1 us  [plane(): return lax.ppermute(value, ('layer', 'row'), route)]
  transfers between devices with their start and end apart: 39 -> 22, of which waited for: 8 -> 13; matrix products, arithmetic and copies ran while one was open for 2% -> 0% of each run, Pallas kernels for 17% -> 13%
where the time goes in v2:
time: 91.2 us; the launch traced here: 90.9 us
  waiting for transfers between devices  32.3 us (35%)
  Pallas kernels  26.8 us (29%)
  starting transfers between devices  26.4 us (29%)
  other arithmetic  1.98 us (2%)
  local copies, waits for them, and re-layouts  1.82 us (2%)
  between operations  1.56 us (2%)
    pallas_call x20, Pallas kernels, call(): pl.pallas_call(kernel, out_shape=outs, in_specs=specs, out_specs=jax.tree...  26.8 us
    ppermute x13, waiting for transfers between devices, plane(): return lax.ppermute(value, ('layer', 'row'), route)  25.1 us
    ppermute x13, starting transfers between devices, plane(): return lax.ppermute(value, ('layer', 'row'), route)  14.8 us
    ppermute x6, starting transfers between devices, along(): lax.ppermute(value, 'col', [(i, (i + shift) % blocks) for i in range(bloc...  11.5 us
    ppermute x6, waiting for transfers between devices, along(): lax.ppermute(value, 'col', [(i, (i + shift) % blocks) for i in range(bloc...  7.21 us
  transfers between devices with their start and end apart: 22, of which 13 were waited for; matrix products, arithmetic and copies ran while one was open for 0% of the time, Pallas kernels for 13%

profile of v2, /device:TPU:0, one launch (start us, length us, event | category | flops | bytes accessed | tf_op | source)
XLA Modules:
  0.0 90.9 jit_solution(5233502910584819965)
XLA Ops:
  3.3 3.1 %collective-permute-start = (f32[256,256]{1,0:T(8,128)S(1)}, f32[256,256]{1,0:T(8,128)S(1)}, u32[]{:S(2)}, u32[]{:S(2)}) collective-permute-start(f32[256,256]{1,0:T(8,128)S(1)} %get-tuple-element.60.refs_1_), channel_id=1, source_target_pairs={{0,1},{1,2},{2,3},{3,0},{4,5},{5,6},{6,7},{7,4},{8,9},{9,10},{10,1... | collective-permute-start | bytes 786440 | tf_op jit(solution)/shard_map/ppermute | solution.py:316
  6.4 1.5 %collective-permute-start.1 = (f32[520,256]{1,0:T(8,128)S(1)}, f32[520,256]{1,0:T(8,128)S(1)}, u32[]{:S(2)}, u32[]{:S(2)}) collective-permute-start(f32[520,256]{1,0:T(8,128)S(1)} %get-tuple-element.61.refs_2_), channel_id=1, source_target_pairs={{0,16},{4,12},{8,24},{12,4},{16,0},{20,28},{24,8},{28,20},{1,17},{... | collective-permute-start | bytes 1597448 | tf_op jit(solution)/shard_map/ppermute | solution.py:273
  8.0 2.3 %collective-permute-start.2 = (f32[256,256]{1,0:T(8,128)S(1)}, f32[256,256]{1,0:T(8,128)S(1)}, u32[]{:S(2)}, u32[]{:S(2)}) collective-permute-start(f32[256,256]{1,0:T(8,128)S(1)} %get-tuple-element.66), channel_id=1, source_target_pairs={{0,3},{1,0},{2,1},{3,2},{4,7},{5,4},{6,5},{7,6},{8,11},{9,8},{10,9... | collective-permute-start | bytes 786440 | tf_op jit(solution)/shard_map/ppermute | solution.py:316
  10.3 1.5 %collective-permute-start.3 = (f32[520,256]{1,0:T(8,128)S(1)}, f32[520,256]{1,0:T(8,128)S(1)}, u32[]{:S(2)}, u32[]{:S(2)}) collective-permute-start(f32[520,256]{1,0:T(8,128)S(1)} %get-tuple-element.62.refs_0_.refs_2_), channel_id=1, source_target_pairs={{0,8},{4,20},{8,0},{12,28},{16,24},{20,4},{24,16},{28,12},{1,9},{5... | collective-permute-start | bytes 1597448 | tf_op jit(solution)/shard_map/ppermute | solution.py:273
  11.8 3.8 %collective-permute-done.refs_1_ = f32[256,256]{1,0:T(8,128)S(1)} collective-permute-done((f32[256,256]{1,0:T(8,128)S(1)}, f32[256,256]{1,0:T(8,128)S(1)}, u32[]{:S(2)}, u32[]{:S(2)}) %collective-permute-start) | collective-permute-done | bytes 262176 | tf_op jit(solution)/shard_map/ppermute | solution.py:316
  15.6 3.7 %collective-permute-done.1.refs_2_ = f32[520,256]{1,0:T(8,128)S(1)} collective-permute-done((f32[520,256]{1,0:T(8,128)S(1)}, f32[520,256]{1,0:T(8,128)S(1)}, u32[]{:S(2)}, u32[]{:S(2)}) %collective-permute-start.1) | collective-permute-done | bytes 532512 | tf_op jit(solution)/shard_map/ppermute | solution.py:273
  19.4 1.6 %collective-permute-start.5 = (f32[256,256]{1,0:T(8,128)S(1)}, f32[256,256]{1,0:T(8,128)S(1)}, u32[]{:S(2)}, u32[]{:S(2)}) collective-permute-start(f32[256,256]{1,0:T(8,128)S(1)} %get-tuple-element.65.refs_1_), channel_id=1, source_target_pairs={{0,16},{4,12},{8,24},{12,4},{16,0},{20,28},{24,8},{28,20},{1,17},{... | collective-permute-start | bytes 786440 | tf_op jit(solution)/shard_map/ppermute | solution.py:273
  20.9 3.6 %collective-permute-start.4 = (f32[256,256]{1,0:T(8,128)S(1)}, f32[256,256]{1,0:T(8,128)S(1)}, u32[]{:S(2)}, u32[]{:S(2)}) collective-permute-start(f32[256,256]{1,0:T(8,128)S(1)} %get-tuple-element.65.refs_1_), channel_id=1, source_target_pairs={{0,1},{1,2},{2,3},{3,0},{4,5},{5,6},{6,7},{7,4},{8,9},{9,10},{10,1... | collective-permute-start | bytes 786440 | tf_op jit(solution)/shard_map/ppermute | solution.py:316
  25.4 1.4 %collective-permute-start.7 = (f32[256,256]{1,0:T(8,128)S(1)}, f32[256,256]{1,0:T(8,128)S(1)}, u32[]{:S(2)}, u32[]{:S(2)}) collective-permute-start(f32[256,256]{1,0:T(8,128)S(1)} %get-tuple-element.67.refs_0_.refs_1_), channel_id=1, source_target_pairs={{0,8},{4,20},{8,0},{12,28},{16,24},{20,4},{24,16},{28,12},{1,9},{5... | collective-permute-start | bytes 786440 | tf_op jit(solution)/shard_map/ppermute | solution.py:273
  29.1 4.9 %collective-permute-done.6.refs_4_ = f32[520,256]{1,0:T(8,128)S(1)} collective-permute-done((f32[520,256]{1,0:T(8,128)S(1)}, f32[520,256]{1,0:T(8,128)S(1)}, u32[]{:S(2)}, u32[]{:S(2)}) %collective-permute-start.6) | collective-permute-done | bytes 532512 | tf_op jit(solution)/shard_map/ppermute | solution.py:273
  34.1 1.7 %collective-permute-start.9 = (f32[256,256]{1,0:T(8,128)S(1)}, f32[256,256]{1,0:T(8,128)S(1)}, u32[]{:S(2)}, u32[]{:S(2)}) collective-permute-start(f32[256,256]{1,0:T(8,128)S(1)} %get-tuple-element.71.refs_4_), channel_id=1, source_target_pairs={{0,8},{4,20},{8,0},{12,28},{16,24},{20,4},{24,16},{28,12},{1,9},{5... | collective-permute-start | bytes 786440 | tf_op jit(solution)/shard_map/ppermute | solution.py:273
  35.8 1.2 %collective-permute-start.10 = (f32[256,256]{1,0:T(8,128)S(1)}, f32[256,256]{1,0:T(8,128)S(1)}, u32[]{:S(2)}, u32[]{:S(2)}) collective-permute-start(f32[256,256]{1,0:T(8,128)S(1)} %get-tuple-element.78.refs_4_), channel_id=1, source_target_pairs={{0,16},{4,12},{8,24},{12,4},{16,0},{20,28},{24,8},{28,20},{1,17},{... | collective-permute-start | bytes 786440 | tf_op jit(solution)/shard_map/ppermute | solution.py:273
  37.5 1.9 %collective-permute-start.12 = (f32[256,256]{1,0:T(8,128)S(1)}, f32[256,256]{1,0:T(8,128)S(1)}, u32[]{:S(2)}, u32[]{:S(2)}) collective-permute-start(f32[256,256]{1,0:T(8,128)S(1)} %get-tuple-element.82.refs_1_), channel_id=1, source_target_pairs={{0,8},{4,20},{8,0},{12,28},{16,24},{20,4},{24,16},{28,12},{1,9},{5... | collective-permute-start | bytes 786440 | tf_op jit(solution)/shard_map/ppermute | solution.py:273
  39.9 2.9 %collective-permute-done.9.refs_1_ = f32[256,256]{1,0:T(8,128)S(1)} collective-permute-done((f32[256,256]{1,0:T(8,128)S(1)}, f32[256,256]{1,0:T(8,128)S(1)}, u32[]{:S(2)}, u32[]{:S(2)}) %collective-permute-start.9) | collective-permute-done | bytes 262176 | tf_op jit(solution)/shard_map/ppermute | solution.py:273
  42.9 2.2 %collective-permute-done.10.refs_2_ = f32[256,256]{1,0:T(8,128)S(1)} collective-permute-done((f32[256,256]{1,0:T(8,128)S(1)}, f32[256,256]{1,0:T(8,128)S(1)}, u32[]{:S(2)}, u32[]{:S(2)}) %collective-permute-start.10) | collective-permute-done | bytes 262176 | tf_op jit(solution)/shard_map/ppermute | solution.py:273
  45.7 1.3 %collective-permute-start.14 = (f32[256,256]{1,0:T(8,128)S(1)}, f32[256,256]{1,0:T(8,128)S(1)}, u32[]{:S(2)}, u32[]{:S(2)}) collective-permute-start(f32[256,256]{1,0:T(8,128)S(1)} %get-tuple-element.85.refs_1_), channel_id=1, source_target_pairs={{0,8},{4,20},{8,0},{12,28},{16,24},{20,4},{24,16},{28,12},{1,9},{5... | collective-permute-start | bytes 786440 | tf_op jit(solution)/shard_map/ppermute | solution.py:273
  49.8 1.6 %collective-permute-start.18 = (f32[256,256]{1,0:T(8,128)S(1)}, f32[256,256]{1,0:T(8,128)S(1)}, u32[]{:S(2)}, u32[]{:S(2)}) collective-permute-start(f32[256,256]{1,0:T(8,128)S(1)} %get-tuple-element.93.refs_12_), channel_id=1, source_target_pairs={{0,3},{1,0},{2,1},{3,2},{4,7},{5,4},{6,5},{7,6},{8,11},{9,8},{10,9... | collective-permute-start | bytes 786440 | tf_op jit(solution)/shard_map/ppermute | solution.py:316
  52.2 2.8 %collective-permute-done.15.refs_2_ = f32[256,256]{1,0:T(8,128)S(1)} collective-permute-done((f32[256,256]{1,0:T(8,128)S(1)}, f32[256,256]{1,0:T(8,128)S(1)}, u32[]{:S(2)}, u32[]{:S(2)}) %collective-permute-start.15) | collective-permute-done | bytes 262176 | tf_op jit(solution)/shard_map/ppermute | solution.py:273
  55.4 2.8 %collective-permute-done.18.refs_2_ = f32[256,256]{1,0:T(8,128)S(1)} collective-permute-done((f32[256,256]{1,0:T(8,128)S(1)}, f32[256,256]{1,0:T(8,128)S(1)}, u32[]{:S(2)}, u32[]{:S(2)}) %collective-permute-start.18) | collective-permute-done | bytes 262176 | tf_op jit(solution)/shard_map/ppermute | solution.py:316
  60.7 2.6 %shard_map.88 = (bf16[2,1024,256]{2,1,0:T(8,128)(2,1)S(1)}, bf16[2,1024,256]{2,1,0:T(8,128)(2,1)S(1)}, bf16[2,1024,256]{2,1,0:T(8,128)(2,1)S(1)}, bf16[2,1024,25...) custom-call(f32[3104,256]{1,0:T(8,128)S(1)} %copy-done.1, ...), custom_call_target="tpu_custom_call" | custom-call | flops 1610612736 | tf_op jit(solution)/shard_map/pallas_call | solution.py:224
  63.2 2.7 %shard_map.91 = (bf16[2,1024,256]{2,1,0:T(8,128)(2,1)S(1)}, bf16[2,1024,256]{2,1,0:T(8,128)(2,1)S(1)}, f32[1024,256]{1,0:T(8,128)S(1)}, f32[1024,256]{1,0:T(8,128)S(1)}, f32[1024,256]{1,0:T(8,128)S(1)}) custom-call(f32[1024,256]{1,0:T(8,128)S(1)} %shard_map.89.refs_0_, ...), custom_call_target="tpu_custom_call", output_to_operand_aliasing={{2}: (6, {}), {3}: (7, {})} | custom-call | flops 2013265920 | tf_op jit(solution)/shard_map/pallas_call | solution.py:224
  66.0 3.6 %shard_map.93 = (bf16[2,1024,256]{2,1,0:T(8,128)(2,1)S(1)}, bf16[2,1024,256]{2,1,0:T(8,128)(2,1)S(1)}, f32[1024,256]{1,0:T(8,128)S(1)}, f32[1024,256]{1,0:T(8,12...) custom-call(f32[1024,256]{1,0:T(8,128)S(1)} %shard_map.92.refs_0_, ...), custom_call_target="tpu_custom_call", output_to_operand_aliasing={{2}: (8, {}), {3}: (9, {}), {4}: (10, {})} | custom-call | flops 2818572288 | tf_op jit(solution)/shard_map/pallas_call | solution.py:224
  69.6 14.1 %shard_map.95.own = f32[256,256]{1,0:T(8,128)S(1)} custom-call(bf16[2,1024,256]{2,1,0:T(8,128)(2,1)S(1)} %get-tuple-element.88.refs_2_.refs_0_, bf16[2,1024,256]{2,1,0:T(8,128)(2,1)S(1)} %get-tuple-element.89.refs_3_.refs_1_, bf16[2,1024,256]{2,1,0:T(8,128)(2,1)S(1)} %get-tuple-element.99.refs_4_.refs_2_, ...), custom_call_target="tpu_custom_call" | custom-call | flops 9663676416 | tf_op jit(solution)/shard_map/pallas_call | solution.py:224
  83.9 6.2 %collective-permute-done.21.across = f32[256,256]{1,0:T(8,128)S(1)} collective-permute-done((f32[256,256]{1,0:T(8,128)S(1)}, f32[256,256]{1,0:T(8,128)S(1)}, u32[]{:S(2)}, u32[]{:S(2)}) %collective-permute-start.21) | collective-permute-done | bytes 262176 | tf_op jit(solution)/shard_map/ppermute | solution.py:273
  (71 shorter events, 14.5 us)
Async XLA Ops:
  3.3 12.3 %collective-permute-start = (f32[256,256]{1,0:T(8,128)S(1)}, f32[256,256]{1,0:T(8,128)S(1)}, u32[]{:S(2)}, u32[]{:S(2)}) collective-permute-start(f32[256,256]{1,0:T(8,128)S(1)} %get-tuple-element.60.refs_1_), channel_id=1, source_target_pairs={{0,1},{1,2},{2,3},{3,0},{4,5},{5,6},{6,7},{7,4},{8,9},{9,10},{10,1... | collective-permute-start | bytes 786440 | tf_op jit(solution)/shard_map/ppermute | solution.py:316
  6.4 12.9 %collective-permute-start.1 = (f32[520,256]{1,0:T(8,128)S(1)}, f32[520,256]{1,0:T(8,128)S(1)}, u32[]{:S(2)}, u32[]{:S(2)}) collective-permute-start(f32[520,256]{1,0:T(8,128)S(1)} %get-tuple-element.61.refs_2_), channel_id=1, source_target_pairs={{0,16},{4,12},{8,24},{12,4},{16,0},{20,28},{24,8},{28,20},{1,17},{... | collective-permute-start | bytes 1597448 | tf_op jit(solution)/shard_map/ppermute | solution.py:273
  8.0 11.4 %copy-start.2 = (f32[520,256]{1,0:T(8,128)}, f32[520,256]{1,0:T(8,128)S(1)}, u32[]{:S(2)}) copy-start(f32[520,256]{1,0:T(8,128)S(1)} %get-tuple-element.62.refs_0_.refs_2_) | copy-start | bytes 1597444
  8.0 17.2 %collective-permute-start.2 = (f32[256,256]{1,0:T(8,128)S(1)}, f32[256,256]{1,0:T(8,128)S(1)}, u32[]{:S(2)}, u32[]{:S(2)}) collective-permute-start(f32[256,256]{1,0:T(8,128)S(1)} %get-tuple-element.66), channel_id=1, source_target_pairs={{0,3},{1,0},{2,1},{3,2},{4,7},{5,4},{6,5},{7,6},{8,11},{9,8},{10,9... | collective-permute-start | bytes 786440 | tf_op jit(solution)/shard_map/ppermute | solution.py:316
  10.3 15.0 %collective-permute-start.3 = (f32[520,256]{1,0:T(8,128)S(1)}, f32[520,256]{1,0:T(8,128)S(1)}, u32[]{:S(2)}, u32[]{:S(2)}) collective-permute-start(f32[520,256]{1,0:T(8,128)S(1)} %get-tuple-element.62.refs_0_.refs_2_), channel_id=1, source_target_pairs={{0,8},{4,20},{8,0},{12,28},{16,24},{20,4},{24,16},{28,12},{1,9},{5... | collective-permute-start | bytes 1597448 | tf_op jit(solution)/shard_map/ppermute | solution.py:273
  19.4 9.2 %collective-permute-start.5 = (f32[256,256]{1,0:T(8,128)S(1)}, f32[256,256]{1,0:T(8,128)S(1)}, u32[]{:S(2)}, u32[]{:S(2)}) collective-permute-start(f32[256,256]{1,0:T(8,128)S(1)} %get-tuple-element.65.refs_1_), channel_id=1, source_target_pairs={{0,16},{4,12},{8,24},{12,4},{16,0},{20,28},{24,8},{28,20},{1,17},{... | collective-permute-start | bytes 786440 | tf_op jit(solution)/shard_map/ppermute | solution.py:273
  20.9 8.2 %collective-permute-start.4 = (f32[256,256]{1,0:T(8,128)S(1)}, f32[256,256]{1,0:T(8,128)S(1)}, u32[]{:S(2)}, u32[]{:S(2)}) collective-permute-start(f32[256,256]{1,0:T(8,128)S(1)} %get-tuple-element.65.refs_1_), channel_id=1, source_target_pairs={{0,1},{1,2},{2,3},{3,0},{4,5},{5,6},{6,7},{7,4},{8,9},{9,10},{10,1... | collective-permute-start | bytes 786440 | tf_op jit(solution)/shard_map/ppermute | solution.py:316
  24.5 9.5 %collective-permute-start.6 = (f32[520,256]{1,0:T(8,128)S(1)}, f32[520,256]{1,0:T(8,128)S(1)}, u32[]{:S(2)}, u32[]{:S(2)}) collective-permute-start(f32[520,256]{1,0:T(8,128)S(1)} %get-tuple-element.68.refs_3_.refs_5_), channel_id=1, source_target_pairs={{0,8},{4,20},{8,0},{12,28},{16,24},{20,4},{24,16},{28,12},{1,9},{5... | collective-permute-start | bytes 1597448 | tf_op jit(solution)/shard_map/ppermute | solution.py:273
  25.3 8.8 %copy-start.6 = (f32[256,256]{1,0:T(8,128)}, f32[256,256]{1,0:T(8,128)S(1)}, u32[]{:S(2)}) copy-start(f32[256,256]{1,0:T(8,128)S(1)} %get-tuple-element.67.refs_0_.refs_1_) | copy-start | bytes 786436
  25.4 12.1 %collective-permute-start.7 = (f32[256,256]{1,0:T(8,128)S(1)}, f32[256,256]{1,0:T(8,128)S(1)}, u32[]{:S(2)}, u32[]{:S(2)}) collective-permute-start(f32[256,256]{1,0:T(8,128)S(1)} %get-tuple-element.67.refs_0_.refs_1_), channel_id=1, source_target_pairs={{0,8},{4,20},{8,0},{12,28},{16,24},{20,4},{24,16},{28,12},{1,9},{5... | collective-permute-start | bytes 786440 | tf_op jit(solution)/shard_map/ppermute | solution.py:273
  26.8 10.7 %collective-permute-start.8 = (f32[256,256]{1,0:T(8,128)S(1)}, f32[256,256]{1,0:T(8,128)S(1)}, u32[]{:S(2)}, u32[]{:S(2)}) collective-permute-start(f32[256,256]{1,0:T(8,128)S(1)} %get-tuple-element.70.refs_1_), channel_id=1, source_target_pairs={{0,16},{4,12},{8,24},{12,4},{16,0},{20,28},{24,8},{28,20},{1,17},{... | collective-permute-start | bytes 786440 | tf_op jit(solution)/shard_map/ppermute | solution.py:273
  34.1 8.7 %collective-permute-start.9 = (f32[256,256]{1,0:T(8,128)S(1)}, f32[256,256]{1,0:T(8,128)S(1)}, u32[]{:S(2)}, u32[]{:S(2)}) collective-permute-start(f32[256,256]{1,0:T(8,128)S(1)} %get-tuple-element.71.refs_4_), channel_id=1, source_target_pairs={{0,8},{4,20},{8,0},{12,28},{16,24},{20,4},{24,16},{28,12},{1,9},{5... | collective-permute-start | bytes 786440 | tf_op jit(solution)/shard_map/ppermute | solution.py:273
  35.8 9.2 %collective-permute-start.10 = (f32[256,256]{1,0:T(8,128)S(1)}, f32[256,256]{1,0:T(8,128)S(1)}, u32[]{:S(2)}, u32[]{:S(2)}) collective-permute-start(f32[256,256]{1,0:T(8,128)S(1)} %get-tuple-element.78.refs_4_), channel_id=1, source_target_pairs={{0,16},{4,12},{8,24},{12,4},{16,0},{20,28},{24,8},{28,20},{1,17},{... | collective-permute-start | bytes 786440 | tf_op jit(solution)/shard_map/ppermute | solution.py:273
  37.1 8.6 %collective-permute-start.11 = (f32[256,256]{1,0:T(8,128)S(1)}, f32[256,256]{1,0:T(8,128)S(1)}, u32[]{:S(2)}, u32[]{:S(2)}) collective-permute-start(f32[256,256]{1,0:T(8,128)S(1)} %get-tuple-element.79.refs_0_), channel_id=1, source_target_pairs={{0,8},{4,20},{8,0},{12,28},{16,24},{20,4},{24,16},{28,12},{1,9},{5... | collective-permute-start | bytes 786440 | tf_op jit(solution)/shard_map/ppermute | solution.py:273
  37.5 10.9 %collective-permute-start.12 = (f32[256,256]{1,0:T(8,128)S(1)}, f32[256,256]{1,0:T(8,128)S(1)}, u32[]{:S(2)}, u32[]{:S(2)}) collective-permute-start(f32[256,256]{1,0:T(8,128)S(1)} %get-tuple-element.82.refs_1_), channel_id=1, source_target_pairs={{0,8},{4,20},{8,0},{12,28},{16,24},{20,4},{24,16},{28,12},{1,9},{5... | collective-permute-start | bytes 786440 | tf_op jit(solution)/shard_map/ppermute | solution.py:273
  39.4 9.1 %collective-permute-start.13 = (f32[256,256]{1,0:T(8,128)S(1)}, f32[256,256]{1,0:T(8,128)S(1)}, u32[]{:S(2)}, u32[]{:S(2)}) collective-permute-start(f32[256,256]{1,0:T(8,128)S(1)} %get-tuple-element.83.refs_3_), channel_id=1, source_target_pairs={{0,1},{1,2},{2,3},{3,0},{4,5},{5,6},{6,7},{7,4},{8,9},{9,10},{10,1... | collective-permute-start | bytes 786440 | tf_op jit(solution)/shard_map/ppermute | solution.py:316
  45.7 6.4 %collective-permute-start.14 = (f32[256,256]{1,0:T(8,128)S(1)}, f32[256,256]{1,0:T(8,128)S(1)}, u32[]{:S(2)}, u32[]{:S(2)}) collective-permute-start(f32[256,256]{1,0:T(8,128)S(1)} %get-tuple-element.85.refs_1_), channel_id=1, source_target_pairs={{0,8},{4,20},{8,0},{12,28},{16,24},{20,4},{24,16},{28,12},{1,9},{5... | collective-permute-start | bytes 786440 | tf_op jit(solution)/shard_map/ppermute | solution.py:273
  47.0 8.0 %collective-permute-start.15 = (f32[256,256]{1,0:T(8,128)S(1)}, f32[256,256]{1,0:T(8,128)S(1)}, u32[]{:S(2)}, u32[]{:S(2)}) collective-permute-start(f32[256,256]{1,0:T(8,128)S(1)} %get-tuple-element.86.refs_0_), channel_id=1, source_target_pairs={{0,8},{4,20},{8,0},{12,28},{16,24},{20,4},{24,16},{28,12},{1,9},{5... | collective-permute-start | bytes 786440 | tf_op jit(solution)/shard_map/ppermute | solution.py:273
  48.1 6.9 %collective-permute-start.16 = (f32[3104,256]{1,0:T(8,128)S(1)}, f32[3104,256]{1,0:T(8,128)S(1)}, u32[]{:S(2)}, u32[]{:S(2)}) collective-permute-start(f32[3104,256]{1,0:T(8,128)S(1)} %shard_map.85.refs_0_), channel_id=1, source_target_pairs={{0,4},{4,0},{8,12},{12,8},{1,5},{5,1},{9,13},{13,9},{2,6},{6,2},{1... | collective-permute-start | bytes 9535496 | tf_op jit(solution)/shard_map/ppermute | solution.py:279
  49.8 8.4 %collective-permute-start.18 = (f32[256,256]{1,0:T(8,128)S(1)}, f32[256,256]{1,0:T(8,128)S(1)}, u32[]{:S(2)}, u32[]{:S(2)}) collective-permute-start(f32[256,256]{1,0:T(8,128)S(1)} %get-tuple-element.93.refs_12_), channel_id=1, source_target_pairs={{0,3},{1,0},{2,1},{3,2},{4,7},{5,4},{6,5},{7,6},{8,11},{9,8},{10,9... | collective-permute-start | bytes 786440 | tf_op jit(solution)/shard_map/ppermute | solution.py:316
  51.4 18.1 %collective-permute-start.20 = (f32[256,256]{1,0:T(8,128)}, f32[256,256]{1,0:T(8,128)}, u32[]{:S(2)}, u32[]{:S(2)}) collective-permute-start(f32[256,256]{1,0:T(8,128)} %get-tuple-element.112.refs_13_), channel_id=1, source_target_pairs={{0,1},{1,2},{2,3},{3,0},{4,5},{5,6},{6,7},{7,4},{8,9},{9,10},{10,1... | collective-permute-start | bytes 786440 | tf_op jit(solution)/shard_map/ppermute | solution.py:316
  52.2 6.0 %collective-permute-start.17 = (f32[1024,256]{1,0:T(8,128)S(1)}, f32[1024,256]{1,0:T(8,128)S(1)}, u32[]{:S(2)}, u32[]{:S(2)}) collective-permute-start(f32[1024,256]{1,0:T(8,128)S(1)} %shard_map.89.refs_0_), channel_id=1, source_target_pairs={{0,4},{4,0},{8,12},{12,8},{1,5},{5,1},{9,13},{13,9},{2,6},{6,2},{1... | collective-permute-start | bytes 3145736 | tf_op jit(solution)/shard_map/ppermute | solution.py:279
  55.3 10.6 %collective-permute-start.19 = (f32[1024,256]{1,0:T(8,128)S(1)}, f32[1024,256]{1,0:T(8,128)S(1)}, u32[]{:S(2)}, u32[]{:S(2)}) collective-permute-start(f32[1024,256]{1,0:T(8,128)S(1)} %shard_map.92.refs_0_), channel_id=1, source_target_pairs={{0,4},{4,0},{8,12},{12,8},{1,5},{5,1},{9,13},{13,9},{2,6},{6,2},{1... | collective-permute-start | bytes 3145736 | tf_op jit(solution)/shard_map/ppermute | solution.py:279
  83.7 6.4 %collective-permute-start.21 = (f32[256,256]{1,0:T(8,128)S(1)}, f32[256,256]{1,0:T(8,128)S(1)}, u32[]{:S(2)}, u32[]{:S(2)}) collective-permute-start(f32[256,256]{1,0:T(8,128)S(1)} %shard_map.95.own), channel_id=1, source_target_pairs={{0,16},{4,20},{8,24},{12,28},{16,0},{20,4},{24,8},{28,12},{1,17},{... | collective-permute-start | bytes 786440 | tf_op jit(solution)/shard_map/ppermute | solution.py:273
  (12 other events, 31.3 us)

commit v3 on v2

--- a/solution.py
+++ b/solution.py
@@ -10,7 +10,32 @@
 NTERMS = 6
 MIB = 2**20
 TILE = 8
-GATE = 10**11
+GATE = 2 * 10**10
+
+SLOTS = {
+    "p1": (0, 3),
+    "a0": (1, 2),
+    "b0": (1, 3),
+    "d0": (2, 4),
+    "q2": (2, 5),
+    "q3": (3, 6),
+    "a1": (3, 5),
+    "b1": (4, 6),
+    "d1": (5, 7),
+    "a2": (5, 7),
+    "b2": (6, 8),
+    "a3": (6, 8),
+    "d2": (7, 9),
+    "b3": (7, 9),
+    "t01": (7, 9),
+    "d3": (8, 10),
+    "l3": (8, 11),
+    "t2": (9, 11),
+    "tx": (9, 11),
+    "t3": (10, 12),
+}
+KERNELS = {'01': 10, '2': 12}
+ANCHOR = 12
 
 
 class Grid:
@@ -90,6 +115,20 @@
     fetch(grid, first, second, out, sem).wait()
 
 
+def number_kernel(ids, out, number, sem):
+    copy = pltpu.make_async_copy(ids, number, sem)
+    copy.start()
+    copy.wait()
+    out[...] = jnp.full(out.shape, number[0].astype(jnp.float32))
+
+
+def extend_kernel(piece, block, number, out):
+    rows = piece.shape[0]
+    out[:rows, :] = piece[...]
+    out[rows : 2 * rows, :] = block[0]
+    out[2 * rows :, :] = number[...]
+
+
 def panel_kernel(grid, start, gains, *refs):
     rows, cols = grid.shape
     panel, weight = refs[-2:]
@@ -131,22 +170,23 @@
         here += stop - start
 
 
-def absorb_kernel(grid, done, new, height, *refs):
-    rows, cols = grid.shape
-    n_pieces = grid.cores * len(grid.hops)
-    pieces = []
-    while len(pieces) < n_pieces:
-        pieces += [refs[0].at[pl.ds(i, height), :] for i in range(0, refs[0].shape[0], height)]
-        refs = refs[1:]
-    old, sums, refs = refs[: 2 * done], refs[2 * done : 3 * done], refs[3 * done :]
+def ingest(grid, refs, new, height, highs, lows):
+    rows = grid.shape[0]
+    pieces = [ref.at[pl.ds(i, height), :] for ref in refs for i in range(0, ref.shape[0], height)]
+    for piece, (side, row) in zip(pieces, grid.origins()):
+        for j in range(new):
+            high, low = split(piece[j * rows : (j + 1) * rows, :])
+            highs[j][side, span(row, rows), :] = high
+            lows[j][side, span(row, rows), :] = low
+
+
+def absorb_kernel(grid, done, new, height, mine, theirs, *refs):
+    cols = grid.shape[1]
+    old, sums = refs[: 2 * done], refs[2 * done : 3 * done]
     refs = refs[-(3 * new + done) :]
     fresh, out_sums = refs[: 2 * new], refs[2 * new :]
     highs, lows = old[:done] + fresh[:new], old[done:] + fresh[new:]
-    for piece, (side, row) in zip(pieces, grid.origins()):
-        for j in range(new):
-            high, low = split(piece[j * rows : (j + 1) * rows, :])
-            highs[done + j][side, span(row, rows), :] = high
-            lows[done + j][side, span(row, rows), :] = low
+    ingest(grid, [mine, theirs], new, height, fresh[:new], fresh[new:])
     for n in range(done + new):
         total = sums[n][...] if n < done else None
         for k in range(done if n < done else 0, done + new):
@@ -156,57 +196,81 @@
         out_sums[n][...] = total
 
 
-def last_kernel(grid, *refs):
+def horner_kernel(grid, *refs):
+    rows, cols = grid.shape
     blocks = grid.blocks
-    highs, lows, sums = refs[:blocks], refs[blocks : 2 * blocks], refs[2 * blocks : 3 * blocks]
-    left, refs = refs[3 * blocks : 4 * blocks], refs[4 * blocks :]
-    base, weight, reflect, out, power_high, power_low, left_high, left_low, state, z_high, z_low = refs
-    rows, cols = left[0].shape
-    upper = grid.upper()
+    old = blocks - 1
+    mine, theirs, refs = refs[0], refs[1], refs[2:]
+    highs, lows, sums, refs = refs[:old], refs[old : 2 * old], refs[2 * old : 3 * old], refs[3 * old :]
+    panel, _, out, high, low, power_high, power_low, pair = refs
+    width = out.shape[1]
+    ingest(grid, [mine, theirs], 1, rows, [high], [low])
+    highs, lows = (*highs, high), (*lows, low)
     places = [grid.place(j) for j in range(blocks)]
-
-    def take(source):
+    for n in range(blocks):
+        total = sums[n][...] if n < old else None
+        for k in range(old if n < old else 0, blocks):
+            here = span(places[k], cols)
+            term = dot3(highs[k][0], lows[k][0], highs[n][1, here, :], lows[n][1, here, :])
+            total = term if total is None else total + term
+        here = pl.ds(n * cols, cols)
+        power_high[:, here], power_low[:, here] = split(total)
+
+    ours = span(lax.rem(grid.row(), grid.cores), width)
+
+    def take(read):
         for j in range(blocks):
+            z_high, z_low = split(read(span(places[j], cols)))
             here = pl.ds(j * cols, cols)
-            z_high[here, :], z_low[here, :] = split(source[span(places[j], cols), :])
-
-    for j in range(blocks):
-        here = pl.ds(j * cols, cols)
-        power_high[:, here], power_low[:, here] = split(sums[j][...])
-
-    @pl.when(upper)
+            pair[here, :width], pair[here, width:] = z_high, z_low
+
+    take(lambda here: panel[here, ours])
+
+    @pl.loop(0, NTERMS - 1)
+    def _(_):
+        both = dot(power_high[...], pair[...])
+        rest = dot(power_low[...], pair[:, :width])
+        out[...] = panel[:, ours] + (both[:, :width] + (both[:, width:] + rest))
+        take(lambda here: out[here, :])
+
+
+def left_kernel(grid, *refs):
+    blocks = grid.blocks
+    highs, lows, left, (weight, _, left_high, left_low) = refs[:blocks], refs[blocks : 2 * blocks], refs[2 * blocks : 3 * blocks], refs[3 * blocks :]
+    rows, cols = grid.shape
+    places = [grid.place(j) for j in range(blocks)]
+    left = [ref.at[pl.ds(ref.shape[0] - rows, rows), :] for ref in left]
+
+    @pl.when(grid.upper())
     def _():
+        scaled = [split(left[j][...] * weight[pl.ds(places[j], 1), :]) for j in range(blocks)]
         for n in range(blocks):
             total = None
             for j in range(blocks):
-                scaled = left[j][...] * weight[pl.ds(places[j], 1), :]
-                term = dot3(*split(scaled), highs[n][1, span(places[j], cols), :], lows[n][1, span(places[j], cols), :])
+                term = dot3(*scaled[j], highs[n][1, span(places[j], cols), :], lows[n][1, span(places[j], cols), :])
                 total = term if total is None else total + term
             here = pl.ds(n * cols, cols)
             left_high[:, here], left_low[:, here] = split(total)
 
-    @pl.when(jnp.logical_not(upper))
+    @pl.when(jnp.logical_not(grid.upper()))
     def _():
         for n in range(blocks):
             here = pl.ds(n * cols, cols)
             left_high[:, here], left_low[:, here] = split(left[n][...])
 
-    take(base)
-
-    @pl.loop(0, NTERMS - 1)
-    def _(_):
-        state[...] = base[...] + dot3(power_high[...], power_low[...], z_high[...], z_low[...])
-        take(state)
-
+
+def last_kernel(grid, left_high, left_low, reflect, *refs):
+    parts, (out, z_high, z_low) = refs[:-3], refs[-3:]
+    cols = grid.shape[1]
+    width = parts[0].shape[1]
+    core = lax.rem(grid.row(), grid.cores)
+    for i, part in enumerate(parts):
+        ours = span(core if i == 0 else 1 - core, width)
+        for j in range(grid.blocks):
+            here = pl.ds(j * cols, cols)
+            z_high[here, ours], z_low[here, ours] = split(part[span(grid.place(j), cols), :])
     result = dot3(left_high[...], left_low[...], z_high[...], z_low[...])
-
-    @pl.when(upper)
-    def _():
-        out[...] = reflect[0] + result
-
-    @pl.when(jnp.logical_not(upper))
-    def _():
-        out[...] = result
+    out[...] = jnp.where(grid.upper(), reflect[0] + result, result)
 
 
 def finish_kernel(grid, own, across, reflect, transmit):
@@ -215,7 +279,7 @@
     transmit[0] = jnp.where(upper, across[...], own[...])
 
 
-def call(kernel, outs, operands, scalars=(), loose=(), far=(), scratch=(), aliases=None, flops=0, limit=4 * MIB):
+def call(kernel, outs, operands, scalars=(), loose=(), far=(), scratch=(), aliases=None, flops=0, moved=0, limit=4 * MIB):
     spaces = [pltpu.VMEM] * len(operands)
     for numbers, space in ((scalars, pltpu.SMEM), (far, pltpu.HBM), (loose, pl.ANY)):
         for i in numbers:
@@ -229,7 +293,7 @@
         scratch_shapes=list(scratch),
         input_output_aliases=aliases or {},
         compiler_params=pltpu.CompilerParams(vmem_limit_bytes=limit),
-        cost_estimate=pl.CostEstimate(flops=flops, bytes_accessed=0, transcendentals=0),
+        cost_estimate=pl.CostEstimate(flops=flops, bytes_accessed=moved, transcendentals=0),
     )(*operands)
 
 
@@ -240,7 +304,7 @@
 def gate(values, *needs):
     count = len(values)
     kernel = functools.partial(gate_kernel, count)
-    return call(kernel, [single(*v.shape) for v in values], [*values, *needs], loose=range(count, count + len(needs)), flops=GATE)
+    return call(kernel, [single(*v.shape) for v in values], [*values, *needs], loose=range(count, count + len(needs)), flops=GATE, moved=10 * GATE)
 
 
 def pack(blocks, *needs):
@@ -321,66 +385,122 @@
     def b_hop(value):
         return plane(value, hops[2])
 
-    p0 = jnp.where(grid.upper(), reflect_bwd[0], reflect_fwd[0])
-    number = jnp.broadcast_to(material_ids.astype(jnp.float32), (TILE, cols))
-    e0 = jnp.concatenate([p0, transmit_fwd[0], number], axis=0)
-
-    token = number
-
-    def step(*values):
-        nonlocal token
-        token, *rest = gate([token, *values])
-        return rest
-
-    p0, e0 = step(p0, e0)
-    p1, a0 = along(p0, 1), a_hop(e0)
-    p0, e0 = step(p0, e0)
-    p2, b0 = along(p0, -1), b_hop(e0)
-    p1, a0 = step(p1, a0)
-    p3, a1, d0 = along(p1, 1), a_hop(p1), b_hop(a0)
-    p1, p2, b0 = step(p1, p2, b0)
-    b1, a2 = b_hop(p1), a_hop(p2)
-    l0 = choose(transmit_bwd, transmit_fwd, p1)
-    p2, p3, a1, d0, l0 = step(p2, p3, a1, d0, l0)
-    d1, a3, b2 = b_hop(a1), a_hop(p3), b_hop(p2)
-    b1, a2, l0 = step(b1, a2, l0)
-    d2, l1 = b_hop(a2), along(l0, 1)
-    d1, a3, b2, p3 = step(d1, a3, b2, p3)
-    d3, b3 = b_hop(a3), b_hop(p3)
-    mine01 = []
-    for zero, one in ((e0, p1), (a0, a1), (b0, b1), (d0, d1)):
-        mine01 += [(zero, 0, rows), one, (zero, rows, zero.shape[0])]
-    mine01 = pack(mine01)
-    theirs01 = sibling(mine01)
-    d2, l1, l0 = step(d2, l1, l0)
-    l2 = along(l0, -1)
-    mine2 = pack([p2, a2, b2, d2])
-    theirs2 = sibling(mine2)
-    d3, b3, theirs01 = step(d3, b3, theirs01)
-    l3 = along(l1, 1)
-    mine3 = pack([p3, a3, b3, d3])
-    theirs3 = sibling(mine3)
-    absorb([mine01, theirs01], 2, 3 * rows + TILE, 1, [])
-    theirs2, l2 = step(theirs2, l2)
+    upper_own = jnp.concatenate([reflect_bwd[0], transmit_bwd[0]], axis=0)
+    lower_own = jnp.concatenate([reflect_fwd[0], transmit_fwd[0]], axis=0)
+    values = {"q0": jnp.where(grid.upper(), upper_own, lower_own)}
+    values["token"] = call(
+        number_kernel,
+        single(TILE, cols),
+        [material_ids],
+        far=(0,),
+        scratch=[pltpu.SMEM(material_ids.shape, jnp.int32), pltpu.SemaphoreType.DMA],
+    )
+    end = 2 * rows + TILE
+    up, down = functools.partial(along, shift=1), functools.partial(along, shift=-1)
+    moves = {
+        "p1": (up, "p0"),
+        "q2": (down, "q0"),
+        "q3": (up, "r1"),
+        "l3": (up, "l1"),
+        **{f"a{i}": (a_hop, "e1" if i == 1 else f"p{i}") for i in range(4)},
+        **{f"b{i}": (b_hop, "e1" if i == 1 else f"p{i}") for i in range(4)},
+        **{f"d{i}": (b_hop, f"a{i}") for i in range(4)},
+        **{f"t{m}": (sibling, f"m{m}") for m in ("01", "2", "3", "x")},
+    }
+
+    def head(name):
+        return (values[name], 0, rows)
+
+    def tail(name, stop):
+        return (values[name], rows, stop)
+
+    def packed(*names):
+        return names, lambda: pack([head(n) for n in names])
+
+    made = {
+        "e1": (("p1",), lambda: call(extend_kernel, single(end, cols), [values["p1"], transmit_fwd, values["token"]])),
+        "r1": (("p1",), lambda: pack([values["p1"], tail("q0", 2 * rows)])),
+        "l1": (("q3",), lambda: pack([tail("q3", 2 * rows)])),
+        "p0": packed("q0"),
+        "p2": packed("q2"),
+        "p3": packed("q3"),
+        "m01": packed("q0", "p1", "a0", "a1", "b0", "b1", "d0", "d1"),
+        "m2": packed("q2", "a2", "b2", "d2"),
+        "m3": packed("q3", "a3", "b3", "d3"),
+        "mx": (("a1", "b1", "d1"), lambda: pack([tail(n, end) for n in ("e1", "a1", "b1", "d1")])),
+    }
+    kernels = {"01": (2, 2 * rows), "2": (1, rows)}
+
+    def absorb_named(name):
+        new, height = kernels[name]
+        absorb([values[f"m{name}"], values[f"t{name}"]], new, height, 1, [])
+
+    def pass_gate(gate_number, *needs):
+        starting = [t for t in SLOTS if t in moves and SLOTS[t][0] == gate_number]
+        ending = [t for t in SLOTS if t in moves and SLOTS[t][1] == gate_number]
+        needs = list(needs)
+        for name, number in KERNELS.items():
+            if number == gate_number:
+                absorb_named(name)
+                needs.append(highs[-1])
+        passed = ["token"]
+        for t in starting:
+            source = moves[t][1]
+            if source not in values:
+                sources = made[source][0]
+                source = max(sources, key=lambda n: SLOTS[n][1] if n in SLOTS else -1) if sources else "token"
+            if source not in passed:
+                passed.append(source)
+        needs += [values[t] for t in ending if t not in passed]
+        for name, value in zip(passed, gate([values[n] for n in passed], *needs)):
+            values[name] = value
+        for t in starting:
+            function, source = moves[t]
+            if source not in values:
+                values[source] = made[source][1]()
+            with jax.named_scope(t):
+                values[t] = function(values[source])
+
+    for gate_number in range(ANCHOR + 1):
+        pass_gate(gate_number)
+    for name in ("01", "2"):
+        if name not in KERNELS:
+            absorb_named(name)
     panel, weight = call(
-        functools.partial(panel_kernel, grid, 2 * rows),
+        functools.partial(panel_kernel, grid, 0),
         [single(order, cols), single(-(-order // cols // TILE) * TILE, cols)],
-        [interface_gain, mine01, theirs01],
+        [interface_gain, values["mx"], values["tx"]],
     )
-    absorb([mine2, theirs2], 1, rows, 1, [])
-    absorb([mine3, theirs3], 1, rows, 1, [])
-    left = [l0, l1, l2, l3]
-
+    width = cols // cores
+    operands = [values["m3"], values["t3"], *highs, *lows, *sums, panel]
+    part, high, low = call(
+        functools.partial(horner_kernel, grid),
+        [single(order, width), half, half],
+        [*operands, values["token"]],
+        loose=(len(operands),),
+        scratch=[pltpu.VMEM((order, order), jnp.bfloat16)] * 2 + [pltpu.VMEM((order, 2 * width), jnp.bfloat16)],
+        flops=10 * 6 * NTERMS * order * order * width,
+        limit=10 * MIB,
+    )
+    highs, lows = highs + [high], lows + [low]
+    parts = [part] + ([sibling(part)] if cores == 2 else [])
+    for gate_number in range(ANCHOR + 1, 1 + max(t[1] for t in SLOTS.values())):
+        pass_gate(gate_number, part)
+    left = [values[n] for n in ("q0", "q3", "q2", "l3")]
+    operands = highs + lows + left + [weight]
+    left = call(
+        functools.partial(left_kernel, grid),
+        [jax.ShapeDtypeStruct((rows, order), jnp.bfloat16)] * 2,
+        [*operands, values["token"]],
+        loose=(len(operands),),
+        flops=6 * rows * order * order,
+    )
     result = call(
         functools.partial(last_kernel, grid),
         single(rows, cols),
-        highs + lows + sums + left + [panel, weight, reflect_fwd],
-        scratch=[pltpu.VMEM((order, order), jnp.bfloat16)] * 2
-        + [pltpu.VMEM((rows, order), jnp.bfloat16)] * 2
-        + [pltpu.VMEM((order, cols), jnp.float32)]
-        + [pltpu.VMEM((order, cols), jnp.bfloat16)] * 2,
-        flops=6 * NTERMS * order * order * cols,
-        limit=16 * MIB,
+        [*left, reflect_fwd, *parts],
+        scratch=[pltpu.VMEM((order, cols), jnp.bfloat16)] * 2,
+        flops=6 * rows * order * cols,
     )
     across = plane(result, both_cores((1, 0)))
     outs = [single(1, rows, cols)] * 2

time: 91.2 us -> 84.9 us (0.931)
  Pallas kernels: 26.8 us -> 21.1 us
  waiting for transfers between devices: 32.3 us -> 34.1 us
  local copies, waits for them, and re-layouts: 1.82 us -> 0.89 us
    ppermute x6 -> x4, waiting for transfers between devices: 7.21 us -> 14.9 us  [along(): lax.ppermute(value, 'col', [(i, (i + shift) % blocks) for i in range(bloc...]
    ppermute x13, waiting for transfers between devices: 25.1 us -> 19.2 us  [plane(): return lax.ppermute(value, ('layer', 'row'), route)]
    pallas_call x20 -> x31, Pallas kernels: 26.8 us -> 21.1 us  [call(): pl.pallas_call(kernel, out_shape=outs, in_specs=specs, out_specs=jax.tree...]
    ppermute x6 -> x4, starting transfers between devices: 11.5 us -> 7.04 us  [along(): lax.ppermute(value, 'col', [(i, (i + shift) % blocks) for i in range(bloc...]
    ppermute x13, starting transfers between devices: 14.8 us -> 17.1 us  [plane(): return lax.ppermute(value, ('layer', 'row'), route)]
    ppermute x3 -> x5, starting transfers between devices: 0.14 us -> 1.37 us  [sibling(): lax.ppermute(value, 'row', [(i, i ^ 1) for i in range(grid.row_count)])]
    concatenate x1 -> x0, other arithmetic: 0.99 us -> none  [on_device(): e0 = jnp.concatenate([p0, transmit_fwd[0], number], axis=0)]
    unnamed x28 -> x10, local copies, waits for them, and re-layouts: 1.82 us -> 0.89 us
  transfers between devices with their start and end apart: 22 -> 22, of which waited for: 13 -> 9; matrix products, arithmetic and copies ran while one was open for 0% -> 0% of each run, Pallas kernels for 13% -> 10%
where the time goes in v3:
time: 84.9 us; the launch traced here: 84.5 us
  waiting for transfers between devices  34.1 us (40%)
  starting transfers between devices  25.6 us (30%)
  Pallas kernels  21.1 us (25%)
  between operations  1.63 us (2%)
  other arithmetic  1.26 us (1%)
  local copies, waits for them, and re-layouts  0.89 us (1%)
    pallas_call x31, Pallas kernels, call(): pl.pallas_call(kernel, out_shape=outs, in_specs=specs, out_specs=jax.tree...  21.1 us
    ppermute x13, waiting for transfers between devices, plane(): return lax.ppermute(value, ('layer', 'row'), route)  19.2 us
    ppermute x13, starting transfers between devices, plane(): return lax.ppermute(value, ('layer', 'row'), route)  17.1 us
    ppermute x4, waiting for transfers between devices, along(): lax.ppermute(value, 'col', [(i, (i + shift) % blocks) for i in range(bloc...  14.9 us
    ppermute x4, starting transfers between devices, along(): lax.ppermute(value, 'col', [(i, (i + shift) % blocks) for i in range(bloc...  7.04 us
  transfers between devices with their start and end apart: 22, of which 9 were waited for; matrix products, arithmetic and copies ran while one was open for 0% of the time, Pallas kernels for 10%

profile of v3, /device:TPU:0, one launch (start us, length us, event | category | flops | bytes accessed | tf_op | source)
XLA Modules:
  0.0 84.5 jit_solution(11460616128901101914)
XLA Ops:
  1.8 1.3 %maximum_select_fusion.refs_1_ = f32[512,256]{1,0:T(8,128)S(1)} fusion(f32[256,256]{1,0:T(8,128)} %bitcast.6, f32[256,256]{1,0:T(8,128)} %bitcast.7, f32[256,256]{1,0:T(8,128)} %bitcast.5, f32[256,256]{1,0:T(8,128)} %bitcast.4, pred[]{:T(512)S(6)} %lt.3), kind=kLoop, calls=%fused_computation | loop fusion | flops 393216 | bytes 1572865 | tf_op jit(solution)/shard_map/jit(_where)/select_n | solution.py:390
  3.2 3.0 %collective-permute-start = (f32[256,256]{1,0:T(8,128)S(1)}, f32[256,256]{1,0:T(8,128)S(1)}, u32[]{:S(2)}, u32[]{:S(2)}) collective-permute-start(f32[256,256]{1,0:T(8,128)S(1)} %get-tuple-element.52), channel_id=1, source_target_pairs={{0,16},{4,12},{8,24},{12,4},{16,0},{20,28},{24,8},{28,20},{1,17},{... | collective-permute-start | bytes 786440 | tf_op jit(solution)/shard_map/a0/ppermute | solution.py:337
  6.2 1.5 %collective-permute-start.2 = (f32[256,256]{1,0:T(8,128)S(1)}, f32[256,256]{1,0:T(8,128)S(1)}, u32[]{:S(2)}, u32[]{:S(2)}) collective-permute-start(f32[256,256]{1,0:T(8,128)S(1)} %get-tuple-element.52), channel_id=1, source_target_pairs={{0,8},{4,20},{8,0},{12,28},{16,24},{20,4},{24,16},{28,12},{1,9},{5... | collective-permute-start | bytes 786440 | tf_op jit(solution)/shard_map/b0/ppermute | solution.py:337
  7.7 1.6 %collective-permute-start.1 = (f32[256,256]{1,0:T(8,128)S(1)}, f32[256,256]{1,0:T(8,128)S(1)}, u32[]{:S(2)}, u32[]{:S(2)}) collective-permute-start(f32[256,256]{1,0:T(8,128)S(1)} %shard_map.79.refs_1_), channel_id=1, source_target_pairs={{0,1},{1,2},{2,3},{3,0},{4,5},{5,6},{6,7},{7,4},{8,9},{9,10},{10,1... | collective-permute-start | bytes 786440 | tf_op jit(solution)/shard_map/p1/ppermute | solution.py:380
  9.3 3.5 %collective-permute-done.refs_1_ = f32[256,256]{1,0:T(8,128)S(1)} collective-permute-done((f32[256,256]{1,0:T(8,128)S(1)}, f32[256,256]{1,0:T(8,128)S(1)}, u32[]{:S(2)}, u32[]{:S(2)}) %collective-permute-start) | collective-permute-done | bytes 262176 | tf_op jit(solution)/shard_map/a0/ppermute | solution.py:337
  12.9 1.6 %collective-permute-start.3 = (f32[256,256]{1,0:T(8,128)S(1)}, f32[256,256]{1,0:T(8,128)S(1)}, u32[]{:S(2)}, u32[]{:S(2)}) collective-permute-start(f32[256,256]{1,0:T(8,128)S(1)} %get-tuple-element.56.refs_2_), channel_id=1, source_target_pairs={{0,8},{4,20},{8,0},{12,28},{16,24},{20,4},{24,16},{28,12},{1,9},{5... | collective-permute-start | bytes 786440 | tf_op jit(solution)/shard_map/d0/ppermute | solution.py:337
  14.5 3.7 %collective-permute-start.5 = (f32[512,256]{1,0:T(8,128)S(1)}, f32[512,256]{1,0:T(8,128)S(1)}, u32[]{:S(2)}, u32[]{:S(2)}) collective-permute-start(f32[512,256]{1,0:T(8,128)S(1)} %get-tuple-element.53.refs_1_.refs_0_.refs_8_), channel_id=1, source_target_pairs={{0,3},{1,0},{2,1},{3,2},{4,7},{5,4},{6,5},{7,6},{8,11},{9,8},{10,9... | collective-permute-start | bytes 1572872 | tf_op jit(solution)/shard_map/q2/ppermute | solution.py:380
  19.3 1.6 %collective-permute-start.4 = (f32[520,256]{1,0:T(8,128)S(1)}, f32[520,256]{1,0:T(8,128)S(1)}, u32[]{:S(2)}, u32[]{:S(2)}) collective-permute-start(f32[520,256]{1,0:T(8,128)S(1)} %shard_map.83.refs_1_), channel_id=1, source_target_pairs={{0,16},{4,12},{8,24},{12,4},{16,0},{20,28},{24,8},{28,20},{1,17},{... | collective-permute-start | bytes 1597448 | tf_op jit(solution)/shard_map/a1/ppermute | solution.py:337
  20.9 1.4 %collective-permute-start.6 = (f32[520,256]{1,0:T(8,128)S(1)}, f32[520,256]{1,0:T(8,128)S(1)}, u32[]{:S(2)}, u32[]{:S(2)}) collective-permute-start(f32[520,256]{1,0:T(8,128)S(1)} %get-tuple-element.60.refs_0_), channel_id=1, source_target_pairs={{0,8},{4,20},{8,0},{12,28},{16,24},{20,4},{24,16},{28,12},{1,9},{5... | collective-permute-start | bytes 1597448 | tf_op jit(solution)/shard_map/b1/ppermute | solution.py:337
  22.3 9.2 %collective-permute-done.5.refs_2_ = f32[512,256]{1,0:T(8,128)S(1)} collective-permute-done((f32[512,256]{1,0:T(8,128)S(1)}, f32[512,256]{1,0:T(8,128)S(1)}, u32[]{:S(2)}, u32[]{:S(2)}) %collective-permute-start.5) | collective-permute-done | bytes 524320 | tf_op jit(solution)/shard_map/q2/ppermute | solution.py:380
  33.9 5.7 %collective-permute-done.7.refs_2_ = f32[512,256]{1,0:T(8,128)S(1)} collective-permute-done((f32[512,256]{1,0:T(8,128)S(1)}, f32[512,256]{1,0:T(8,128)S(1)}, u32[]{:S(2)}, u32[]{:S(2)}) %collective-permute-start.7) | collective-permute-done | bytes 524320 | tf_op jit(solution)/shard_map/q3/ppermute | solution.py:380
  40.2 1.4 %collective-permute-start.11 = (f32[256,256]{1,0:T(8,128)S(1)}, f32[256,256]{1,0:T(8,128)S(1)}, u32[]{:S(2)}, u32[]{:S(2)}) collective-permute-start(f32[256,256]{1,0:T(8,128)S(1)} %get-tuple-element.69), channel_id=1, source_target_pairs={{0,8},{4,20},{8,0},{12,28},{16,24},{20,4},{24,16},{28,12},{1,9},{5... | collective-permute-start | bytes 786440 | tf_op jit(solution)/shard_map/b2/ppermute | solution.py:337
  41.6 3.7 %collective-permute-done.9.refs_3_ = f32[520,256]{1,0:T(8,128)S(1)} collective-permute-done((f32[520,256]{1,0:T(8,128)S(1)}, f32[520,256]{1,0:T(8,128)S(1)}, u32[]{:S(2)}, u32[]{:S(2)}) %collective-permute-start.9) | collective-permute-done | bytes 532512 | tf_op jit(solution)/shard_map/d1/ppermute | solution.py:337
  45.7 2.0 %collective-permute-start.13 = (f32[256,256]{1,0:T(8,128)S(1)}, f32[256,256]{1,0:T(8,128)S(1)}, u32[]{:S(2)}, u32[]{:S(2)}) collective-permute-start(f32[256,256]{1,0:T(8,128)S(1)} %get-tuple-element.68.refs_1_), channel_id=1, source_target_pairs={{0,8},{4,20},{8,0},{12,28},{16,24},{20,4},{24,16},{28,12},{1,9},{5... | collective-permute-start | bytes 786440 | tf_op jit(solution)/shard_map/d2/ppermute | solution.py:337
  48.2 1.7 %collective-permute-start.19 = (f32[256,256]{1,0:T(8,128)S(1)}, f32[256,256]{1,0:T(8,128)S(1)}, u32[]{:S(2)}, u32[]{:S(2)}) collective-permute-start(f32[256,256]{1,0:T(8,128)S(1)} %shard_map.101), channel_id=1, source_target_pairs={{0,1},{1,2},{2,3},{3,0},{4,5},{5,6},{6,7},{7,4},{8,9},{9,10},{10,1... | collective-permute-start | bytes 786440 | tf_op jit(solution)/shard_map/l3/ppermute | solution.py:380
  49.8 1.5 %collective-permute-start.16 = (f32[256,256]{1,0:T(8,128)S(1)}, f32[256,256]{1,0:T(8,128)S(1)}, u32[]{:S(2)}, u32[]{:S(2)}) collective-permute-start(f32[256,256]{1,0:T(8,128)S(1)} %get-tuple-element.80.refs_1_), channel_id=1, source_target_pairs={{0,8},{4,20},{8,0},{12,28},{16,24},{20,4},{24,16},{28,12},{1,9},{5... | collective-permute-start | bytes 786440 | tf_op jit(solution)/shard_map/d3/ppermute | solution.py:337
  52.0 2.8 %collective-permute-done.13.refs_1_ = f32[256,256]{1,0:T(8,128)S(1)} collective-permute-done((f32[256,256]{1,0:T(8,128)S(1)}, f32[256,256]{1,0:T(8,128)S(1)}, u32[]{:S(2)}, u32[]{:S(2)}) %collective-permute-start.13) | collective-permute-done | bytes 262176 | tf_op jit(solution)/shard_map/d2/ppermute | solution.py:337
  55.7 2.6 %shard_map.92 = (bf16[2,1024,256]{2,1,0:T(8,128)(2,1)S(1)}, bf16[2,1024,256]{2,1,0:T(8,128)(2,1)S(1)}, bf16[2,1024,256]{2,1,0:T(8,128)(2,1)S(1)}, bf16[2,1024,25...) custom-call(f32[2048,256]{1,0:T(8,128)S(1)} %shard_map.91.mine, ...), custom_call_target="tpu_custom_call" | custom-call | flops 1610612736 | tf_op jit(solution)/shard_map/pallas_call | solution.py:288
  58.5 2.7 %shard_map.96 = (bf16[2,1024,256]{2,1,0:T(8,128)(2,1)S(1)}, bf16[2,1024,256]{2,1,0:T(8,128)(2,1)S(1)}, f32[1024,256]{1,0:T(8,128)S(1)}, f32[1024,256]{1,0:T(8,128)S(1)}, f32[1024,256]{1,0:T(8,128)S(1)}) custom-call(f32[1024,256]{1,0:T(8,128)S(1)} %shard_map.95.mine, ...), custom_call_target="tpu_custom_call", output_to_operand_aliasing={{2}: (6, {}), {3}: (7, {})} | custom-call | flops 2013265920 | tf_op jit(solution)/shard_map/pallas_call | solution.py:288
  61.8 10.2 %shard_map.104 = (f32[1024,128]{1,0:T(8,128)S(1)}, bf16[2,1024,256]{2,1,0:T(8,128)(2,1)S(1)}, bf16[2,1024,256]{2,1,0:T(8,128)(2,1)S(1)}) custom-call(f32[1024,256]{1,0:T(8,128)S(1)} %shard_map.98.refs_0_, f32[1024,256]{1,0:T(8,128)S(1)} %collective-permute-done.17.refs_2_.refs_1_, bf16[2,1024,256]{2,1,0:T(8,128)(2,1)S(1)} %get-tuple-element.66.refs_0_.refs_2_, ...), custom_call_target="tpu_custom_call" | custom-call | flops 48318382080 | tf_op jit(solution)/shard_map/pallas_call | solution.py:288
  72.6 1.8 %shard_map.105 = (bf16[256,1024]{1,0:T(8,128)(2,1)S(1)}, bf16[256,1024]{1,0:T(8,128)(2,1)S(1)}) custom-call(bf16[2,1024,256]{2,1,0:T(8,128)(2,1)S(1)} %get-tuple-element.66.refs_0_.refs_2_, bf16[2,1024,256]{2,1,0:T(8,128)(2,1)S(1)} %get-tuple-element.67.refs_1_.refs_2_.refs_3_, bf16[2,1024,256]{2,1,0:T(8,128)(2,1)S(1)} %get-tuple-element.78.refs_1_.refs_4_.refs_2_, ...), custom_call_target="tpu_custom_call" | custom-call | flops 1610612736 | tf_op jit(solution)/shard_map/pallas_call | solution.py:288
  74.5 0.9 %shard_map.106.own = f32[256,256]{1,0:T(8,128)S(1)} custom-call(bf16[256,1024]{1,0:T(8,128)(2,1)S(1)} %get-tuple-element.93.left_high, bf16[256,1024]{1,0:T(8,128)(2,1)S(1)} %get-tuple-element.94.left_low, f32[1,256,256]{2,1,0:T(8,128)S(1)} %copy-done.2, f32[1024,128]{1,0:T(8,128)S(1)} %get-tuple-element.95.refs_0_, ...), custom_call_target="tpu_custom_call" | custom-call | flops 402653184 | tf_op jit(solution)/shard_map/pallas_call | solution.py:288
  75.4 1.1 %collective-permute-start.21 = (f32[256,256]{1,0:T(8,128)S(1)}, f32[256,256]{1,0:T(8,128)S(1)}, u32[]{:S(2)}, u32[]{:S(2)}) collective-permute-start(f32[256,256]{1,0:T(8,128)S(1)} %shard_map.106.own), channel_id=1, source_target_pairs={{0,16},{4,20},{8,24},{12,28},{16,0},{20,4},{24,8},{28,12},{1,17},{... | collective-permute-start | bytes 786440 | tf_op jit(solution)/shard_map/ppermute | solution.py:337
  76.4 7.3 %collective-permute-done.21.across = f32[256,256]{1,0:T(8,128)S(1)} collective-permute-done((f32[256,256]{1,0:T(8,128)S(1)}, f32[256,256]{1,0:T(8,128)S(1)}, u32[]{:S(2)}, u32[]{:S(2)}) %collective-permute-start.21) | collective-permute-done | bytes 262176 | tf_op jit(solution)/shard_map/ppermute | solution.py:337
  (62 shorter events, 9.3 us)
Async XLA Ops:
  3.2 9.6 %collective-permute-start = (f32[256,256]{1,0:T(8,128)S(1)}, f32[256,256]{1,0:T(8,128)S(1)}, u32[]{:S(2)}, u32[]{:S(2)}) collective-permute-start(f32[256,256]{1,0:T(8,128)S(1)} %get-tuple-element.52), channel_id=1, source_target_pairs={{0,16},{4,12},{8,24},{12,4},{16,0},{20,28},{24,8},{28,20},{1,17},{... | collective-permute-start | bytes 786440 | tf_op jit(solution)/shard_map/a0/ppermute | solution.py:337
  6.2 12.0 %collective-permute-start.2 = (f32[256,256]{1,0:T(8,128)S(1)}, f32[256,256]{1,0:T(8,128)S(1)}, u32[]{:S(2)}, u32[]{:S(2)}) collective-permute-start(f32[256,256]{1,0:T(8,128)S(1)} %get-tuple-element.52), channel_id=1, source_target_pairs={{0,8},{4,20},{8,0},{12,28},{16,24},{20,4},{24,16},{28,12},{1,9},{5... | collective-permute-start | bytes 786440 | tf_op jit(solution)/shard_map/b0/ppermute | solution.py:337
  7.7 10.5 %collective-permute-start.1 = (f32[256,256]{1,0:T(8,128)S(1)}, f32[256,256]{1,0:T(8,128)S(1)}, u32[]{:S(2)}, u32[]{:S(2)}) collective-permute-start(f32[256,256]{1,0:T(8,128)S(1)} %shard_map.79.refs_1_), channel_id=1, source_target_pairs={{0,1},{1,2},{2,3},{3,0},{4,5},{5,6},{6,7},{7,4},{8,9},{9,10},{10,1... | collective-permute-start | bytes 786440 | tf_op jit(solution)/shard_map/p1/ppermute | solution.py:380
  12.9 32.5 %copy-start = (f32[512,256]{1,0:T(8,128)}, f32[512,256]{1,0:T(8,128)S(1)}, u32[]{:S(2)}) copy-start(f32[512,256]{1,0:T(8,128)S(1)} %get-tuple-element.53.refs_1_.refs_0_.refs_8_) | copy-start | bytes 1572868
  12.9 8.0 %collective-permute-start.3 = (f32[256,256]{1,0:T(8,128)S(1)}, f32[256,256]{1,0:T(8,128)S(1)}, u32[]{:S(2)}, u32[]{:S(2)}) collective-permute-start(f32[256,256]{1,0:T(8,128)S(1)} %get-tuple-element.56.refs_2_), channel_id=1, source_target_pairs={{0,8},{4,20},{8,0},{12,28},{16,24},{20,4},{24,16},{28,12},{1,9},{5... | collective-permute-start | bytes 786440 | tf_op jit(solution)/shard_map/d0/ppermute | solution.py:337
  14.5 17.0 %collective-permute-start.5 = (f32[512,256]{1,0:T(8,128)S(1)}, f32[512,256]{1,0:T(8,128)S(1)}, u32[]{:S(2)}, u32[]{:S(2)}) collective-permute-start(f32[512,256]{1,0:T(8,128)S(1)} %get-tuple-element.53.refs_1_.refs_0_.refs_8_), channel_id=1, source_target_pairs={{0,3},{1,0},{2,1},{3,2},{4,7},{5,4},{6,5},{7,6},{8,11},{9,8},{10,9... | collective-permute-start | bytes 1572872 | tf_op jit(solution)/shard_map/q2/ppermute | solution.py:380
  19.2 20.3 %collective-permute-start.7 = (f32[512,256]{1,0:T(8,128)S(1)}, f32[512,256]{1,0:T(8,128)S(1)}, u32[]{:S(2)}, u32[]{:S(2)}) collective-permute-start(f32[512,256]{1,0:T(8,128)S(1)} %shard_map.87), channel_id=1, source_target_pairs={{0,1},{1,2},{2,3},{3,0},{4,5},{5,6},{6,7},{7,4},{8,9},{9,10},{10,1... | collective-permute-start | bytes 1572872 | tf_op jit(solution)/shard_map/q3/ppermute | solution.py:380
  19.3 13.0 %collective-permute-start.4 = (f32[520,256]{1,0:T(8,128)S(1)}, f32[520,256]{1,0:T(8,128)S(1)}, u32[]{:S(2)}, u32[]{:S(2)}) collective-permute-start(f32[520,256]{1,0:T(8,128)S(1)} %shard_map.83.refs_1_), channel_id=1, source_target_pairs={{0,16},{4,12},{8,24},{12,4},{16,0},{20,28},{24,8},{28,20},{1,17},{... | collective-permute-start | bytes 1597448 | tf_op jit(solution)/shard_map/a1/ppermute | solution.py:337
  20.9 18.7 %collective-permute-start.6 = (f32[520,256]{1,0:T(8,128)S(1)}, f32[520,256]{1,0:T(8,128)S(1)}, u32[]{:S(2)}, u32[]{:S(2)}) collective-permute-start(f32[520,256]{1,0:T(8,128)S(1)} %get-tuple-element.60.refs_0_), channel_id=1, source_target_pairs={{0,8},{4,20},{8,0},{12,28},{16,24},{20,4},{24,16},{28,12},{1,9},{5... | collective-permute-start | bytes 1597448 | tf_op jit(solution)/shard_map/b1/ppermute | solution.py:337
  32.4 9.2 %collective-permute-start.8 = (f32[256,256]{1,0:T(8,128)S(1)}, f32[256,256]{1,0:T(8,128)S(1)}, u32[]{:S(2)}, u32[]{:S(2)}) collective-permute-start(f32[256,256]{1,0:T(8,128)S(1)} %shard_map.86.refs_1_), channel_id=1, source_target_pairs={{0,16},{4,12},{8,24},{12,4},{16,0},{20,28},{24,8},{28,20},{1,17},{... | collective-permute-start | bytes 786440 | tf_op jit(solution)/shard_map/a2/ppermute | solution.py:337
  33.2 12.1 %collective-permute-start.9 = (f32[520,256]{1,0:T(8,128)S(1)}, f32[520,256]{1,0:T(8,128)S(1)}, u32[]{:S(2)}, u32[]{:S(2)}) collective-permute-start(f32[520,256]{1,0:T(8,128)S(1)} %get-tuple-element.59.refs_3_.refs_1_), channel_id=1, source_target_pairs={{0,8},{4,20},{8,0},{12,28},{16,24},{20,4},{24,16},{28,12},{1,9},{5... | collective-permute-start | bytes 1597448 | tf_op jit(solution)/shard_map/d1/ppermute | solution.py:337
  39.7 8.0 %collective-permute-start.12 = (f32[256,256]{1,0:T(8,128)S(1)}, f32[256,256]{1,0:T(8,128)S(1)}, u32[]{:S(2)}, u32[]{:S(2)}) collective-permute-start(f32[256,256]{1,0:T(8,128)S(1)} %shard_map.89.refs_2_), channel_id=1, source_target_pairs={{0,16},{4,12},{8,24},{12,4},{16,0},{20,28},{24,8},{28,20},{1,17},{... | collective-permute-start | bytes 786440 | tf_op jit(solution)/shard_map/a3/ppermute | solution.py:337
  40.2 7.8 %collective-permute-start.11 = (f32[256,256]{1,0:T(8,128)S(1)}, f32[256,256]{1,0:T(8,128)S(1)}, u32[]{:S(2)}, u32[]{:S(2)}) collective-permute-start(f32[256,256]{1,0:T(8,128)S(1)} %get-tuple-element.69), channel_id=1, source_target_pairs={{0,8},{4,20},{8,0},{12,28},{16,24},{20,4},{24,16},{28,12},{1,9},{5... | collective-permute-start | bytes 786440 | tf_op jit(solution)/shard_map/b2/ppermute | solution.py:337
  45.5 9.3 %collective-permute-start.10 = (f32[2048,256]{1,0:T(8,128)S(1)}, f32[2048,256]{1,0:T(8,128)S(1)}, u32[]{:S(2)}, u32[]{:S(2)}) collective-permute-start(f32[2048,256]{1,0:T(8,128)S(1)} %shard_map.91.mine), channel_id=1, source_target_pairs={{0,4},{4,0},{8,12},{12,8},{1,5},{5,1},{9,13},{13,9},{2,6},{6,2},{1... | collective-permute-start | bytes 6291464 | tf_op jit(solution)/shard_map/t01/ppermute | solution.py:343
  45.6 6.4 %collective-permute-start.14 = (f32[256,256]{1,0:T(8,128)S(1)}, f32[256,256]{1,0:T(8,128)S(1)}, u32[]{:S(2)}, u32[]{:S(2)}) collective-permute-start(f32[256,256]{1,0:T(8,128)S(1)} %get-tuple-element.72), channel_id=1, source_target_pairs={{0,8},{4,20},{8,0},{12,28},{16,24},{20,4},{24,16},{28,12},{1,9},{5... | collective-permute-start | bytes 786440 | tf_op jit(solution)/shard_map/b3/ppermute | solution.py:337
  45.7 9.2 %collective-permute-start.13 = (f32[256,256]{1,0:T(8,128)S(1)}, f32[256,256]{1,0:T(8,128)S(1)}, u32[]{:S(2)}, u32[]{:S(2)}) collective-permute-start(f32[256,256]{1,0:T(8,128)S(1)} %get-tuple-element.68.refs_1_), channel_id=1, source_target_pairs={{0,8},{4,20},{8,0},{12,28},{16,24},{20,4},{24,16},{28,12},{1,9},{5... | collective-permute-start | bytes 786440 | tf_op jit(solution)/shard_map/d2/ppermute | solution.py:337
  48.2 13.6 %collective-permute-start.19 = (f32[256,256]{1,0:T(8,128)S(1)}, f32[256,256]{1,0:T(8,128)S(1)}, u32[]{:S(2)}, u32[]{:S(2)}) collective-permute-start(f32[256,256]{1,0:T(8,128)S(1)} %shard_map.101), channel_id=1, source_target_pairs={{0,1},{1,2},{2,3},{3,0},{4,5},{5,6},{6,7},{7,4},{8,9},{9,10},{10,1... | collective-permute-start | bytes 786440 | tf_op jit(solution)/shard_map/l3/ppermute | solution.py:380
  49.8 8.4 %collective-permute-start.16 = (f32[256,256]{1,0:T(8,128)S(1)}, f32[256,256]{1,0:T(8,128)S(1)}, u32[]{:S(2)}, u32[]{:S(2)}) collective-permute-start(f32[256,256]{1,0:T(8,128)S(1)} %get-tuple-element.80.refs_1_), channel_id=1, source_target_pairs={{0,8},{4,20},{8,0},{12,28},{16,24},{20,4},{24,16},{28,12},{1,9},{5... | collective-permute-start | bytes 786440 | tf_op jit(solution)/shard_map/d3/ppermute | solution.py:337
  55.0 3.5 %collective-permute-start.15 = (f32[1024,256]{1,0:T(8,128)S(1)}, f32[1024,256]{1,0:T(8,128)S(1)}, u32[]{:S(2)}, u32[]{:S(2)}) collective-permute-start(f32[1024,256]{1,0:T(8,128)S(1)} %shard_map.95.mine), channel_id=1, source_target_pairs={{0,4},{4,0},{8,12},{12,8},{1,5},{5,1},{9,13},{13,9},{2,6},{6,2},{1... | collective-permute-start | bytes 3145736 | tf_op jit(solution)/shard_map/t2/ppermute | solution.py:343
  55.1 6.1 %collective-permute-start.18 = (f32[1056,256]{1,0:T(8,128)S(1)}, f32[1056,256]{1,0:T(8,128)S(1)}, u32[]{:S(2)}, u32[]{:S(2)}) collective-permute-start(f32[1056,256]{1,0:T(8,128)S(1)} %shard_map.99.refs_0_), channel_id=1, source_target_pairs={{0,4},{4,0},{8,12},{12,8},{1,5},{5,1},{9,13},{13,9},{2,6},{6,2},{1... | collective-permute-start | bytes 3244040 | tf_op jit(solution)/shard_map/tx/ppermute | solution.py:343
  58.4 3.4 %collective-permute-start.17 = (f32[1024,256]{1,0:T(8,128)S(1)}, f32[1024,256]{1,0:T(8,128)S(1)}, u32[]{:S(2)}, u32[]{:S(2)}) collective-permute-start(f32[1024,256]{1,0:T(8,128)S(1)} %shard_map.98.refs_0_), channel_id=1, source_target_pairs={{0,4},{4,0},{8,12},{12,8},{1,5},{5,1},{9,13},{13,9},{2,6},{6,2},{1... | collective-permute-start | bytes 3145736 | tf_op jit(solution)/shard_map/t3/ppermute | solution.py:343
  61.8 10.8 %copy-start.1 = (f32[512,256]{1,0:T(8,128)S(1)}, f32[512,256]{1,0:T(8,128)}, u32[]{:S(2)}) copy-start(f32[512,256]{1,0:T(8,128)} %copy-done) | copy-start | bytes 1572868
  72.1 2.4 %collective-permute-start.20 = (f32[1024,128]{1,0:T(8,128)S(1)}, f32[1024,128]{1,0:T(8,128)S(1)}, u32[]{:S(2)}, u32[]{:S(2)}) collective-permute-start(f32[1024,128]{1,0:T(8,128)S(1)} %get-tuple-element.95.refs_0_), channel_id=1, source_target_pairs={{0,4},{4,0},{8,12},{12,8},{1,5},{5,1},{9,13},{13,9},{2,6},{6,2},{1... | collective-permute-start | bytes 1572872 | tf_op jit(solution)/shard_map/ppermute | solution.py:343
  75.4 8.3 %collective-permute-start.21 = (f32[256,256]{1,0:T(8,128)S(1)}, f32[256,256]{1,0:T(8,128)S(1)}, u32[]{:S(2)}, u32[]{:S(2)}) collective-permute-start(f32[256,256]{1,0:T(8,128)S(1)} %shard_map.106.own), channel_id=1, source_target_pairs={{0,16},{4,20},{8,24},{12,28},{16,0},{20,4},{24,8},{28,12},{1,17},{... | collective-permute-start | bytes 786440 | tf_op jit(solution)/shard_map/ppermute | solution.py:337
  (3 other events, 5.5 us)

commit v4 on v3

--- a/solution.py
+++ b/solution.py
@@ -13,29 +13,35 @@
 GATE = 2 * 10**10
 
 SLOTS = {
-    "p1": (0, 3),
-    "a0": (1, 2),
+    "p1": (1, 3),
+    "a0": (0, 2),
     "b0": (1, 3),
+    "xx": (1, 3),
+    "p2": (2, 4),
     "d0": (2, 4),
-    "q2": (2, 5),
-    "q3": (3, 6),
     "a1": (3, 5),
-    "b1": (4, 6),
+    "b1": (4, 7),
+    "p3": (3, 5),
+    "a2": (4, 6),
+    "xy": (3, 5),
     "d1": (5, 7),
-    "a2": (5, 7),
+    "a3": (5, 7),
+    "d2": (6, 8),
     "b2": (6, 8),
-    "a3": (6, 8),
-    "d2": (7, 9),
     "b3": (7, 9),
+    "d3": (7, 10),
     "t01": (7, 9),
-    "d3": (8, 10),
-    "l3": (8, 11),
-    "t2": (9, 11),
-    "tx": (9, 11),
-    "t3": (10, 12),
+    "tx": (8, 10),
+    "t2": (8, 10),
+    "td": (10, 11),
+    "l1": (9, 11),
+    "t3": (9, 11),
+    "l2": (10, 12),
+    "l3": (11, 12),
 }
-KERNELS = {'01': 10, '2': 12}
-ANCHOR = 12
+KERNELS = {'01': 9, '2': 10}
+DIAGONAL = {'d1': 'p', 'd2': 'z', 'd3': 'p'}
+ANCHOR = 11
 
 
 class Grid:
@@ -98,69 +104,34 @@
     return pl.ds(pl.multiple_of(index * size, size), size)
 
 
-def fetch(grid, first, second, out, sem):
-    @pl.when(grid.upper())
-    def _():
-        pltpu.make_async_copy(first.at[0], out, sem).start()
-
-    @pl.when(jnp.logical_not(grid.upper()))
-    def _():
-        pltpu.make_async_copy(second.at[0], out, sem).start()
-
-    return pltpu.make_async_copy(first.at[0], out, sem)
-
-
-def choose_kernel(grid, first, second, *refs):
-    out, sem = refs[-2:]
-    fetch(grid, first, second, out, sem).wait()
-
-
-def number_kernel(ids, out, number, sem):
+def extend_kernel(ids, block, late, out, number, sem):
+    del late
+    rows = block.shape[1]
     copy = pltpu.make_async_copy(ids, number, sem)
     copy.start()
+    out[:rows, :] = block[0]
     copy.wait()
-    out[...] = jnp.full(out.shape, number[0].astype(jnp.float32))
-
-
-def extend_kernel(piece, block, number, out):
-    rows = piece.shape[0]
-    out[:rows, :] = piece[...]
-    out[rows : 2 * rows, :] = block[0]
-    out[2 * rows :, :] = number[...]
-
-
-def panel_kernel(grid, start, gains, *refs):
+    out[rows:, :] = jnp.full((TILE, out.shape[1]), number[0].astype(jnp.float32))
+
+
+def scale_kernel(grid, own, across, gains, panel, weight):
     rows, cols = grid.shape
-    panel, weight = refs[-2:]
-    height = start + rows + TILE
-    pieces = [ref.at[pl.ds(i, height), :] for ref in refs[:-2] for i in range(0, ref.shape[0], height)]
-    for piece, (side, row) in zip(pieces, grid.origins()):
-        @pl.when(side == 0)
-        def _(piece=piece, row=row):
-            panel[span(row, rows), :] = piece[start : start + rows, :]
-
-    def gain(piece, i):
-        number = piece[start + rows : start + rows + 1, :]
+
+    def gain(block, i):
+        number = block[rows : rows + 1, :]
         here = pl.ds(i * cols, cols)
         return sum(jnp.where(number == m, gains[m : m + 1, here], 0.0) for m in range(gains.shape[0]))
 
     for i in range(gains.shape[1] // cols):
-        weight[i : i + 1, :] = gain(pieces[0], i) * gain(pieces[len(grid.hops) - 1], i)
-    for row in range(grid.row_count):
-        here = weight[row * rows // cols : row * rows // cols + 1, :]
-        column = jnp.concatenate([here] * 8, axis=0).T[:, :1]
-        panel[row * rows : (row + 1) * rows, :] = panel[row * rows : (row + 1) * rows, :] * column
+        weight[i : i + 1, :] = gain(own, i) * gain(across, i)
+    here = weight[pl.ds(lax.div(grid.row() * rows, cols), 1), :]
+    column = jnp.concatenate([here] * 8, axis=0).T[:, :1]
+    panel[...] = jnp.where(grid.upper(), own[:rows, :], across[:rows, :]) * column
 
 
 def gate_kernel(count, *refs):
     for value, out in zip(refs[:count], refs[-count:]):
         out[...] = value[...]
-
-
-def unpack_kernel(whole, *outs):
-    rows = outs[0].shape[0]
-    for i, out in enumerate(outs):
-        out[...] = whole[i * rows : (i + 1) * rows, :]
 
 
 def pack_kernel(parts, *refs):
@@ -200,11 +171,11 @@
     rows, cols = grid.shape
     blocks = grid.blocks
     old = blocks - 1
-    mine, theirs, refs = refs[0], refs[1], refs[2:]
+    last, refs = refs[:4], refs[4:]
     highs, lows, sums, refs = refs[:old], refs[old : 2 * old], refs[2 * old : 3 * old], refs[3 * old :]
-    panel, _, out, high, low, power_high, power_low, pair = refs
+    mine_x, theirs_x, _, out, high, low, power_high, power_low, pair, base = refs
     width = out.shape[1]
-    ingest(grid, [mine, theirs], 1, rows, [high], [low])
+    ingest(grid, last, 1, rows, [high], [low])
     highs, lows = (*highs, high), (*lows, low)
     places = [grid.place(j) for j in range(blocks)]
     for n in range(blocks):
@@ -224,13 +195,17 @@
             here = pl.ds(j * cols, cols)
             pair[here, :width], pair[here, width:] = z_high, z_low
 
-    take(lambda here: panel[here, ours])
+    pieces = [ref.at[pl.ds(i, rows), :] for ref in (mine_x, theirs_x) for i in range(0, ref.shape[0], rows)]
+    starts = [grid.row_of(hop, other) for other in range(grid.cores) for hop in range(grid.chips)]
+    for piece, start in zip(pieces, starts):
+        base[span(start, rows), :] = piece[:, ours]
+    take(lambda here: base[here, :])
 
     @pl.loop(0, NTERMS - 1)
     def _(_):
         both = dot(power_high[...], pair[...])
         rest = dot(power_low[...], pair[:, :width])
-        out[...] = panel[:, ours] + (both[:, :width] + (both[:, width:] + rest))
+        out[...] = base[...] + (both[:, :width] + (both[:, width:] + rest))
         take(lambda here: out[here, :])
 
 
@@ -316,11 +291,6 @@
     return call(functools.partial(pack_kernel, parts), single(*shape), [*arrays, *needs], loose=loose)
 
 
-def unpack(whole, count):
-    rows, cols = whole.shape
-    return call(unpack_kernel, [single(rows // count, cols)] * count, [whole])
-
-
 def on_device(reflect_fwd, transmit_fwd, reflect_bwd, transmit_bwd, material_ids, interface_gain):
     rows, cols = reflect_fwd.shape[1:]
     grid = Grid((rows, cols), *(lax.axis_size(a) for a in ("layer", "row", "col")))
@@ -347,16 +317,6 @@
         source = found[max(k - 2, 0)] if top is None else top
         shift = 1 if k % 2 else -1
         found.append(lax.ppermute(source, "col", [(i, (i + shift) % blocks) for i in range(blocks)]))
-
-    def choose(first, second, *late):
-        return call(
-            functools.partial(choose_kernel, grid),
-            single(rows, cols),
-            [first, second, *late],
-            far=(0, 1),
-            loose=range(2, 2 + len(late)),
-            scratch=[pltpu.SemaphoreType.DMA],
-        )
 
     highs, lows, sums = [], [], []
     half = jax.ShapeDtypeStruct((2, order, cols), jnp.bfloat16)
@@ -388,46 +348,56 @@
     upper_own = jnp.concatenate([reflect_bwd[0], transmit_bwd[0]], axis=0)
     lower_own = jnp.concatenate([reflect_fwd[0], transmit_fwd[0]], axis=0)
     values = {"q0": jnp.where(grid.upper(), upper_own, lower_own)}
-    values["token"] = call(
-        number_kernel,
-        single(TILE, cols),
-        [material_ids],
-        far=(0,),
-        scratch=[pltpu.SMEM(material_ids.shape, jnp.int32), pltpu.SemaphoreType.DMA],
-    )
-    end = 2 * rows + TILE
+    values["token"] = pack([(values["q0"], 0, TILE)])
     up, down = functools.partial(along, shift=1), functools.partial(along, shift=-1)
+    flip, over = (functools.partial(plane, hop=both_cores(hop)) for hop in ((1, 0), (0, 1)))
     moves = {
         "p1": (up, "p0"),
-        "q2": (down, "q0"),
-        "q3": (up, "r1"),
+        "p2": (down, "p0"),
+        "p3": (up, "p1"),
+        "l1": (up, "l0"),
+        "l2": (down, "l0"),
         "l3": (up, "l1"),
-        **{f"a{i}": (a_hop, "e1" if i == 1 else f"p{i}") for i in range(4)},
-        **{f"b{i}": (b_hop, "e1" if i == 1 else f"p{i}") for i in range(4)},
-        **{f"d{i}": (b_hop, f"a{i}") for i in range(4)},
+        **{f"a{i}": (a_hop, f"p{i}") for i in range(4)},
+        **{f"b{i}": (b_hop, f"p{i}") for i in range(4)},
+        "d0": (b_hop, "a0"),
+        "d1": (up, "d0") if DIAGONAL["d1"] == "z" else (b_hop, "a1"),
+        "d2": (down, "d0") if DIAGONAL["d2"] == "z" else (b_hop, "a2"),
+        "d3": (up, "d1") if DIAGONAL["d3"] == "z" else (b_hop, "a3"),
         **{f"t{m}": (sibling, f"m{m}") for m in ("01", "2", "3", "x")},
+        "td": (sibling, "d3"),
+        "xx": (flip, "x0"),
+        "xy": (over, "x1"),
     }
 
-    def head(name):
-        return (values[name], 0, rows)
-
-    def tail(name, stop):
-        return (values[name], rows, stop)
-
     def packed(*names):
-        return names, lambda: pack([head(n) for n in names])
+        return names, lambda: pack([values[n] for n in names])
+
+    def extend():
+        return call(
+            extend_kernel,
+            single(rows + TILE, cols),
+            [material_ids, transmit_fwd, values["token"]],
+            far=(0,),
+            loose=(2,),
+            scratch=[pltpu.SMEM(material_ids.shape, jnp.int32), pltpu.SemaphoreType.DMA],
+        )
+
+    def scale():
+        outs = [single(rows, cols), single(-(-order // cols // TILE) * TILE, cols)]
+        operands = [values["x0"], values["xx"], interface_gain]
+        panel, values["weight"] = call(functools.partial(scale_kernel, grid), outs, operands)
+        return panel
 
     made = {
-        "e1": (("p1",), lambda: call(extend_kernel, single(end, cols), [values["p1"], transmit_fwd, values["token"]])),
-        "r1": (("p1",), lambda: pack([values["p1"], tail("q0", 2 * rows)])),
-        "l1": (("q3",), lambda: pack([tail("q3", 2 * rows)])),
-        "p0": packed("q0"),
-        "p2": packed("q2"),
-        "p3": packed("q3"),
-        "m01": packed("q0", "p1", "a0", "a1", "b0", "b1", "d0", "d1"),
-        "m2": packed("q2", "a2", "b2", "d2"),
-        "m3": packed("q3", "a3", "b3", "d3"),
-        "mx": (("a1", "b1", "d1"), lambda: pack([tail(n, end) for n in ("e1", "a1", "b1", "d1")])),
+        "p0": ((), lambda: pack([(values["q0"], 0, rows)])),
+        "l0": ((), lambda: pack([(values["q0"], rows, 2 * rows)])),
+        "x0": ((), extend),
+        "x1": (("xx",), scale),
+        "m01": packed("p0", "p1", "a0", "a1", "b0", "b1", "d0", "d1"),
+        "m2": packed("p2", "a2", "b2", "d2"),
+        "m3": packed("p3", "a3", "b3"),
+        "mx": packed("x1", "xy"),
     }
     kernels = {"01": (2, 2 * rows), "2": (1, rows)}
 
@@ -466,19 +436,14 @@
     for name in ("01", "2"):
         if name not in KERNELS:
             absorb_named(name)
-    panel, weight = call(
-        functools.partial(panel_kernel, grid, 0),
-        [single(order, cols), single(-(-order // cols // TILE) * TILE, cols)],
-        [interface_gain, values["mx"], values["tx"]],
-    )
     width = cols // cores
-    operands = [values["m3"], values["t3"], *highs, *lows, *sums, panel]
+    operands = [values[n] for n in ("m3", "d3", "t3", "td")] + [*highs, *lows, *sums, values["mx"], values["tx"]]
     part, high, low = call(
         functools.partial(horner_kernel, grid),
         [single(order, width), half, half],
         [*operands, values["token"]],
         loose=(len(operands),),
-        scratch=[pltpu.VMEM((order, order), jnp.bfloat16)] * 2 + [pltpu.VMEM((order, 2 * width), jnp.bfloat16)],
+        scratch=[pltpu.VMEM((order, order), jnp.bfloat16)] * 2 + [pltpu.VMEM((order, 2 * width), jnp.bfloat16), pltpu.VMEM((order, width), jnp.float32)],
         flops=10 * 6 * NTERMS * order * order * width,
         limit=10 * MIB,
     )
@@ -486,8 +451,8 @@
     parts = [part] + ([sibling(part)] if cores == 2 else [])
     for gate_number in range(ANCHOR + 1, 1 + max(t[1] for t in SLOTS.values())):
         pass_gate(gate_number, part)
-    left = [values[n] for n in ("q0", "q3", "q2", "l3")]
-    operands = highs + lows + left + [weight]
+    left = [values[n] for n in ("l0", "l1", "l2", "l3")]
+    operands = highs + lows + left + [values["weight"]]
     left = call(
         functools.partial(left_kernel, grid),
         [jax.ShapeDtypeStruct((rows, order), jnp.bfloat16)] * 2,

time: 84.9 us -> 80 us (0.942)
  waiting for transfers between devices: 34.1 us -> 22.4 us
  starting transfers between devices: 25.6 us -> 34.1 us
  local copies, waits for them, and re-layouts: 0.89 us -> 0.01 us
    ppermute x4 -> x7, waiting for transfers between devices: 14.9 us -> 3.23 us  [along(): lax.ppermute(value, 'col', [(i, (i + shift) % blocks) for i in range(bloc...]
    ppermute x4 -> x7, starting transfers between devices: 7.04 us -> 13.6 us  [along(): lax.ppermute(value, 'col', [(i, (i + shift) % blocks) for i in range(bloc...]
    ppermute x13 -> x14, starting transfers between devices: 17.1 us -> 18.5 us  [plane(): return lax.ppermute(value, ('layer', 'row'), route)]
    unnamed x10 -> x6, local copies, waits for them, and re-layouts: 0.89 us -> 0.01 us
    pallas_call x31 -> x28, Pallas kernels: 21.1 us -> 20.5 us  [call(): pl.pallas_call(kernel, out_shape=outs, in_specs=specs, out_specs=jax.tree...]
    ppermute x5 -> x6, starting transfers between devices: 1.37 us -> 1.93 us  [sibling(): lax.ppermute(value, 'row', [(i, i ^ 1) for i in range(grid.row_count)])]
    ppermute x13 -> x14, waiting for transfers between devices: 19.2 us -> 19.2 us  [plane(): return lax.ppermute(value, ('layer', 'row'), route)]
  transfers between devices with their start and end apart: 22 -> 27, of which waited for: 9 -> 8; matrix products, arithmetic and copies ran while one was open for 0% -> 0% of each run, Pallas kernels for 10% -> 24%
where the time goes in v4:
time: 80 us; the launch traced here: 79.9 us
  starting transfers between devices  34.1 us (43%)
  waiting for transfers between devices  22.4 us (28%)
  Pallas kernels  20.5 us (26%)
  between operations  1.54 us (2%)
  other arithmetic  1.26 us (2%)
    pallas_call x28, Pallas kernels, call(): pl.pallas_call(kernel, out_shape=outs, in_specs=specs, out_specs=jax.tree...  20.5 us
    ppermute x14, waiting for transfers between devices, plane(): return lax.ppermute(value, ('layer', 'row'), route)  19.2 us
    ppermute x14, starting transfers between devices, plane(): return lax.ppermute(value, ('layer', 'row'), route)  18.5 us
    ppermute x7, starting transfers between devices, along(): lax.ppermute(value, 'col', [(i, (i + shift) % blocks) for i in range(bloc...  13.6 us
    ppermute x7, waiting for transfers between devices, along(): lax.ppermute(value, 'col', [(i, (i + shift) % blocks) for i in range(bloc...  3.23 us
    ppermute x6, starting transfers between devices, sibling(): lax.ppermute(value, 'row', [(i, i ^ 1) for i in range(grid.row_count)])  1.93 us
  transfers between devices with their start and end apart: 27, of which 8 were waited for; matrix products, arithmetic and copies ran while one was open for 0% of the time, Pallas kernels for 24%

profile of v4, /device:TPU:0, one launch (start us, length us, event | category | flops | bytes accessed | tf_op | source)
XLA Modules:
  0.0 79.9 jit_solution(15476782946366987986)
XLA Ops:
  0.6 1.3 %maximum_select_fusion.refs_0_ = f32[512,256]{1,0:T(8,128)S(1)} fusion(f32[256,256]{1,0:T(8,128)} %bitcast.6, f32[256,256]{1,0:T(8,128)} %bitcast.7, f32[256,256]{1,0:T(8,128)} %bitcast.5, f32[256,256]{1,0:T(8,128)} %bitcast.4, pred[]{:T(512)S(6)} %lt.3), kind=kLoop, calls=%fused_computation | loop fusion | flops 393216 | bytes 1572865 | tf_op jit(solution)/shard_map/jit(_where)/select_n | solution.py:350
  1.9 3.0 %collective-permute-start = (f32[256,256]{1,0:T(8,128)S(1)}, f32[256,256]{1,0:T(8,128)S(1)}, u32[]{:S(2)}, u32[]{:S(2)}) collective-permute-start(f32[256,256]{1,0:T(8,128)S(1)} %shard_map.79.refs_1_), channel_id=1, source_target_pairs={{0,16},{4,12},{8,24},{12,4},{16,0},{20,28},{24,8},{28,20},{1,17},{... | collective-permute-start | bytes 786440 | tf_op jit(solution)/shard_map/a0/ppermute | solution.py:307
  5.0 1.6 %collective-permute-start.3 = (f32[256,256]{1,0:T(8,128)S(1)}, f32[256,256]{1,0:T(8,128)S(1)}, u32[]{:S(2)}, u32[]{:S(2)}) collective-permute-start(f32[256,256]{1,0:T(8,128)S(1)} %get-tuple-element.52.refs_1_), channel_id=1, source_target_pairs={{0,8},{4,20},{8,0},{12,28},{16,24},{20,4},{24,16},{28,12},{1,9},{5... | collective-permute-start | bytes 786440 | tf_op jit(solution)/shard_map/b0/ppermute | solution.py:307
  6.5 1.6 %collective-permute-start.1 = (f32[256,256]{1,0:T(8,128)S(1)}, f32[256,256]{1,0:T(8,128)S(1)}, u32[]{:S(2)}, u32[]{:S(2)}) collective-permute-start(f32[256,256]{1,0:T(8,128)S(1)} %get-tuple-element.52.refs_1_), channel_id=1, source_target_pairs={{0,1},{1,2},{2,3},{3,0},{4,5},{5,6},{6,7},{7,4},{8,9},{9,10},{10,1... | collective-permute-start | bytes 786440 | tf_op jit(solution)/shard_map/p1/ppermute | solution.py:340
  9.9 1.5 %collective-permute-done.refs_2_ = f32[256,256]{1,0:T(8,128)S(1)} collective-permute-done((f32[256,256]{1,0:T(8,128)S(1)}, f32[256,256]{1,0:T(8,128)S(1)}, u32[]{:S(2)}, u32[]{:S(2)}) %collective-permute-start) | collective-permute-done | bytes 262176 | tf_op jit(solution)/shard_map/a0/ppermute | solution.py:307
  11.5 2.8 %collective-permute-start.5 = (f32[256,256]{1,0:T(8,128)S(1)}, f32[256,256]{1,0:T(8,128)S(1)}, u32[]{:S(2)}, u32[]{:S(2)}) collective-permute-start(f32[256,256]{1,0:T(8,128)S(1)} %get-tuple-element.57.refs_2_), channel_id=1, source_target_pairs={{0,8},{4,20},{8,0},{12,28},{16,24},{20,4},{24,16},{28,12},{1,9},{5... | collective-permute-start | bytes 786440 | tf_op jit(solution)/shard_map/d0/ppermute | solution.py:307
  14.2 3.6 %collective-permute-start.4 = (f32[256,256]{1,0:T(8,128)S(1)}, f32[256,256]{1,0:T(8,128)S(1)}, u32[]{:S(2)}, u32[]{:S(2)}) collective-permute-start(f32[256,256]{1,0:T(8,128)S(1)} %get-tuple-element.53.refs_0_), channel_id=1, source_target_pairs={{0,3},{1,0},{2,1},{3,2},{4,7},{5,4},{6,5},{7,6},{8,11},{9,8},{10,9... | collective-permute-start | bytes 786440 | tf_op jit(solution)/shard_map/p2/ppermute | solution.py:340
  19.8 1.6 %collective-permute-start.7 = (f32[256,256]{1,0:T(8,128)S(1)}, f32[256,256]{1,0:T(8,128)S(1)}, u32[]{:S(2)}, u32[]{:S(2)}) collective-permute-start(f32[256,256]{1,0:T(8,128)S(1)} %get-tuple-element.56.refs_1_), channel_id=1, source_target_pairs={{0,1},{1,2},{2,3},{3,0},{4,5},{5,6},{6,7},{7,4},{8,9},{9,10},{10,1... | collective-permute-start | bytes 786440 | tf_op jit(solution)/shard_map/p3/ppermute | solution.py:340
  21.7 1.8 %collective-permute-start.8 = (f32[256,256]{1,0:T(8,128)S(1)}, f32[256,256]{1,0:T(8,128)S(1)}, u32[]{:S(2)}, u32[]{:S(2)}) collective-permute-start(f32[256,256]{1,0:T(8,128)S(1)} %get-tuple-element.61.refs_0_), channel_id=1, source_target_pairs={{0,8},{4,12},{8,0},{12,4},{16,24},{20,28},{24,16},{28,20},{1,9},{5... | collective-permute-start | bytes 786440 | tf_op jit(solution)/shard_map/xy/ppermute | solution.py:307
  23.5 1.1 %collective-permute-start.9 = (f32[256,256]{1,0:T(8,128)S(1)}, f32[256,256]{1,0:T(8,128)S(1)}, u32[]{:S(2)}, u32[]{:S(2)}) collective-permute-start(f32[256,256]{1,0:T(8,128)S(1)} %get-tuple-element.64.refs_2_), channel_id=1, source_target_pairs={{0,16},{4,12},{8,24},{12,4},{16,0},{20,28},{24,8},{28,20},{1,17},{... | collective-permute-start | bytes 786440 | tf_op jit(solution)/shard_map/a2/ppermute | solution.py:307
  25.0 5.9 %collective-permute-done.8.refs_3_.refs_1_ = f32[256,256]{1,0:T(8,128)S(1)} collective-permute-done((f32[256,256]{1,0:T(8,128)S(1)}, f32[256,256]{1,0:T(8,128)S(1)}, u32[]{:S(2)}, u32[]{:S(2)}) %collective-permute-start.8) | collective-permute-done | bytes 262176 | tf_op jit(solution)/shard_map/xy/ppermute | solution.py:307
  31.0 1.2 %collective-permute-start.10 = (f32[256,256]{1,0:T(8,128)S(1)}, f32[256,256]{1,0:T(8,128)S(1)}, u32[]{:S(2)}, u32[]{:S(2)}) collective-permute-start(f32[256,256]{1,0:T(8,128)S(1)} %get-tuple-element.66.refs_1_), channel_id=1, source_target_pairs={{0,16},{4,12},{8,24},{12,4},{16,0},{20,28},{24,8},{28,20},{1,17},{... | collective-permute-start | bytes 786440 | tf_op jit(solution)/shard_map/a3/ppermute | solution.py:307
  34.4 2.2 %collective-permute-start.15 = (f32[256,256]{1,0:T(8,128)S(1)}, f32[256,256]{1,0:T(8,128)S(1)}, u32[]{:S(2)}, u32[]{:S(2)}) collective-permute-start(f32[256,256]{1,0:T(8,128)S(1)} %get-tuple-element.68.refs_6_), channel_id=1, source_target_pairs={{0,3},{1,0},{2,1},{3,2},{4,7},{5,4},{6,5},{7,6},{8,11},{9,8},{10,9... | collective-permute-start | bytes 786440 | tf_op jit(solution)/shard_map/d2/ppermute | solution.py:340
  36.6 1.4 %collective-permute-done.10.refs_2_ = f32[256,256]{1,0:T(8,128)S(1)} collective-permute-done((f32[256,256]{1,0:T(8,128)S(1)}, f32[256,256]{1,0:T(8,128)S(1)}, u32[]{:S(2)}, u32[]{:S(2)}) %collective-permute-start.10) | collective-permute-done | bytes 262176 | tf_op jit(solution)/shard_map/a3/ppermute | solution.py:307
  38.0 1.9 %collective-permute-done.12.refs_4_.refs_7_ = f32[256,256]{1,0:T(8,128)S(1)} collective-permute-done((f32[256,256]{1,0:T(8,128)S(1)}, f32[256,256]{1,0:T(8,128)S(1)}, u32[]{:S(2)}, u32[]{:S(2)}) %collective-permute-start.12) | collective-permute-done | bytes 262176 | tf_op jit(solution)/shard_map/d1/ppermute | solution.py:307
  40.7 1.7 %collective-permute-start.22 = (f32[256,256]{1,0:T(8,128)S(1)}, f32[256,256]{1,0:T(8,128)S(1)}, u32[]{:S(2)}, u32[]{:S(2)}) collective-permute-start(f32[256,256]{1,0:T(8,128)S(1)} %shard_map.96.refs_2_), channel_id=1, source_target_pairs={{0,1},{1,2},{2,3},{3,0},{4,5},{5,6},{6,7},{7,4},{8,9},{9,10},{10,1... | collective-permute-start | bytes 786440 | tf_op jit(solution)/shard_map/l1/ppermute | solution.py:340
  43.3 1.1 %collective-permute-start.18 = (f32[256,256]{1,0:T(8,128)S(1)}, f32[256,256]{1,0:T(8,128)S(1)}, u32[]{:S(2)}, u32[]{:S(2)}) collective-permute-start(f32[256,256]{1,0:T(8,128)S(1)} %get-tuple-element.80.refs_1_), channel_id=1, source_target_pairs={{0,8},{4,20},{8,0},{12,28},{16,24},{20,4},{24,16},{28,12},{1,9},{5... | collective-permute-start | bytes 786440 | tf_op jit(solution)/shard_map/d3/ppermute | solution.py:307
  45.2 2.6 %shard_map.90 = (bf16[2,1024,256]{2,1,0:T(8,128)(2,1)S(1)}, bf16[2,1024,256]{2,1,0:T(8,128)(2,1)S(1)}, bf16[2,1024,256]{2,1,0:T(8,128)(2,1)S(1)}, bf16[2,1024,25...) custom-call(f32[2048,256]{1,0:T(8,128)S(1)} %shard_map.89.mine, ...), custom_call_target="tpu_custom_call" | custom-call | flops 1610612736 | tf_op jit(solution)/shard_map/pallas_call | solution.py:263
  48.9 2.7 %shard_map.93 = (bf16[2,1024,256]{2,1,0:T(8,128)(2,1)S(1)}, bf16[2,1024,256]{2,1,0:T(8,128)(2,1)S(1)}, f32[1024,256]{1,0:T(8,128)S(1)}, f32[1024,256]{1,0:T(8,128)S(1)}, f32[1024,256]{1,0:T(8,128)S(1)}) custom-call(f32[1024,256]{1,0:T(8,128)S(1)} %shard_map.92.mine, ...), custom_call_target="tpu_custom_call", output_to_operand_aliasing={{2}: (6, {}), {3}: (7, {})} | custom-call | flops 2013265920 | tf_op jit(solution)/shard_map/pallas_call | solution.py:263
  52.3 2.9 %collective-permute-start.23 = (f32[256,256]{1,0:T(8,128)S(1)}, f32[256,256]{1,0:T(8,128)S(1)}, u32[]{:S(2)}, u32[]{:S(2)}) collective-permute-start(f32[256,256]{1,0:T(8,128)S(1)} %get-tuple-element.94.refs_8_), channel_id=1, source_target_pairs={{0,3},{1,0},{2,1},{3,2},{4,7},{5,4},{6,5},{7,6},{8,11},{9,8},{10,9... | collective-permute-start | bytes 786440 | tf_op jit(solution)/shard_map/l2/ppermute | solution.py:340
  55.3 10.2 %shard_map.100 = (f32[1024,128]{1,0:T(8,128)S(1)}, bf16[2,1024,256]{2,1,0:T(8,128)(2,1)S(1)}, bf16[2,1024,256]{2,1,0:T(8,128)(2,1)S(1)}) custom-call(f32[768,256]{1,0:T(8,128)S(1)} %shard_map.95.refs_0_, f32[256,256]{1,0:T(8,128)S(1)} %get-tuple-element.85.refs_1_, f32[768,256]{1,0:T(8,128)S(1)} %collective-permute-done.20.refs_3_.refs_2_, ...), custom_call_target="tpu_custom_call" | custom-call | flops 48318382080 | tf_op jit(solution)/shard_map/pallas_call | solution.py:263
  65.6 3.2 %collective-permute-done.24.refs_3_.refs_11_ = f32[256,256]{1,0:T(8,128)S(1)} collective-permute-done((f32[256,256]{1,0:T(8,128)S(1)}, f32[256,256]{1,0:T(8,128)S(1)}, u32[]{:S(2)}, u32[]{:S(2)}) %collective-permute-start.24) | collective-permute-done | bytes 262176 | tf_op jit(solution)/shard_map/l3/ppermute | solution.py:340
  68.8 1.8 %shard_map.102 = (bf16[256,1024]{1,0:T(8,128)(2,1)S(1)}, bf16[256,1024]{1,0:T(8,128)(2,1)S(1)}) custom-call(bf16[2,1024,256]{2,1,0:T(8,128)(2,1)S(1)} %get-tuple-element.69.refs_0_.refs_4_, bf16[2,1024,256]{2,1,0:T(8,128)(2,1)S(1)} %get-tuple-element.70.refs_1_.refs_2_.refs_5_, bf16[2,1024,256]{2,1,0:T(8,128)(2,1)S(1)} %get-tuple-element.78.refs_3_.refs_6_.refs_2_, ...), custom_call_target="tpu_custom_call" | custom-call | flops 1610612736 | tf_op jit(solution)/shard_map/pallas_call | solution.py:263
  72.5 6.5 %collective-permute-done.26.across = f32[256,256]{1,0:T(8,128)S(1)} collective-permute-done((f32[256,256]{1,0:T(8,128)S(1)}, f32[256,256]{1,0:T(8,128)S(1)}, u32[]{:S(2)}, u32[]{:S(2)}) %collective-permute-start.26) | collective-permute-done | bytes 262176 | tf_op jit(solution)/shard_map/ppermute | solution.py:307
  (65 shorter events, 13.3 us)
Async XLA Ops:
  1.9 9.5 %collective-permute-start = (f32[256,256]{1,0:T(8,128)S(1)}, f32[256,256]{1,0:T(8,128)S(1)}, u32[]{:S(2)}, u32[]{:S(2)}) collective-permute-start(f32[256,256]{1,0:T(8,128)S(1)} %shard_map.79.refs_1_), channel_id=1, source_target_pairs={{0,16},{4,12},{8,24},{12,4},{16,0},{20,28},{24,8},{28,20},{1,17},{... | collective-permute-start | bytes 786440 | tf_op jit(solution)/shard_map/a0/ppermute | solution.py:307
  5.0 12.9 %collective-permute-start.3 = (f32[256,256]{1,0:T(8,128)S(1)}, f32[256,256]{1,0:T(8,128)S(1)}, u32[]{:S(2)}, u32[]{:S(2)}) collective-permute-start(f32[256,256]{1,0:T(8,128)S(1)} %get-tuple-element.52.refs_1_), channel_id=1, source_target_pairs={{0,8},{4,20},{8,0},{12,28},{16,24},{20,4},{24,16},{28,12},{1,9},{5... | collective-permute-start | bytes 786440 | tf_op jit(solution)/shard_map/b0/ppermute | solution.py:307
  6.5 11.3 %collective-permute-start.1 = (f32[256,256]{1,0:T(8,128)S(1)}, f32[256,256]{1,0:T(8,128)S(1)}, u32[]{:S(2)}, u32[]{:S(2)}) collective-permute-start(f32[256,256]{1,0:T(8,128)S(1)} %get-tuple-element.52.refs_1_), channel_id=1, source_target_pairs={{0,1},{1,2},{2,3},{3,0},{4,5},{5,6},{6,7},{7,4},{8,9},{9,10},{10,1... | collective-permute-start | bytes 786440 | tf_op jit(solution)/shard_map/p1/ppermute | solution.py:340
  9.3 9.5 %collective-permute-start.2 = (f32[264,256]{1,0:T(8,128)S(1)}, f32[264,256]{1,0:T(8,128)S(1)}, u32[]{:S(2)}, u32[]{:S(2)}) collective-permute-start(f32[264,256]{1,0:T(8,128)S(1)} %shard_map.82.own), channel_id=1, source_target_pairs={{0,16},{4,20},{8,24},{12,28},{16,0},{20,4},{24,8},{28,12},{1,17},{... | collective-permute-start | bytes 811016 | tf_op jit(solution)/shard_map/xx/ppermute | solution.py:307
  11.5 12.0 %collective-permute-start.5 = (f32[256,256]{1,0:T(8,128)S(1)}, f32[256,256]{1,0:T(8,128)S(1)}, u32[]{:S(2)}, u32[]{:S(2)}) collective-permute-start(f32[256,256]{1,0:T(8,128)S(1)} %get-tuple-element.57.refs_2_), channel_id=1, source_target_pairs={{0,8},{4,20},{8,0},{12,28},{16,24},{20,4},{24,16},{28,12},{1,9},{5... | collective-permute-start | bytes 786440 | tf_op jit(solution)/shard_map/d0/ppermute | solution.py:307
  14.2 9.2 %collective-permute-start.4 = (f32[256,256]{1,0:T(8,128)S(1)}, f32[256,256]{1,0:T(8,128)S(1)}, u32[]{:S(2)}, u32[]{:S(2)}) collective-permute-start(f32[256,256]{1,0:T(8,128)S(1)} %get-tuple-element.53.refs_0_), channel_id=1, source_target_pairs={{0,3},{1,0},{2,1},{3,2},{4,7},{5,4},{6,5},{7,6},{8,11},{9,8},{10,9... | collective-permute-start | bytes 786440 | tf_op jit(solution)/shard_map/p2/ppermute | solution.py:340
  18.9 12.1 %collective-permute-start.6 = (f32[256,256]{1,0:T(8,128)S(1)}, f32[256,256]{1,0:T(8,128)S(1)}, u32[]{:S(2)}, u32[]{:S(2)}) collective-permute-start(f32[256,256]{1,0:T(8,128)S(1)} %get-tuple-element.56.refs_1_), channel_id=1, source_target_pairs={{0,16},{4,12},{8,24},{12,4},{16,0},{20,28},{24,8},{28,20},{1,17},{... | collective-permute-start | bytes 786440 | tf_op jit(solution)/shard_map/a1/ppermute | solution.py:307
  19.8 11.2 %collective-permute-start.7 = (f32[256,256]{1,0:T(8,128)S(1)}, f32[256,256]{1,0:T(8,128)S(1)}, u32[]{:S(2)}, u32[]{:S(2)}) collective-permute-start(f32[256,256]{1,0:T(8,128)S(1)} %get-tuple-element.56.refs_1_), channel_id=1, source_target_pairs={{0,1},{1,2},{2,3},{3,0},{4,5},{5,6},{6,7},{7,4},{8,9},{9,10},{10,1... | collective-permute-start | bytes 786440 | tf_op jit(solution)/shard_map/p3/ppermute | solution.py:340
  21.7 9.3 %collective-permute-start.8 = (f32[256,256]{1,0:T(8,128)S(1)}, f32[256,256]{1,0:T(8,128)S(1)}, u32[]{:S(2)}, u32[]{:S(2)}) collective-permute-start(f32[256,256]{1,0:T(8,128)S(1)} %get-tuple-element.61.refs_0_), channel_id=1, source_target_pairs={{0,8},{4,12},{8,0},{12,4},{16,24},{20,28},{24,16},{28,20},{1,9},{5... | collective-permute-start | bytes 786440 | tf_op jit(solution)/shard_map/xy/ppermute | solution.py:307
  23.5 9.8 %collective-permute-start.9 = (f32[256,256]{1,0:T(8,128)S(1)}, f32[256,256]{1,0:T(8,128)S(1)}, u32[]{:S(2)}, u32[]{:S(2)}) collective-permute-start(f32[256,256]{1,0:T(8,128)S(1)} %get-tuple-element.64.refs_2_), channel_id=1, source_target_pairs={{0,16},{4,12},{8,24},{12,4},{16,0},{20,28},{24,8},{28,20},{1,17},{... | collective-permute-start | bytes 786440 | tf_op jit(solution)/shard_map/a2/ppermute | solution.py:307
  24.5 12.1 %collective-permute-start.11 = (f32[256,256]{1,0:T(8,128)S(1)}, f32[256,256]{1,0:T(8,128)S(1)}, u32[]{:S(2)}, u32[]{:S(2)}) collective-permute-start(f32[256,256]{1,0:T(8,128)S(1)} %get-tuple-element.58.refs_1_), channel_id=1, source_target_pairs={{0,8},{4,20},{8,0},{12,28},{16,24},{20,4},{24,16},{28,12},{1,9},{5... | collective-permute-start | bytes 786440 | tf_op jit(solution)/shard_map/b1/ppermute | solution.py:307
  31.0 7.0 %collective-permute-start.10 = (f32[256,256]{1,0:T(8,128)S(1)}, f32[256,256]{1,0:T(8,128)S(1)}, u32[]{:S(2)}, u32[]{:S(2)}) collective-permute-start(f32[256,256]{1,0:T(8,128)S(1)} %get-tuple-element.66.refs_1_), channel_id=1, source_target_pairs={{0,16},{4,12},{8,24},{12,4},{16,0},{20,28},{24,8},{28,20},{1,17},{... | collective-permute-start | bytes 786440 | tf_op jit(solution)/shard_map/a3/ppermute | solution.py:307
  32.3 7.6 %collective-permute-start.12 = (f32[256,256]{1,0:T(8,128)S(1)}, f32[256,256]{1,0:T(8,128)S(1)}, u32[]{:S(2)}, u32[]{:S(2)}) collective-permute-start(f32[256,256]{1,0:T(8,128)S(1)} %get-tuple-element.62.refs_3_), channel_id=1, source_target_pairs={{0,8},{4,20},{8,0},{12,28},{16,24},{20,4},{24,16},{28,12},{1,9},{5... | collective-permute-start | bytes 786440 | tf_op jit(solution)/shard_map/d1/ppermute | solution.py:307
  33.4 10.0 %collective-permute-start.14 = (f32[256,256]{1,0:T(8,128)S(1)}, f32[256,256]{1,0:T(8,128)S(1)}, u32[]{:S(2)}, u32[]{:S(2)}) collective-permute-start(f32[256,256]{1,0:T(8,128)S(1)} %get-tuple-element.71.refs_0_), channel_id=1, source_target_pairs={{0,8},{4,20},{8,0},{12,28},{16,24},{20,4},{24,16},{28,12},{1,9},{5... | collective-permute-start | bytes 786440 | tf_op jit(solution)/shard_map/b2/ppermute | solution.py:307
  34.4 10.0 %collective-permute-start.15 = (f32[256,256]{1,0:T(8,128)S(1)}, f32[256,256]{1,0:T(8,128)S(1)}, u32[]{:S(2)}, u32[]{:S(2)}) collective-permute-start(f32[256,256]{1,0:T(8,128)S(1)} %get-tuple-element.68.refs_6_), channel_id=1, source_target_pairs={{0,3},{1,0},{2,1},{3,2},{4,7},{5,4},{6,5},{7,6},{8,11},{9,8},{10,9... | collective-permute-start | bytes 786440 | tf_op jit(solution)/shard_map/d2/ppermute | solution.py:340
  40.7 14.5 %collective-permute-start.22 = (f32[256,256]{1,0:T(8,128)S(1)}, f32[256,256]{1,0:T(8,128)S(1)}, u32[]{:S(2)}, u32[]{:S(2)}) collective-permute-start(f32[256,256]{1,0:T(8,128)S(1)} %shard_map.96.refs_2_), channel_id=1, source_target_pairs={{0,1},{1,2},{2,3},{3,0},{4,5},{5,6},{6,7},{7,4},{8,9},{9,10},{10,1... | collective-permute-start | bytes 786440 | tf_op jit(solution)/shard_map/l1/ppermute | solution.py:340
  42.4 6.4 %collective-permute-start.17 = (f32[256,256]{1,0:T(8,128)S(1)}, f32[256,256]{1,0:T(8,128)S(1)}, u32[]{:S(2)}, u32[]{:S(2)}) collective-permute-start(f32[256,256]{1,0:T(8,128)S(1)} %get-tuple-element.79.refs_0_), channel_id=1, source_target_pairs={{0,8},{4,20},{8,0},{12,28},{16,24},{20,4},{24,16},{28,12},{1,9},{5... | collective-permute-start | bytes 786440 | tf_op jit(solution)/shard_map/b3/ppermute | solution.py:307
  43.3 8.3 %collective-permute-start.18 = (f32[256,256]{1,0:T(8,128)S(1)}, f32[256,256]{1,0:T(8,128)S(1)}, u32[]{:S(2)}, u32[]{:S(2)}) collective-permute-start(f32[256,256]{1,0:T(8,128)S(1)} %get-tuple-element.80.refs_1_), channel_id=1, source_target_pairs={{0,8},{4,20},{8,0},{12,28},{16,24},{20,4},{24,16},{28,12},{1,9},{5... | collective-permute-start | bytes 786440 | tf_op jit(solution)/shard_map/d3/ppermute | solution.py:307
  44.7 7.0 %collective-permute-start.19 = (f32[512,256]{1,0:T(8,128)S(1)}, f32[512,256]{1,0:T(8,128)S(1)}, u32[]{:S(2)}, u32[]{:S(2)}) collective-permute-start(f32[512,256]{1,0:T(8,128)S(1)} %shard_map.97.refs_13_), channel_id=1, source_target_pairs={{0,4},{4,0},{8,12},{12,8},{1,5},{5,1},{9,13},{13,9},{2,6},{6,2},{1... | collective-permute-start | bytes 1572872 | tf_op jit(solution)/shard_map/tx/ppermute | solution.py:313
  48.9 6.3 %collective-permute-start.20 = (f32[768,256]{1,0:T(8,128)S(1)}, f32[768,256]{1,0:T(8,128)S(1)}, u32[]{:S(2)}, u32[]{:S(2)}) collective-permute-start(f32[768,256]{1,0:T(8,128)S(1)} %shard_map.95.refs_0_), channel_id=1, source_target_pairs={{0,4},{4,0},{8,12},{12,8},{1,5},{5,1},{9,13},{13,9},{2,6},{6,2},{1... | collective-permute-start | bytes 2359304 | tf_op jit(solution)/shard_map/t3/ppermute | solution.py:313
  52.3 13.3 %collective-permute-start.23 = (f32[256,256]{1,0:T(8,128)S(1)}, f32[256,256]{1,0:T(8,128)S(1)}, u32[]{:S(2)}, u32[]{:S(2)}) collective-permute-start(f32[256,256]{1,0:T(8,128)S(1)} %get-tuple-element.94.refs_8_), channel_id=1, source_target_pairs={{0,3},{1,0},{2,1},{3,2},{4,7},{5,4},{6,5},{7,6},{8,11},{9,8},{10,9... | collective-permute-start | bytes 786440 | tf_op jit(solution)/shard_map/l2/ppermute | solution.py:340
  55.2 13.6 %collective-permute-start.24 = (f32[256,256]{1,0:T(8,128)S(1)}, f32[256,256]{1,0:T(8,128)S(1)}, u32[]{:S(2)}, u32[]{:S(2)}) collective-permute-start(f32[256,256]{1,0:T(8,128)S(1)} %get-tuple-element.95.refs_9_), channel_id=1, source_target_pairs={{0,1},{1,2},{2,3},{3,0},{4,5},{5,6},{6,7},{7,4},{8,9},{9,10},{10,1... | collective-permute-start | bytes 786440 | tf_op jit(solution)/shard_map/l3/ppermute | solution.py:340
  65.4 5.2 %collective-permute-start.25 = (f32[1024,128]{1,0:T(8,128)S(1)}, f32[1024,128]{1,0:T(8,128)S(1)}, u32[]{:S(2)}, u32[]{:S(2)}) collective-permute-start(f32[1024,128]{1,0:T(8,128)S(1)} %get-tuple-element.97.refs_1_.refs_0_), channel_id=1, source_target_pairs={{0,4},{4,0},{8,12},{12,8},{1,5},{5,1},{9,13},{13,9},{2,6},{6,2},{1... | collective-permute-start | bytes 1572872 | tf_op jit(solution)/shard_map/ppermute | solution.py:313
  71.5 7.5 %collective-permute-start.26 = (f32[256,256]{1,0:T(8,128)S(1)}, f32[256,256]{1,0:T(8,128)S(1)}, u32[]{:S(2)}, u32[]{:S(2)}) collective-permute-start(f32[256,256]{1,0:T(8,128)S(1)} %shard_map.103.own), channel_id=1, source_target_pairs={{0,16},{4,20},{8,24},{12,28},{16,0},{20,4},{24,8},{28,12},{1,17},{... | collective-permute-start | bytes 786440 | tf_op jit(solution)/shard_map/ppermute | solution.py:307
  (6 other events, 20.6 us)

commit v5 on v4

--- a/solution.py
+++ b/solution.py
@@ -15,14 +15,14 @@
 SLOTS = {
     "p1": (1, 3),
     "a0": (0, 2),
-    "b0": (1, 3),
+    "b0": (0, 2),
+    "t01": (7, 9),
     "xx": (1, 3),
     "p2": (2, 4),
     "d0": (2, 4),
     "a1": (3, 5),
     "b1": (4, 7),
     "p3": (3, 5),
-    "a2": (4, 6),
     "xy": (3, 5),
     "d1": (5, 7),
     "a3": (5, 7),
@@ -30,12 +30,12 @@
     "b2": (6, 8),
     "b3": (7, 9),
     "d3": (7, 10),
-    "t01": (7, 9),
-    "tx": (8, 10),
     "t2": (8, 10),
     "td": (10, 11),
     "l1": (9, 11),
     "t3": (9, 11),
+    "tx": (8, 10),
+    "a2": (4, 6),
     "l2": (10, 12),
     "l3": (11, 12),
 }

time: 80 us -> 79.6 us (level)
  starting transfers between devices: 34.1 us -> 32.8 us
    ppermute x14, starting transfers between devices: 18.5 us -> 17.3 us  [plane(): return lax.ppermute(value, ('layer', 'row'), route)]
    ppermute x7, starting transfers between devices: 13.6 us -> 14.6 us  [along(): lax.ppermute(value, 'col', [(i, (i + shift) % blocks) for i in range(bloc...]
    ppermute x6, starting transfers between devices: 1.93 us -> 0.97 us  [sibling(): lax.ppermute(value, 'row', [(i, i ^ 1) for i in range(grid.row_count)])]
  transfers between devices with their start and end apart: 27 -> 27, of which waited for: 8 -> 13; matrix products, arithmetic and copies ran while one was open for 0% -> 0% of each run, Pallas kernels for 24% -> 24%
where the time goes in v5:
time: 79.6 us; the launch traced here: 79.4 us
  starting transfers between devices  32.8 us (41%)
  waiting for transfers between devices  22.9 us (29%)
  Pallas kernels  20.5 us (26%)
  between operations  1.59 us (2%)
  other arithmetic  1.26 us (2%)
    pallas_call x28, Pallas kernels, call(): pl.pallas_call(kernel, out_shape=outs, in_specs=specs, out_specs=jax.tree...  20.5 us
    ppermute x14, waiting for transfers between devices, plane(): return lax.ppermute(value, ('layer', 'row'), route)  19.5 us
    ppermute x14, starting transfers between devices, plane(): return lax.ppermute(value, ('layer', 'row'), route)  17.3 us
    ppermute x7, starting transfers between devices, along(): lax.ppermute(value, 'col', [(i, (i + shift) % blocks) for i in range(bloc...  14.6 us
    ppermute x7, waiting for transfers between devices, along(): lax.ppermute(value, 'col', [(i, (i + shift) % blocks) for i in range(bloc...  2.99 us
  transfers between devices with their start and end apart: 27, of which 13 were waited for; matrix products, arithmetic and copies ran while one was open for 0% of the time, Pallas kernels for 24%

profile of v5, /device:TPU:0, one launch (start us, length us, event | category | flops | bytes accessed | tf_op | source)
XLA Modules:
  0.0 79.4 jit_solution(16866672648845161961)
XLA Ops:
  0.6 1.3 %maximum_select_fusion.refs_0_ = f32[512,256]{1,0:T(8,128)S(1)} fusion(f32[256,256]{1,0:T(8,128)} %bitcast.6, f32[256,256]{1,0:T(8,128)} %bitcast.7, f32[256,256]{1,0:T(8,128)} %bitcast.5, f32[256,256]{1,0:T(8,128)} %bitcast.4, pred[]{:T(512)S(6)} %lt.3), kind=kLoop, calls=%fused_computation | loop fusion | flops 393216 | bytes 1572865 | tf_op jit(solution)/shard_map/jit(_where)/select_n | solution.py:350
  1.9 3.0 %collective-permute-start.1 = (f32[256,256]{1,0:T(8,128)S(1)}, f32[256,256]{1,0:T(8,128)S(1)}, u32[]{:S(2)}, u32[]{:S(2)}) collective-permute-start(f32[256,256]{1,0:T(8,128)S(1)} %shard_map.79.refs_1_), channel_id=1, source_target_pairs={{0,8},{4,20},{8,0},{12,28},{16,24},{20,4},{24,16},{28,12},{1,9},{5... | collective-permute-start | bytes 786440 | tf_op jit(solution)/shard_map/b0/ppermute | solution.py:307
  5.0 1.5 %collective-permute-start = (f32[256,256]{1,0:T(8,128)S(1)}, f32[256,256]{1,0:T(8,128)S(1)}, u32[]{:S(2)}, u32[]{:S(2)}) collective-permute-start(f32[256,256]{1,0:T(8,128)S(1)} %shard_map.79.refs_1_), channel_id=1, source_target_pairs={{0,16},{4,12},{8,24},{12,4},{16,0},{20,28},{24,8},{28,20},{1,17},{... | collective-permute-start | bytes 786440 | tf_op jit(solution)/shard_map/a0/ppermute | solution.py:307
  8.6 1.6 %collective-permute-start.2 = (f32[256,256]{1,0:T(8,128)S(1)}, f32[256,256]{1,0:T(8,128)S(1)}, u32[]{:S(2)}, u32[]{:S(2)}) collective-permute-start(f32[256,256]{1,0:T(8,128)S(1)} %get-tuple-element.52.refs_1_), channel_id=1, source_target_pairs={{0,1},{1,2},{2,3},{3,0},{4,5},{5,6},{6,7},{7,4},{8,9},{9,10},{10,1... | collective-permute-start | bytes 786440 | tf_op jit(solution)/shard_map/p1/ppermute | solution.py:340
  10.2 1.4 %collective-permute-done.1.refs_3_.refs_4_ = f32[256,256]{1,0:T(8,128)S(1)} collective-permute-done((f32[256,256]{1,0:T(8,128)S(1)}, f32[256,256]{1,0:T(8,128)S(1)}, u32[]{:S(2)}, u32[]{:S(2)}) %collective-permute-start.1) | collective-permute-done | bytes 262176 | tf_op jit(solution)/shard_map/b0/ppermute | solution.py:307
  11.6 1.4 %collective-permute-done.refs_2_ = f32[256,256]{1,0:T(8,128)S(1)} collective-permute-done((f32[256,256]{1,0:T(8,128)S(1)}, f32[256,256]{1,0:T(8,128)S(1)}, u32[]{:S(2)}, u32[]{:S(2)}) %collective-permute-start) | collective-permute-done | bytes 262176 | tf_op jit(solution)/shard_map/a0/ppermute | solution.py:307
  13.0 1.3 %collective-permute-start.5 = (f32[256,256]{1,0:T(8,128)S(1)}, f32[256,256]{1,0:T(8,128)S(1)}, u32[]{:S(2)}, u32[]{:S(2)}) collective-permute-start(f32[256,256]{1,0:T(8,128)S(1)} %get-tuple-element.57.refs_2_), channel_id=1, source_target_pairs={{0,8},{4,20},{8,0},{12,28},{16,24},{20,4},{24,16},{28,12},{1,9},{5... | collective-permute-start | bytes 786440 | tf_op jit(solution)/shard_map/d0/ppermute | solution.py:307
  14.3 4.1 %collective-permute-start.4 = (f32[256,256]{1,0:T(8,128)S(1)}, f32[256,256]{1,0:T(8,128)S(1)}, u32[]{:S(2)}, u32[]{:S(2)}) collective-permute-start(f32[256,256]{1,0:T(8,128)S(1)} %get-tuple-element.53.refs_0_), channel_id=1, source_target_pairs={{0,3},{1,0},{2,1},{3,2},{4,7},{5,4},{6,5},{7,6},{8,11},{9,8},{10,9... | collective-permute-start | bytes 786440 | tf_op jit(solution)/shard_map/p2/ppermute | solution.py:340
  18.8 2.5 %collective-permute-start.6 = (f32[256,256]{1,0:T(8,128)S(1)}, f32[256,256]{1,0:T(8,128)S(1)}, u32[]{:S(2)}, u32[]{:S(2)}) collective-permute-start(f32[256,256]{1,0:T(8,128)S(1)} %get-tuple-element.56.refs_1_), channel_id=1, source_target_pairs={{0,16},{4,12},{8,24},{12,4},{16,0},{20,28},{24,8},{28,20},{1,17},{... | collective-permute-start | bytes 786440 | tf_op jit(solution)/shard_map/a1/ppermute | solution.py:307
  21.4 1.6 %collective-permute-start.7 = (f32[256,256]{1,0:T(8,128)S(1)}, f32[256,256]{1,0:T(8,128)S(1)}, u32[]{:S(2)}, u32[]{:S(2)}) collective-permute-start(f32[256,256]{1,0:T(8,128)S(1)} %get-tuple-element.56.refs_1_), channel_id=1, source_target_pairs={{0,1},{1,2},{2,3},{3,0},{4,5},{5,6},{6,7},{7,4},{8,9},{9,10},{10,1... | collective-permute-start | bytes 786440 | tf_op jit(solution)/shard_map/p3/ppermute | solution.py:340
  25.1 1.7 %collective-permute-start.9 = (f32[256,256]{1,0:T(8,128)S(1)}, f32[256,256]{1,0:T(8,128)S(1)}, u32[]{:S(2)}, u32[]{:S(2)}) collective-permute-start(f32[256,256]{1,0:T(8,128)S(1)} %get-tuple-element.64.refs_2_), channel_id=1, source_target_pairs={{0,16},{4,12},{8,24},{12,4},{16,0},{20,28},{24,8},{28,20},{1,17},{... | collective-permute-start | bytes 786440 | tf_op jit(solution)/shard_map/a2/ppermute | solution.py:307
  26.8 1.3 %collective-permute-start.10 = (f32[256,256]{1,0:T(8,128)S(1)}, f32[256,256]{1,0:T(8,128)S(1)}, u32[]{:S(2)}, u32[]{:S(2)}) collective-permute-start(f32[256,256]{1,0:T(8,128)S(1)} %get-tuple-element.58.refs_1_), channel_id=1, source_target_pairs={{0,8},{4,20},{8,0},{12,28},{16,24},{20,4},{24,16},{28,12},{1,9},{5... | collective-permute-start | bytes 786440 | tf_op jit(solution)/shard_map/b1/ppermute | solution.py:307
  28.1 4.4 %collective-permute-done.8.refs_3_.refs_2_ = f32[256,256]{1,0:T(8,128)S(1)} collective-permute-done((f32[256,256]{1,0:T(8,128)S(1)}, f32[256,256]{1,0:T(8,128)S(1)}, u32[]{:S(2)}, u32[]{:S(2)}) %collective-permute-start.8) | collective-permute-done | bytes 262176 | tf_op jit(solution)/shard_map/xy/ppermute | solution.py:307
  32.7 1.2 %collective-permute-start.12 = (f32[256,256]{1,0:T(8,128)S(1)}, f32[256,256]{1,0:T(8,128)S(1)}, u32[]{:S(2)}, u32[]{:S(2)}) collective-permute-start(f32[256,256]{1,0:T(8,128)S(1)} %get-tuple-element.62.refs_3_), channel_id=1, source_target_pairs={{0,8},{4,20},{8,0},{12,28},{16,24},{20,4},{24,16},{28,12},{1,9},{5... | collective-permute-start | bytes 786440 | tf_op jit(solution)/shard_map/d1/ppermute | solution.py:307
  35.4 2.6 %collective-permute-start.15 = (f32[256,256]{1,0:T(8,128)S(1)}, f32[256,256]{1,0:T(8,128)S(1)}, u32[]{:S(2)}, u32[]{:S(2)}) collective-permute-start(f32[256,256]{1,0:T(8,128)S(1)} %get-tuple-element.68.refs_6_), channel_id=1, source_target_pairs={{0,3},{1,0},{2,1},{3,2},{4,7},{5,4},{6,5},{7,6},{8,11},{9,8},{10,9... | collective-permute-start | bytes 786440 | tf_op jit(solution)/shard_map/d2/ppermute | solution.py:340
  38.0 2.9 %collective-permute-done.11.refs_3_ = f32[256,256]{1,0:T(8,128)S(1)} collective-permute-done((f32[256,256]{1,0:T(8,128)S(1)}, f32[256,256]{1,0:T(8,128)S(1)}, u32[]{:S(2)}, u32[]{:S(2)}) %collective-permute-start.11) | collective-permute-done | bytes 262176 | tf_op jit(solution)/shard_map/a3/ppermute | solution.py:307
  41.2 1.2 %collective-permute-start.22 = (f32[256,256]{1,0:T(8,128)S(1)}, f32[256,256]{1,0:T(8,128)S(1)}, u32[]{:S(2)}, u32[]{:S(2)}) collective-permute-start(f32[256,256]{1,0:T(8,128)S(1)} %shard_map.96.refs_2_), channel_id=1, source_target_pairs={{0,1},{1,2},{2,3},{3,0},{4,5},{5,6},{6,7},{7,4},{8,9},{9,10},{10,1... | collective-permute-start | bytes 786440 | tf_op jit(solution)/shard_map/l1/ppermute | solution.py:340
  45.4 2.6 %shard_map.90 = (bf16[2,1024,256]{2,1,0:T(8,128)(2,1)S(1)}, bf16[2,1024,256]{2,1,0:T(8,128)(2,1)S(1)}, bf16[2,1024,256]{2,1,0:T(8,128)(2,1)S(1)}, bf16[2,1024,25...) custom-call(f32[2048,256]{1,0:T(8,128)S(1)} %shard_map.89.mine, ...), custom_call_target="tpu_custom_call" | custom-call | flops 1610612736 | tf_op jit(solution)/shard_map/pallas_call | solution.py:263
  49.0 2.7 %shard_map.93 = (bf16[2,1024,256]{2,1,0:T(8,128)(2,1)S(1)}, bf16[2,1024,256]{2,1,0:T(8,128)(2,1)S(1)}, f32[1024,256]{1,0:T(8,128)S(1)}, f32[1024,256]{1,0:T(8,128)S(1)}, f32[1024,256]{1,0:T(8,128)S(1)}) custom-call(f32[1024,256]{1,0:T(8,128)S(1)} %shard_map.92.mine, ...), custom_call_target="tpu_custom_call", output_to_operand_aliasing={{2}: (6, {}), {3}: (7, {})} | custom-call | flops 2013265920 | tf_op jit(solution)/shard_map/pallas_call | solution.py:263
  52.3 3.5 %collective-permute-start.23 = (f32[256,256]{1,0:T(8,128)S(1)}, f32[256,256]{1,0:T(8,128)S(1)}, u32[]{:S(2)}, u32[]{:S(2)}) collective-permute-start(f32[256,256]{1,0:T(8,128)S(1)} %get-tuple-element.94.refs_8_), channel_id=1, source_target_pairs={{0,3},{1,0},{2,1},{3,2},{4,7},{5,4},{6,5},{7,6},{8,11},{9,8},{10,9... | collective-permute-start | bytes 786440 | tf_op jit(solution)/shard_map/l2/ppermute | solution.py:340
  55.9 10.2 %shard_map.100 = (f32[1024,128]{1,0:T(8,128)S(1)}, bf16[2,1024,256]{2,1,0:T(8,128)(2,1)S(1)}, bf16[2,1024,256]{2,1,0:T(8,128)(2,1)S(1)}) custom-call(f32[768,256]{1,0:T(8,128)S(1)} %shard_map.95.refs_0_, f32[256,256]{1,0:T(8,128)S(1)} %get-tuple-element.85.refs_1_, f32[768,256]{1,0:T(8,128)S(1)} %collective-permute-done.20.refs_3_.refs_2_, ...), custom_call_target="tpu_custom_call" | custom-call | flops 48318382080 | tf_op jit(solution)/shard_map/pallas_call | solution.py:263
  66.2 1.8 %collective-permute-done.24.refs_3_.refs_11_ = f32[256,256]{1,0:T(8,128)S(1)} collective-permute-done((f32[256,256]{1,0:T(8,128)S(1)}, f32[256,256]{1,0:T(8,128)S(1)}, u32[]{:S(2)}, u32[]{:S(2)}) %collective-permute-start.24) | collective-permute-done | bytes 262176 | tf_op jit(solution)/shard_map/l3/ppermute | solution.py:340
  68.0 1.8 %shard_map.102 = (bf16[256,1024]{1,0:T(8,128)(2,1)S(1)}, bf16[256,1024]{1,0:T(8,128)(2,1)S(1)}) custom-call(bf16[2,1024,256]{2,1,0:T(8,128)(2,1)S(1)} %get-tuple-element.69.refs_0_.refs_4_, bf16[2,1024,256]{2,1,0:T(8,128)(2,1)S(1)} %get-tuple-element.70.refs_1_.refs_2_.refs_5_, bf16[2,1024,256]{2,1,0:T(8,128)(2,1)S(1)} %get-tuple-element.78.refs_3_.refs_6_.refs_2_, ...), custom_call_target="tpu_custom_call" | custom-call | flops 1610612736 | tf_op jit(solution)/shard_map/pallas_call | solution.py:263
  71.3 7.2 %collective-permute-done.26.across = f32[256,256]{1,0:T(8,128)S(1)} collective-permute-done((f32[256,256]{1,0:T(8,128)S(1)}, f32[256,256]{1,0:T(8,128)S(1)}, u32[]{:S(2)}, u32[]{:S(2)}) %collective-permute-start.26) | collective-permute-done | bytes 262176 | tf_op jit(solution)/shard_map/ppermute | solution.py:307
  (65 shorter events, 13.0 us)
Async XLA Ops:
  1.9 9.7 %collective-permute-start.1 = (f32[256,256]{1,0:T(8,128)S(1)}, f32[256,256]{1,0:T(8,128)S(1)}, u32[]{:S(2)}, u32[]{:S(2)}) collective-permute-start(f32[256,256]{1,0:T(8,128)S(1)} %shard_map.79.refs_1_), channel_id=1, source_target_pairs={{0,8},{4,20},{8,0},{12,28},{16,24},{20,4},{24,16},{28,12},{1,9},{5... | collective-permute-start | bytes 786440 | tf_op jit(solution)/shard_map/b0/ppermute | solution.py:307
  5.0 8.1 %collective-permute-start = (f32[256,256]{1,0:T(8,128)S(1)}, f32[256,256]{1,0:T(8,128)S(1)}, u32[]{:S(2)}, u32[]{:S(2)}) collective-permute-start(f32[256,256]{1,0:T(8,128)S(1)} %shard_map.79.refs_1_), channel_id=1, source_target_pairs={{0,16},{4,12},{8,24},{12,4},{16,0},{20,28},{24,8},{28,20},{1,17},{... | collective-permute-start | bytes 786440 | tf_op jit(solution)/shard_map/a0/ppermute | solution.py:307
  8.0 10.8 %collective-permute-start.3 = (f32[264,256]{1,0:T(8,128)S(1)}, f32[264,256]{1,0:T(8,128)S(1)}, u32[]{:S(2)}, u32[]{:S(2)}) collective-permute-start(f32[264,256]{1,0:T(8,128)S(1)} %shard_map.82.own), channel_id=1, source_target_pairs={{0,16},{4,20},{8,24},{12,28},{16,0},{20,4},{24,8},{28,12},{1,17},{... | collective-permute-start | bytes 811016 | tf_op jit(solution)/shard_map/xx/ppermute | solution.py:307
  8.6 9.8 %collective-permute-start.2 = (f32[256,256]{1,0:T(8,128)S(1)}, f32[256,256]{1,0:T(8,128)S(1)}, u32[]{:S(2)}, u32[]{:S(2)}) collective-permute-start(f32[256,256]{1,0:T(8,128)S(1)} %get-tuple-element.52.refs_1_), channel_id=1, source_target_pairs={{0,1},{1,2},{2,3},{3,0},{4,5},{5,6},{6,7},{7,4},{8,9},{9,10},{10,1... | collective-permute-start | bytes 786440 | tf_op jit(solution)/shard_map/p1/ppermute | solution.py:340
  13.0 11.0 %collective-permute-start.5 = (f32[256,256]{1,0:T(8,128)S(1)}, f32[256,256]{1,0:T(8,128)S(1)}, u32[]{:S(2)}, u32[]{:S(2)}) collective-permute-start(f32[256,256]{1,0:T(8,128)S(1)} %get-tuple-element.57.refs_2_), channel_id=1, source_target_pairs={{0,8},{4,20},{8,0},{12,28},{16,24},{20,4},{24,16},{28,12},{1,9},{5... | collective-permute-start | bytes 786440 | tf_op jit(solution)/shard_map/d0/ppermute | solution.py:307
  14.3 10.7 %collective-permute-start.4 = (f32[256,256]{1,0:T(8,128)S(1)}, f32[256,256]{1,0:T(8,128)S(1)}, u32[]{:S(2)}, u32[]{:S(2)}) collective-permute-start(f32[256,256]{1,0:T(8,128)S(1)} %get-tuple-element.53.refs_0_), channel_id=1, source_target_pairs={{0,3},{1,0},{2,1},{3,2},{4,7},{5,4},{6,5},{7,6},{8,11},{9,8},{10,9... | collective-permute-start | bytes 786440 | tf_op jit(solution)/shard_map/p2/ppermute | solution.py:340
  18.8 13.7 %collective-permute-start.6 = (f32[256,256]{1,0:T(8,128)S(1)}, f32[256,256]{1,0:T(8,128)S(1)}, u32[]{:S(2)}, u32[]{:S(2)}) collective-permute-start(f32[256,256]{1,0:T(8,128)S(1)} %get-tuple-element.56.refs_1_), channel_id=1, source_target_pairs={{0,16},{4,12},{8,24},{12,4},{16,0},{20,28},{24,8},{28,20},{1,17},{... | collective-permute-start | bytes 786440 | tf_op jit(solution)/shard_map/a1/ppermute | solution.py:307
  21.4 11.1 %collective-permute-start.7 = (f32[256,256]{1,0:T(8,128)S(1)}, f32[256,256]{1,0:T(8,128)S(1)}, u32[]{:S(2)}, u32[]{:S(2)}) collective-permute-start(f32[256,256]{1,0:T(8,128)S(1)} %get-tuple-element.56.refs_1_), channel_id=1, source_target_pairs={{0,1},{1,2},{2,3},{3,0},{4,5},{5,6},{6,7},{7,4},{8,9},{9,10},{10,1... | collective-permute-start | bytes 786440 | tf_op jit(solution)/shard_map/p3/ppermute | solution.py:340
  23.3 9.2 %collective-permute-start.8 = (f32[256,256]{1,0:T(8,128)S(1)}, f32[256,256]{1,0:T(8,128)S(1)}, u32[]{:S(2)}, u32[]{:S(2)}) collective-permute-start(f32[256,256]{1,0:T(8,128)S(1)} %get-tuple-element.61.refs_0_), channel_id=1, source_target_pairs={{0,8},{4,12},{8,0},{12,4},{16,24},{20,28},{24,16},{28,20},{1,9},{5... | collective-permute-start | bytes 786440 | tf_op jit(solution)/shard_map/xy/ppermute | solution.py:307
  25.1 9.1 %collective-permute-start.9 = (f32[256,256]{1,0:T(8,128)S(1)}, f32[256,256]{1,0:T(8,128)S(1)}, u32[]{:S(2)}, u32[]{:S(2)}) collective-permute-start(f32[256,256]{1,0:T(8,128)S(1)} %get-tuple-element.64.refs_2_), channel_id=1, source_target_pairs={{0,16},{4,12},{8,24},{12,4},{16,0},{20,28},{24,8},{28,20},{1,17},{... | collective-permute-start | bytes 786440 | tf_op jit(solution)/shard_map/a2/ppermute | solution.py:307
  26.8 11.2 %collective-permute-start.10 = (f32[256,256]{1,0:T(8,128)S(1)}, f32[256,256]{1,0:T(8,128)S(1)}, u32[]{:S(2)}, u32[]{:S(2)}) collective-permute-start(f32[256,256]{1,0:T(8,128)S(1)} %get-tuple-element.58.refs_1_), channel_id=1, source_target_pairs={{0,8},{4,20},{8,0},{12,28},{16,24},{20,4},{24,16},{28,12},{1,9},{5... | collective-permute-start | bytes 786440 | tf_op jit(solution)/shard_map/b1/ppermute | solution.py:307
  32.5 8.3 %collective-permute-start.11 = (f32[256,256]{1,0:T(8,128)S(1)}, f32[256,256]{1,0:T(8,128)S(1)}, u32[]{:S(2)}, u32[]{:S(2)}) collective-permute-start(f32[256,256]{1,0:T(8,128)S(1)} %get-tuple-element.66.refs_2_), channel_id=1, source_target_pairs={{0,16},{4,12},{8,24},{12,4},{16,0},{20,28},{24,8},{28,20},{1,17},{... | collective-permute-start | bytes 786440 | tf_op jit(solution)/shard_map/a3/ppermute | solution.py:307
  32.7 8.1 %collective-permute-start.12 = (f32[256,256]{1,0:T(8,128)S(1)}, f32[256,256]{1,0:T(8,128)S(1)}, u32[]{:S(2)}, u32[]{:S(2)}) collective-permute-start(f32[256,256]{1,0:T(8,128)S(1)} %get-tuple-element.62.refs_3_), channel_id=1, source_target_pairs={{0,8},{4,20},{8,0},{12,28},{16,24},{20,4},{24,16},{28,12},{1,9},{5... | collective-permute-start | bytes 786440 | tf_op jit(solution)/shard_map/d1/ppermute | solution.py:307
  34.3 9.3 %collective-permute-start.14 = (f32[256,256]{1,0:T(8,128)S(1)}, f32[256,256]{1,0:T(8,128)S(1)}, u32[]{:S(2)}, u32[]{:S(2)}) collective-permute-start(f32[256,256]{1,0:T(8,128)S(1)} %get-tuple-element.71.refs_0_), channel_id=1, source_target_pairs={{0,8},{4,20},{8,0},{12,28},{16,24},{20,4},{24,16},{28,12},{1,9},{5... | collective-permute-start | bytes 786440 | tf_op jit(solution)/shard_map/b2/ppermute | solution.py:307
  35.4 9.2 %collective-permute-start.15 = (f32[256,256]{1,0:T(8,128)S(1)}, f32[256,256]{1,0:T(8,128)S(1)}, u32[]{:S(2)}, u32[]{:S(2)}) collective-permute-start(f32[256,256]{1,0:T(8,128)S(1)} %get-tuple-element.68.refs_6_), channel_id=1, source_target_pairs={{0,3},{1,0},{2,1},{3,2},{4,7},{5,4},{6,5},{7,6},{8,11},{9,8},{10,9... | collective-permute-start | bytes 786440 | tf_op jit(solution)/shard_map/d2/ppermute | solution.py:340
  41.1 4.2 %collective-permute-start.13 = (f32[2048,256]{1,0:T(8,128)S(1)}, f32[2048,256]{1,0:T(8,128)S(1)}, u32[]{:S(2)}, u32[]{:S(2)}) collective-permute-start(f32[2048,256]{1,0:T(8,128)S(1)} %shard_map.89.mine), channel_id=1, source_target_pairs={{0,4},{4,0},{8,12},{12,8},{1,5},{5,1},{9,13},{13,9},{2,6},{6,2},{1... | collective-permute-start | bytes 6291464 | tf_op jit(solution)/shard_map/t01/ppermute | solution.py:313
  41.2 14.6 %collective-permute-start.22 = (f32[256,256]{1,0:T(8,128)S(1)}, f32[256,256]{1,0:T(8,128)S(1)}, u32[]{:S(2)}, u32[]{:S(2)}) collective-permute-start(f32[256,256]{1,0:T(8,128)S(1)} %shard_map.96.refs_2_), channel_id=1, source_target_pairs={{0,1},{1,2},{2,3},{3,0},{4,5},{5,6},{6,7},{7,4},{8,9},{9,10},{10,1... | collective-permute-start | bytes 786440 | tf_op jit(solution)/shard_map/l1/ppermute | solution.py:340
  42.4 6.4 %collective-permute-start.17 = (f32[256,256]{1,0:T(8,128)S(1)}, f32[256,256]{1,0:T(8,128)S(1)}, u32[]{:S(2)}, u32[]{:S(2)}) collective-permute-start(f32[256,256]{1,0:T(8,128)S(1)} %get-tuple-element.79.refs_0_), channel_id=1, source_target_pairs={{0,8},{4,20},{8,0},{12,28},{16,24},{20,4},{24,16},{28,12},{1,9},{5... | collective-permute-start | bytes 786440 | tf_op jit(solution)/shard_map/b3/ppermute | solution.py:307
  43.6 8.1 %collective-permute-start.18 = (f32[256,256]{1,0:T(8,128)S(1)}, f32[256,256]{1,0:T(8,128)S(1)}, u32[]{:S(2)}, u32[]{:S(2)}) collective-permute-start(f32[256,256]{1,0:T(8,128)S(1)} %get-tuple-element.80.refs_1_), channel_id=1, source_target_pairs={{0,8},{4,20},{8,0},{12,28},{16,24},{20,4},{24,16},{28,12},{1,9},{5... | collective-permute-start | bytes 786440 | tf_op jit(solution)/shard_map/d3/ppermute | solution.py:307
  45.3 6.4 %collective-permute-start.19 = (f32[512,256]{1,0:T(8,128)S(1)}, f32[512,256]{1,0:T(8,128)S(1)}, u32[]{:S(2)}, u32[]{:S(2)}) collective-permute-start(f32[512,256]{1,0:T(8,128)S(1)} %shard_map.97.refs_13_), channel_id=1, source_target_pairs={{0,4},{4,0},{8,12},{12,8},{1,5},{5,1},{9,13},{13,9},{2,6},{6,2},{1... | collective-permute-start | bytes 1572872 | tf_op jit(solution)/shard_map/tx/ppermute | solution.py:313
  48.9 6.9 %collective-permute-start.20 = (f32[768,256]{1,0:T(8,128)S(1)}, f32[768,256]{1,0:T(8,128)S(1)}, u32[]{:S(2)}, u32[]{:S(2)}) collective-permute-start(f32[768,256]{1,0:T(8,128)S(1)} %shard_map.95.refs_0_), channel_id=1, source_target_pairs={{0,4},{4,0},{8,12},{12,8},{1,5},{5,1},{9,13},{13,9},{2,6},{6,2},{1... | collective-permute-start | bytes 2359304 | tf_op jit(solution)/shard_map/t3/ppermute | solution.py:313
  52.3 13.8 %collective-permute-start.23 = (f32[256,256]{1,0:T(8,128)S(1)}, f32[256,256]{1,0:T(8,128)S(1)}, u32[]{:S(2)}, u32[]{:S(2)}) collective-permute-start(f32[256,256]{1,0:T(8,128)S(1)} %get-tuple-element.94.refs_8_), channel_id=1, source_target_pairs={{0,3},{1,0},{2,1},{3,2},{4,7},{5,4},{6,5},{7,6},{8,11},{9,8},{10,9... | collective-permute-start | bytes 786440 | tf_op jit(solution)/shard_map/l2/ppermute | solution.py:340
  55.8 12.1 %collective-permute-start.24 = (f32[256,256]{1,0:T(8,128)S(1)}, f32[256,256]{1,0:T(8,128)S(1)}, u32[]{:S(2)}, u32[]{:S(2)}) collective-permute-start(f32[256,256]{1,0:T(8,128)S(1)} %get-tuple-element.95.refs_9_), channel_id=1, source_target_pairs={{0,1},{1,2},{2,3},{3,0},{4,5},{5,6},{6,7},{7,4},{8,9},{9,10},{10,1... | collective-permute-start | bytes 786440 | tf_op jit(solution)/shard_map/l3/ppermute | solution.py:340
  70.7 7.8 %collective-permute-start.26 = (f32[256,256]{1,0:T(8,128)S(1)}, f32[256,256]{1,0:T(8,128)S(1)}, u32[]{:S(2)}, u32[]{:S(2)}) collective-permute-start(f32[256,256]{1,0:T(8,128)S(1)} %shard_map.103.own), channel_id=1, source_target_pairs={{0,16},{4,20},{8,24},{12,28},{16,0},{20,4},{24,8},{28,12},{1,17},{... | collective-permute-start | bytes 786440 | tf_op jit(solution)/shard_map/ppermute | solution.py:307
  (6 other events, 19.0 us)

commit v6 on v5

--- a/solution.py
+++ b/solution.py
@@ -209,23 +209,37 @@
         take(lambda here: out[here, :])
 
 
+def part_kernel(grid, count, *refs):
+    blocks = grid.blocks
+    highs, lows, left, (weight, out) = refs[:blocks], refs[blocks : 2 * blocks], refs[2 * blocks : 2 * blocks + count], refs[-2:]
+    cols = grid.shape[1]
+
+    @pl.when(grid.upper())
+    def _():
+        places = [grid.place(j) for j in range(count)]
+        scaled = [split(left[j][...] * weight[pl.ds(places[j], 1), :]) for j in range(count)]
+        for n in range(blocks):
+            total = None
+            for j in range(count):
+                term = dot3(*scaled[j], highs[n][1, span(places[j], cols), :], lows[n][1, span(places[j], cols), :])
+                total = term if total is None else total + term
+            out[:, n * cols : (n + 1) * cols] = total
+
+
 def left_kernel(grid, *refs):
     blocks = grid.blocks
-    highs, lows, left, (weight, _, left_high, left_low) = refs[:blocks], refs[blocks : 2 * blocks], refs[2 * blocks : 3 * blocks], refs[3 * blocks :]
-    rows, cols = grid.shape
-    places = [grid.place(j) for j in range(blocks)]
-    left = [ref.at[pl.ds(ref.shape[0] - rows, rows), :] for ref in left]
+    highs, lows, left, refs = refs[:blocks], refs[blocks : 2 * blocks], refs[2 * blocks : 3 * blocks], refs[3 * blocks :]
+    weight, part, _, left_high, left_low = refs
+    cols = grid.shape[1]
 
     @pl.when(grid.upper())
     def _():
-        scaled = [split(left[j][...] * weight[pl.ds(places[j], 1), :]) for j in range(blocks)]
+        place = grid.place(blocks - 1)
+        scaled = split(left[-1][...] * weight[pl.ds(place, 1), :])
         for n in range(blocks):
-            total = None
-            for j in range(blocks):
-                term = dot3(*scaled[j], highs[n][1, span(places[j], cols), :], lows[n][1, span(places[j], cols), :])
-                total = term if total is None else total + term
             here = pl.ds(n * cols, cols)
-            left_high[:, here], left_low[:, here] = split(total)
+            term = dot3(*scaled, highs[n][1, span(place, cols), :], lows[n][1, span(place, cols), :])
+            left_high[:, here], left_low[:, here] = split(part[:, here] + term)
 
     @pl.when(jnp.logical_not(grid.upper()))
     def _():
@@ -449,10 +463,17 @@
     )
     highs, lows = highs + [high], lows + [low]
     parts = [part] + ([sibling(part)] if cores == 2 else [])
+    first = [values[n] for n in ("l0", "l1", "l2")]
+    partial = call(
+        functools.partial(part_kernel, grid, len(first)),
+        single(rows, order),
+        highs + lows + first + [values["weight"]],
+        flops=6 * rows * order * order,
+    )
     for gate_number in range(ANCHOR + 1, 1 + max(t[1] for t in SLOTS.values())):
-        pass_gate(gate_number, part)
+        pass_gate(gate_number, part, partial)
     left = [values[n] for n in ("l0", "l1", "l2", "l3")]
-    operands = highs + lows + left + [values["weight"]]
+    operands = highs + lows + left + [values["weight"], partial]
     left = call(
         functools.partial(left_kernel, grid),
         [jax.ShapeDtypeStruct((rows, order), jnp.bfloat16)] * 2,

time: 79.6 us -> 79.2 us (level)
  waiting for transfers between devices: 22.9 us -> 20.9 us
  starting transfers between devices: 32.8 us -> 33.8 us
    ppermute x7, waiting for transfers between devices: 2.99 us -> 1.37 us  [along(): lax.ppermute(value, 'col', [(i, (i + shift) % blocks) for i in range(bloc...]
    ppermute x14, starting transfers between devices: 17.3 us -> 18.2 us  [plane(): return lax.ppermute(value, ('layer', 'row'), route)]
    pallas_call x28 -> x29, Pallas kernels: 20.5 us -> 20.9 us  [call(): pl.pallas_call(kernel, out_shape=outs, in_specs=specs, out_specs=jax.tree...]
where the time goes in v6:
time: 79.2 us; the launch traced here: 79 us
  starting transfers between devices  33.8 us (43%)
  Pallas kernels  20.9 us (26%)
  waiting for transfers between devices  20.9 us (26%)
  between operations  1.59 us (2%)
  other arithmetic  1.26 us (2%)
    pallas_call x29, Pallas kernels, call(): pl.pallas_call(kernel, out_shape=outs, in_specs=specs, out_specs=jax.tree...  20.9 us
    ppermute x14, waiting for transfers between devices, plane(): return lax.ppermute(value, ('layer', 'row'), route)  19.1 us
    ppermute x14, starting transfers between devices, plane(): return lax.ppermute(value, ('layer', 'row'), route)  18.2 us
    ppermute x7, starting transfers between devices, along(): lax.ppermute(value, 'col', [(i, (i + shift) % blocks) for i in range(bloc...  14.6 us
  transfers between devices with their start and end apart: 27, of which 13 were waited for; matrix products, arithmetic and copies ran while one was open for 0% of the time, Pallas kernels for 24%

profile of v6, /device:TPU:0, one launch (start us, length us, event | category | flops | bytes accessed | tf_op | source)
XLA Modules:
  0.0 79.0 jit_solution(2620156023123241468)
XLA Ops:
  0.6 1.3 %maximum_select_fusion.refs_0_ = f32[512,256]{1,0:T(8,128)S(1)} fusion(f32[256,256]{1,0:T(8,128)} %bitcast.6, f32[256,256]{1,0:T(8,128)} %bitcast.7, f32[256,256]{1,0:T(8,128)} %bitcast.5, f32[256,256]{1,0:T(8,128)} %bitcast.4, pred[]{:T(512)S(6)} %lt.3), kind=kLoop, calls=%fused_computation | loop fusion | flops 393216 | bytes 1572865 | tf_op jit(solution)/shard_map/jit(_where)/select_n | solution.py:364
  1.9 3.0 %collective-permute-start.1 = (f32[256,256]{1,0:T(8,128)S(1)}, f32[256,256]{1,0:T(8,128)S(1)}, u32[]{:S(2)}, u32[]{:S(2)}) collective-permute-start(f32[256,256]{1,0:T(8,128)S(1)} %shard_map.79.refs_1_), channel_id=1, source_target_pairs={{0,8},{4,20},{8,0},{12,28},{16,24},{20,4},{24,16},{28,12},{1,9},{5... | collective-permute-start | bytes 786440 | tf_op jit(solution)/shard_map/b0/ppermute | solution.py:321
  5.0 1.5 %collective-permute-start = (f32[256,256]{1,0:T(8,128)S(1)}, f32[256,256]{1,0:T(8,128)S(1)}, u32[]{:S(2)}, u32[]{:S(2)}) collective-permute-start(f32[256,256]{1,0:T(8,128)S(1)} %shard_map.79.refs_1_), channel_id=1, source_target_pairs={{0,16},{4,12},{8,24},{12,4},{16,0},{20,28},{24,8},{28,20},{1,17},{... | collective-permute-start | bytes 786440 | tf_op jit(solution)/shard_map/a0/ppermute | solution.py:321
  8.6 1.6 %collective-permute-start.2 = (f32[256,256]{1,0:T(8,128)S(1)}, f32[256,256]{1,0:T(8,128)S(1)}, u32[]{:S(2)}, u32[]{:S(2)}) collective-permute-start(f32[256,256]{1,0:T(8,128)S(1)} %get-tuple-element.52.refs_1_), channel_id=1, source_target_pairs={{0,1},{1,2},{2,3},{3,0},{4,5},{5,6},{6,7},{7,4},{8,9},{9,10},{10,1... | collective-permute-start | bytes 786440 | tf_op jit(solution)/shard_map/p1/ppermute | solution.py:354
  10.2 1.4 %collective-permute-done.1.refs_3_.refs_4_ = f32[256,256]{1,0:T(8,128)S(1)} collective-permute-done((f32[256,256]{1,0:T(8,128)S(1)}, f32[256,256]{1,0:T(8,128)S(1)}, u32[]{:S(2)}, u32[]{:S(2)}) %collective-permute-start.1) | collective-permute-done | bytes 262176 | tf_op jit(solution)/shard_map/b0/ppermute | solution.py:321
  11.6 1.4 %collective-permute-done.refs_2_ = f32[256,256]{1,0:T(8,128)S(1)} collective-permute-done((f32[256,256]{1,0:T(8,128)S(1)}, f32[256,256]{1,0:T(8,128)S(1)}, u32[]{:S(2)}, u32[]{:S(2)}) %collective-permute-start) | collective-permute-done | bytes 262176 | tf_op jit(solution)/shard_map/a0/ppermute | solution.py:321
  13.0 1.3 %collective-permute-start.5 = (f32[256,256]{1,0:T(8,128)S(1)}, f32[256,256]{1,0:T(8,128)S(1)}, u32[]{:S(2)}, u32[]{:S(2)}) collective-permute-start(f32[256,256]{1,0:T(8,128)S(1)} %get-tuple-element.57.refs_2_), channel_id=1, source_target_pairs={{0,8},{4,20},{8,0},{12,28},{16,24},{20,4},{24,16},{28,12},{1,9},{5... | collective-permute-start | bytes 786440 | tf_op jit(solution)/shard_map/d0/ppermute | solution.py:321
  14.3 4.1 %collective-permute-start.4 = (f32[256,256]{1,0:T(8,128)S(1)}, f32[256,256]{1,0:T(8,128)S(1)}, u32[]{:S(2)}, u32[]{:S(2)}) collective-permute-start(f32[256,256]{1,0:T(8,128)S(1)} %get-tuple-element.53.refs_0_), channel_id=1, source_target_pairs={{0,3},{1,0},{2,1},{3,2},{4,7},{5,4},{6,5},{7,6},{8,11},{9,8},{10,9... | collective-permute-start | bytes 786440 | tf_op jit(solution)/shard_map/p2/ppermute | solution.py:354
  18.8 2.5 %collective-permute-start.6 = (f32[256,256]{1,0:T(8,128)S(1)}, f32[256,256]{1,0:T(8,128)S(1)}, u32[]{:S(2)}, u32[]{:S(2)}) collective-permute-start(f32[256,256]{1,0:T(8,128)S(1)} %get-tuple-element.56.refs_1_), channel_id=1, source_target_pairs={{0,16},{4,12},{8,24},{12,4},{16,0},{20,28},{24,8},{28,20},{1,17},{... | collective-permute-start | bytes 786440 | tf_op jit(solution)/shard_map/a1/ppermute | solution.py:321
  21.4 1.6 %collective-permute-start.7 = (f32[256,256]{1,0:T(8,128)S(1)}, f32[256,256]{1,0:T(8,128)S(1)}, u32[]{:S(2)}, u32[]{:S(2)}) collective-permute-start(f32[256,256]{1,0:T(8,128)S(1)} %get-tuple-element.56.refs_1_), channel_id=1, source_target_pairs={{0,1},{1,2},{2,3},{3,0},{4,5},{5,6},{6,7},{7,4},{8,9},{9,10},{10,1... | collective-permute-start | bytes 786440 | tf_op jit(solution)/shard_map/p3/ppermute | solution.py:354
  25.1 1.7 %collective-permute-start.9 = (f32[256,256]{1,0:T(8,128)S(1)}, f32[256,256]{1,0:T(8,128)S(1)}, u32[]{:S(2)}, u32[]{:S(2)}) collective-permute-start(f32[256,256]{1,0:T(8,128)S(1)} %get-tuple-element.64.refs_2_), channel_id=1, source_target_pairs={{0,16},{4,12},{8,24},{12,4},{16,0},{20,28},{24,8},{28,20},{1,17},{... | collective-permute-start | bytes 786440 | tf_op jit(solution)/shard_map/a2/ppermute | solution.py:321
  26.8 1.3 %collective-permute-start.10 = (f32[256,256]{1,0:T(8,128)S(1)}, f32[256,256]{1,0:T(8,128)S(1)}, u32[]{:S(2)}, u32[]{:S(2)}) collective-permute-start(f32[256,256]{1,0:T(8,128)S(1)} %get-tuple-element.58.refs_1_), channel_id=1, source_target_pairs={{0,8},{4,20},{8,0},{12,28},{16,24},{20,4},{24,16},{28,12},{1,9},{5... | collective-permute-start | bytes 786440 | tf_op jit(solution)/shard_map/b1/ppermute | solution.py:321
  28.1 4.4 %collective-permute-done.8.refs_3_.refs_2_ = f32[256,256]{1,0:T(8,128)S(1)} collective-permute-done((f32[256,256]{1,0:T(8,128)S(1)}, f32[256,256]{1,0:T(8,128)S(1)}, u32[]{:S(2)}, u32[]{:S(2)}) %collective-permute-start.8) | collective-permute-done | bytes 262176 | tf_op jit(solution)/shard_map/xy/ppermute | solution.py:321
  32.7 1.2 %collective-permute-start.12 = (f32[256,256]{1,0:T(8,128)S(1)}, f32[256,256]{1,0:T(8,128)S(1)}, u32[]{:S(2)}, u32[]{:S(2)}) collective-permute-start(f32[256,256]{1,0:T(8,128)S(1)} %get-tuple-element.62.refs_3_), channel_id=1, source_target_pairs={{0,8},{4,20},{8,0},{12,28},{16,24},{20,4},{24,16},{28,12},{1,9},{5... | collective-permute-start | bytes 786440 | tf_op jit(solution)/shard_map/d1/ppermute | solution.py:321
  35.4 2.6 %collective-permute-start.15 = (f32[256,256]{1,0:T(8,128)S(1)}, f32[256,256]{1,0:T(8,128)S(1)}, u32[]{:S(2)}, u32[]{:S(2)}) collective-permute-start(f32[256,256]{1,0:T(8,128)S(1)} %get-tuple-element.68.refs_6_), channel_id=1, source_target_pairs={{0,3},{1,0},{2,1},{3,2},{4,7},{5,4},{6,5},{7,6},{8,11},{9,8},{10,9... | collective-permute-start | bytes 786440 | tf_op jit(solution)/shard_map/d2/ppermute | solution.py:354
  38.0 2.9 %collective-permute-done.11.refs_3_ = f32[256,256]{1,0:T(8,128)S(1)} collective-permute-done((f32[256,256]{1,0:T(8,128)S(1)}, f32[256,256]{1,0:T(8,128)S(1)}, u32[]{:S(2)}, u32[]{:S(2)}) %collective-permute-start.11) | collective-permute-done | bytes 262176 | tf_op jit(solution)/shard_map/a3/ppermute | solution.py:321
  41.2 1.2 %collective-permute-start.22 = (f32[256,256]{1,0:T(8,128)S(1)}, f32[256,256]{1,0:T(8,128)S(1)}, u32[]{:S(2)}, u32[]{:S(2)}) collective-permute-start(f32[256,256]{1,0:T(8,128)S(1)} %shard_map.96.refs_2_), channel_id=1, source_target_pairs={{0,1},{1,2},{2,3},{3,0},{4,5},{5,6},{6,7},{7,4},{8,9},{9,10},{10,1... | collective-permute-start | bytes 786440 | tf_op jit(solution)/shard_map/l1/ppermute | solution.py:354
  45.4 2.5 %shard_map.90 = (bf16[2,1024,256]{2,1,0:T(8,128)(2,1)S(1)}, bf16[2,1024,256]{2,1,0:T(8,128)(2,1)S(1)}, bf16[2,1024,256]{2,1,0:T(8,128)(2,1)S(1)}, bf16[2,1024,25...) custom-call(f32[2048,256]{1,0:T(8,128)S(1)} %shard_map.89.mine, ...), custom_call_target="tpu_custom_call" | custom-call | flops 1610612736 | tf_op jit(solution)/shard_map/pallas_call | solution.py:277
  49.0 2.7 %shard_map.93 = (bf16[2,1024,256]{2,1,0:T(8,128)(2,1)S(1)}, bf16[2,1024,256]{2,1,0:T(8,128)(2,1)S(1)}, f32[1024,256]{1,0:T(8,128)S(1)}, f32[1024,256]{1,0:T(8,128)S(1)}, f32[1024,256]{1,0:T(8,128)S(1)}) custom-call(f32[1024,256]{1,0:T(8,128)S(1)} %shard_map.92.mine, ...), custom_call_target="tpu_custom_call", output_to_operand_aliasing={{2}: (6, {}), {3}: (7, {})} | custom-call | flops 2013265920 | tf_op jit(solution)/shard_map/pallas_call | solution.py:277
  52.3 3.5 %collective-permute-start.23 = (f32[256,256]{1,0:T(8,128)S(1)}, f32[256,256]{1,0:T(8,128)S(1)}, u32[]{:S(2)}, u32[]{:S(2)}) collective-permute-start(f32[256,256]{1,0:T(8,128)S(1)} %get-tuple-element.94.refs_8_), channel_id=1, source_target_pairs={{0,3},{1,0},{2,1},{3,2},{4,7},{5,4},{6,5},{7,6},{8,11},{9,8},{10,9... | collective-permute-start | bytes 786440 | tf_op jit(solution)/shard_map/l2/ppermute | solution.py:354
  55.9 10.2 %shard_map.100 = (f32[1024,128]{1,0:T(8,128)S(1)}, bf16[2,1024,256]{2,1,0:T(8,128)(2,1)S(1)}, bf16[2,1024,256]{2,1,0:T(8,128)(2,1)S(1)}) custom-call(f32[768,256]{1,0:T(8,128)S(1)} %shard_map.95.refs_0_, f32[256,256]{1,0:T(8,128)S(1)} %get-tuple-element.85.refs_1_, f32[768,256]{1,0:T(8,128)S(1)} %collective-permute-done.20.refs_3_.refs_2_, ...), custom_call_target="tpu_custom_call" | custom-call | flops 48318382080 | tf_op jit(solution)/shard_map/pallas_call | solution.py:277
  66.2 1.6 %shard_map.101.refs_2_.refs_13_ = f32[256,1024]{1,0:T(8,128)S(1)} custom-call(bf16[2,1024,256]{2,1,0:T(8,128)(2,1)S(1)} %get-tuple-element.69.refs_0_.refs_4_, bf16[2,1024,256]{2,1,0:T(8,128)(2,1)S(1)} %get-tuple-element.70.refs_1_.refs_2_.refs_5_, bf16[2,1024,256]{2,1,0:T(8,128)(2,1)S(1)} %get-tuple-element.78.refs_3_.refs_6_.refs_2_, ...), custom_call_target="tpu_custom_call" | custom-call | flops 1610612736 | tf_op jit(solution)/shard_map/pallas_call | solution.py:277
  69.8 1.5 %collective-permute-start.26 = (f32[256,256]{1,0:T(8,128)S(1)}, f32[256,256]{1,0:T(8,128)S(1)}, u32[]{:S(2)}, u32[]{:S(2)}) collective-permute-start(f32[256,256]{1,0:T(8,128)S(1)} %shard_map.104.own), channel_id=1, source_target_pairs={{0,16},{4,20},{8,24},{12,28},{16,0},{20,4},{24,8},{28,12},{1,17},{... | collective-permute-start | bytes 786440 | tf_op jit(solution)/shard_map/ppermute | solution.py:321
  71.3 6.9 %collective-permute-done.26.across = f32[256,256]{1,0:T(8,128)S(1)} collective-permute-done((f32[256,256]{1,0:T(8,128)S(1)}, f32[256,256]{1,0:T(8,128)S(1)}, u32[]{:S(2)}, u32[]{:S(2)}) %collective-permute-start.26) | collective-permute-done | bytes 262176 | tf_op jit(solution)/shard_map/ppermute | solution.py:321
  (66 shorter events, 13.5 us)
Async XLA Ops:
  1.9 9.7 %collective-permute-start.1 = (f32[256,256]{1,0:T(8,128)S(1)}, f32[256,256]{1,0:T(8,128)S(1)}, u32[]{:S(2)}, u32[]{:S(2)}) collective-permute-start(f32[256,256]{1,0:T(8,128)S(1)} %shard_map.79.refs_1_), channel_id=1, source_target_pairs={{0,8},{4,20},{8,0},{12,28},{16,24},{20,4},{24,16},{28,12},{1,9},{5... | collective-permute-start | bytes 786440 | tf_op jit(solution)/shard_map/b0/ppermute | solution.py:321
  5.0 8.1 %collective-permute-start = (f32[256,256]{1,0:T(8,128)S(1)}, f32[256,256]{1,0:T(8,128)S(1)}, u32[]{:S(2)}, u32[]{:S(2)}) collective-permute-start(f32[256,256]{1,0:T(8,128)S(1)} %shard_map.79.refs_1_), channel_id=1, source_target_pairs={{0,16},{4,12},{8,24},{12,4},{16,0},{20,28},{24,8},{28,20},{1,17},{... | collective-permute-start | bytes 786440 | tf_op jit(solution)/shard_map/a0/ppermute | solution.py:321
  8.0 10.8 %collective-permute-start.3 = (f32[264,256]{1,0:T(8,128)S(1)}, f32[264,256]{1,0:T(8,128)S(1)}, u32[]{:S(2)}, u32[]{:S(2)}) collective-permute-start(f32[264,256]{1,0:T(8,128)S(1)} %shard_map.82.own), channel_id=1, source_target_pairs={{0,16},{4,20},{8,24},{12,28},{16,0},{20,4},{24,8},{28,12},{1,17},{... | collective-permute-start | bytes 811016 | tf_op jit(solution)/shard_map/xx/ppermute | solution.py:321
  8.6 9.8 %collective-permute-start.2 = (f32[256,256]{1,0:T(8,128)S(1)}, f32[256,256]{1,0:T(8,128)S(1)}, u32[]{:S(2)}, u32[]{:S(2)}) collective-permute-start(f32[256,256]{1,0:T(8,128)S(1)} %get-tuple-element.52.refs_1_), channel_id=1, source_target_pairs={{0,1},{1,2},{2,3},{3,0},{4,5},{5,6},{6,7},{7,4},{8,9},{9,10},{10,1... | collective-permute-start | bytes 786440 | tf_op jit(solution)/shard_map/p1/ppermute | solution.py:354
  13.0 11.0 %collective-permute-start.5 = (f32[256,256]{1,0:T(8,128)S(1)}, f32[256,256]{1,0:T(8,128)S(1)}, u32[]{:S(2)}, u32[]{:S(2)}) collective-permute-start(f32[256,256]{1,0:T(8,128)S(1)} %get-tuple-element.57.refs_2_), channel_id=1, source_target_pairs={{0,8},{4,20},{8,0},{12,28},{16,24},{20,4},{24,16},{28,12},{1,9},{5... | collective-permute-start | bytes 786440 | tf_op jit(solution)/shard_map/d0/ppermute | solution.py:321
  14.3 10.7 %collective-permute-start.4 = (f32[256,256]{1,0:T(8,128)S(1)}, f32[256,256]{1,0:T(8,128)S(1)}, u32[]{:S(2)}, u32[]{:S(2)}) collective-permute-start(f32[256,256]{1,0:T(8,128)S(1)} %get-tuple-element.53.refs_0_), channel_id=1, source_target_pairs={{0,3},{1,0},{2,1},{3,2},{4,7},{5,4},{6,5},{7,6},{8,11},{9,8},{10,9... | collective-permute-start | bytes 786440 | tf_op jit(solution)/shard_map/p2/ppermute | solution.py:354
  18.8 13.7 %collective-permute-start.6 = (f32[256,256]{1,0:T(8,128)S(1)}, f32[256,256]{1,0:T(8,128)S(1)}, u32[]{:S(2)}, u32[]{:S(2)}) collective-permute-start(f32[256,256]{1,0:T(8,128)S(1)} %get-tuple-element.56.refs_1_), channel_id=1, source_target_pairs={{0,16},{4,12},{8,24},{12,4},{16,0},{20,28},{24,8},{28,20},{1,17},{... | collective-permute-start | bytes 786440 | tf_op jit(solution)/shard_map/a1/ppermute | solution.py:321
  21.4 11.1 %collective-permute-start.7 = (f32[256,256]{1,0:T(8,128)S(1)}, f32[256,256]{1,0:T(8,128)S(1)}, u32[]{:S(2)}, u32[]{:S(2)}) collective-permute-start(f32[256,256]{1,0:T(8,128)S(1)} %get-tuple-element.56.refs_1_), channel_id=1, source_target_pairs={{0,1},{1,2},{2,3},{3,0},{4,5},{5,6},{6,7},{7,4},{8,9},{9,10},{10,1... | collective-permute-start | bytes 786440 | tf_op jit(solution)/shard_map/p3/ppermute | solution.py:354
  23.3 9.2 %collective-permute-start.8 = (f32[256,256]{1,0:T(8,128)S(1)}, f32[256,256]{1,0:T(8,128)S(1)}, u32[]{:S(2)}, u32[]{:S(2)}) collective-permute-start(f32[256,256]{1,0:T(8,128)S(1)} %get-tuple-element.61.refs_0_), channel_id=1, source_target_pairs={{0,8},{4,12},{8,0},{12,4},{16,24},{20,28},{24,16},{28,20},{1,9},{5... | collective-permute-start | bytes 786440 | tf_op jit(solution)/shard_map/xy/ppermute | solution.py:321
  25.1 9.1 %collective-permute-start.9 = (f32[256,256]{1,0:T(8,128)S(1)}, f32[256,256]{1,0:T(8,128)S(1)}, u32[]{:S(2)}, u32[]{:S(2)}) collective-permute-start(f32[256,256]{1,0:T(8,128)S(1)} %get-tuple-element.64.refs_2_), channel_id=1, source_target_pairs={{0,16},{4,12},{8,24},{12,4},{16,0},{20,28},{24,8},{28,20},{1,17},{... | collective-permute-start | bytes 786440 | tf_op jit(solution)/shard_map/a2/ppermute | solution.py:321
  26.8 11.2 %collective-permute-start.10 = (f32[256,256]{1,0:T(8,128)S(1)}, f32[256,256]{1,0:T(8,128)S(1)}, u32[]{:S(2)}, u32[]{:S(2)}) collective-permute-start(f32[256,256]{1,0:T(8,128)S(1)} %get-tuple-element.58.refs_1_), channel_id=1, source_target_pairs={{0,8},{4,20},{8,0},{12,28},{16,24},{20,4},{24,16},{28,12},{1,9},{5... | collective-permute-start | bytes 786440 | tf_op jit(solution)/shard_map/b1/ppermute | solution.py:321
  32.5 8.3 %collective-permute-start.11 = (f32[256,256]{1,0:T(8,128)S(1)}, f32[256,256]{1,0:T(8,128)S(1)}, u32[]{:S(2)}, u32[]{:S(2)}) collective-permute-start(f32[256,256]{1,0:T(8,128)S(1)} %get-tuple-element.66.refs_2_), channel_id=1, source_target_pairs={{0,16},{4,12},{8,24},{12,4},{16,0},{20,28},{24,8},{28,20},{1,17},{... | collective-permute-start | bytes 786440 | tf_op jit(solution)/shard_map/a3/ppermute | solution.py:321
  32.7 8.1 %collective-permute-start.12 = (f32[256,256]{1,0:T(8,128)S(1)}, f32[256,256]{1,0:T(8,128)S(1)}, u32[]{:S(2)}, u32[]{:S(2)}) collective-permute-start(f32[256,256]{1,0:T(8,128)S(1)} %get-tuple-element.62.refs_3_), channel_id=1, source_target_pairs={{0,8},{4,20},{8,0},{12,28},{16,24},{20,4},{24,16},{28,12},{1,9},{5... | collective-permute-start | bytes 786440 | tf_op jit(solution)/shard_map/d1/ppermute | solution.py:321
  34.3 9.3 %collective-permute-start.14 = (f32[256,256]{1,0:T(8,128)S(1)}, f32[256,256]{1,0:T(8,128)S(1)}, u32[]{:S(2)}, u32[]{:S(2)}) collective-permute-start(f32[256,256]{1,0:T(8,128)S(1)} %get-tuple-element.71.refs_0_), channel_id=1, source_target_pairs={{0,8},{4,20},{8,0},{12,28},{16,24},{20,4},{24,16},{28,12},{1,9},{5... | collective-permute-start | bytes 786440 | tf_op jit(solution)/shard_map/b2/ppermute | solution.py:321
  35.4 9.2 %collective-permute-start.15 = (f32[256,256]{1,0:T(8,128)S(1)}, f32[256,256]{1,0:T(8,128)S(1)}, u32[]{:S(2)}, u32[]{:S(2)}) collective-permute-start(f32[256,256]{1,0:T(8,128)S(1)} %get-tuple-element.68.refs_6_), channel_id=1, source_target_pairs={{0,3},{1,0},{2,1},{3,2},{4,7},{5,4},{6,5},{7,6},{8,11},{9,8},{10,9... | collective-permute-start | bytes 786440 | tf_op jit(solution)/shard_map/d2/ppermute | solution.py:354
  41.1 4.2 %collective-permute-start.13 = (f32[2048,256]{1,0:T(8,128)S(1)}, f32[2048,256]{1,0:T(8,128)S(1)}, u32[]{:S(2)}, u32[]{:S(2)}) collective-permute-start(f32[2048,256]{1,0:T(8,128)S(1)} %shard_map.89.mine), channel_id=1, source_target_pairs={{0,4},{4,0},{8,12},{12,8},{1,5},{5,1},{9,13},{13,9},{2,6},{6,2},{1... | collective-permute-start | bytes 6291464 | tf_op jit(solution)/shard_map/t01/ppermute | solution.py:327
  41.2 14.6 %collective-permute-start.22 = (f32[256,256]{1,0:T(8,128)S(1)}, f32[256,256]{1,0:T(8,128)S(1)}, u32[]{:S(2)}, u32[]{:S(2)}) collective-permute-start(f32[256,256]{1,0:T(8,128)S(1)} %shard_map.96.refs_2_), channel_id=1, source_target_pairs={{0,1},{1,2},{2,3},{3,0},{4,5},{5,6},{6,7},{7,4},{8,9},{9,10},{10,1... | collective-permute-start | bytes 786440 | tf_op jit(solution)/shard_map/l1/ppermute | solution.py:354
  42.4 6.4 %collective-permute-start.17 = (f32[256,256]{1,0:T(8,128)S(1)}, f32[256,256]{1,0:T(8,128)S(1)}, u32[]{:S(2)}, u32[]{:S(2)}) collective-permute-start(f32[256,256]{1,0:T(8,128)S(1)} %get-tuple-element.79.refs_0_), channel_id=1, source_target_pairs={{0,8},{4,20},{8,0},{12,28},{16,24},{20,4},{24,16},{28,12},{1,9},{5... | collective-permute-start | bytes 786440 | tf_op jit(solution)/shard_map/b3/ppermute | solution.py:321
  43.6 8.1 %collective-permute-start.18 = (f32[256,256]{1,0:T(8,128)S(1)}, f32[256,256]{1,0:T(8,128)S(1)}, u32[]{:S(2)}, u32[]{:S(2)}) collective-permute-start(f32[256,256]{1,0:T(8,128)S(1)} %get-tuple-element.80.refs_1_), channel_id=1, source_target_pairs={{0,8},{4,20},{8,0},{12,28},{16,24},{20,4},{24,16},{28,12},{1,9},{5... | collective-permute-start | bytes 786440 | tf_op jit(solution)/shard_map/d3/ppermute | solution.py:321
  45.3 6.4 %collective-permute-start.19 = (f32[512,256]{1,0:T(8,128)S(1)}, f32[512,256]{1,0:T(8,128)S(1)}, u32[]{:S(2)}, u32[]{:S(2)}) collective-permute-start(f32[512,256]{1,0:T(8,128)S(1)} %shard_map.97.refs_13_), channel_id=1, source_target_pairs={{0,4},{4,0},{8,12},{12,8},{1,5},{5,1},{9,13},{13,9},{2,6},{6,2},{1... | collective-permute-start | bytes 1572872 | tf_op jit(solution)/shard_map/tx/ppermute | solution.py:327
  48.9 6.9 %collective-permute-start.20 = (f32[768,256]{1,0:T(8,128)S(1)}, f32[768,256]{1,0:T(8,128)S(1)}, u32[]{:S(2)}, u32[]{:S(2)}) collective-permute-start(f32[768,256]{1,0:T(8,128)S(1)} %shard_map.95.refs_0_), channel_id=1, source_target_pairs={{0,4},{4,0},{8,12},{12,8},{1,5},{5,1},{9,13},{13,9},{2,6},{6,2},{1... | collective-permute-start | bytes 2359304 | tf_op jit(solution)/shard_map/t3/ppermute | solution.py:327
  52.3 13.9 %collective-permute-start.23 = (f32[256,256]{1,0:T(8,128)S(1)}, f32[256,256]{1,0:T(8,128)S(1)}, u32[]{:S(2)}, u32[]{:S(2)}) collective-permute-start(f32[256,256]{1,0:T(8,128)S(1)} %get-tuple-element.94.refs_8_), channel_id=1, source_target_pairs={{0,3},{1,0},{2,1},{3,2},{4,7},{5,4},{6,5},{7,6},{8,11},{9,8},{10,9... | collective-permute-start | bytes 786440 | tf_op jit(solution)/shard_map/l2/ppermute | solution.py:354
  55.8 12.1 %collective-permute-start.24 = (f32[256,256]{1,0:T(8,128)S(1)}, f32[256,256]{1,0:T(8,128)S(1)}, u32[]{:S(2)}, u32[]{:S(2)}) collective-permute-start(f32[256,256]{1,0:T(8,128)S(1)} %get-tuple-element.95.refs_9_), channel_id=1, source_target_pairs={{0,1},{1,2},{2,3},{3,0},{4,5},{5,6},{6,7},{7,4},{8,9},{9,10},{10,1... | collective-permute-start | bytes 786440 | tf_op jit(solution)/shard_map/l3/ppermute | solution.py:354
  69.8 8.4 %collective-permute-start.26 = (f32[256,256]{1,0:T(8,128)S(1)}, f32[256,256]{1,0:T(8,128)S(1)}, u32[]{:S(2)}, u32[]{:S(2)}) collective-permute-start(f32[256,256]{1,0:T(8,128)S(1)} %shard_map.104.own), channel_id=1, source_target_pairs={{0,16},{4,20},{8,24},{12,28},{16,0},{20,4},{24,8},{28,12},{1,17},{... | collective-permute-start | bytes 786440 | tf_op jit(solution)/shard_map/ppermute | solution.py:321
  (6 other events, 16.8 us)

commit v7 on v6

--- a/solution.py
+++ b/solution.py
@@ -32,12 +32,12 @@
     "d3": (7, 10),
     "t2": (8, 10),
     "td": (10, 11),
-    "l1": (9, 11),
+    "l1": (8, 10),
     "t3": (9, 11),
     "tx": (8, 10),
     "a2": (4, 6),
     "l2": (10, 12),
-    "l3": (11, 12),
+    "l3": (10, 12),
 }
 KERNELS = {'01': 9, '2': 10}
 DIAGONAL = {'d1': 'p', 'd2': 'z', 'd3': 'p'}

time: 79.2 us -> 79.2 us (level)
  no operation moved by 1% of the time
where the time goes in v7:
time: 79.2 us; the launch traced here: 79 us
  starting transfers between devices  33.7 us (43%)
  waiting for transfers between devices  21 us (27%)
  Pallas kernels  20.9 us (26%)
  between operations  1.57 us (2%)
  other arithmetic  1.26 us (2%)
    pallas_call x29, Pallas kernels, call(): pl.pallas_call(kernel, out_shape=outs, in_specs=specs, out_specs=jax.tree...  20.9 us
    ppermute x14, waiting for transfers between devices, plane(): return lax.ppermute(value, ('layer', 'row'), route)  19 us
    ppermute x14, starting transfers between devices, plane(): return lax.ppermute(value, ('layer', 'row'), route)  18.2 us
    ppermute x7, starting transfers between devices, along(): lax.ppermute(value, 'col', [(i, (i + shift) % blocks) for i in range(bloc...  14.5 us
  transfers between devices with their start and end apart: 27, of which 13 were waited for; matrix products, arithmetic and copies ran while one was open for 0% of the time, Pallas kernels for 24%

profile of v7, /device:TPU:0, one launch (start us, length us, event | category | flops | bytes accessed | tf_op | source)
XLA Modules:
  0.0 79.0 jit_solution(5283231220358166490)
XLA Ops:
  0.6 1.3 %maximum_select_fusion.refs_0_ = f32[512,256]{1,0:T(8,128)S(1)} fusion(f32[256,256]{1,0:T(8,128)} %bitcast.6, f32[256,256]{1,0:T(8,128)} %bitcast.7, f32[256,256]{1,0:T(8,128)} %bitcast.5, f32[256,256]{1,0:T(8,128)} %bitcast.4, pred[]{:T(512)S(6)} %lt.3), kind=kLoop, calls=%fused_computation | loop fusion | flops 393216 | bytes 1572865 | tf_op jit(solution)/shard_map/jit(_where)/select_n | solution.py:364
  1.9 3.0 %collective-permute-start.1 = (f32[256,256]{1,0:T(8,128)S(1)}, f32[256,256]{1,0:T(8,128)S(1)}, u32[]{:S(2)}, u32[]{:S(2)}) collective-permute-start(f32[256,256]{1,0:T(8,128)S(1)} %shard_map.79.refs_1_), channel_id=1, source_target_pairs={{0,8},{4,20},{8,0},{12,28},{16,24},{20,4},{24,16},{28,12},{1,9},{5... | collective-permute-start | bytes 786440 | tf_op jit(solution)/shard_map/b0/ppermute | solution.py:321
  5.0 1.5 %collective-permute-start = (f32[256,256]{1,0:T(8,128)S(1)}, f32[256,256]{1,0:T(8,128)S(1)}, u32[]{:S(2)}, u32[]{:S(2)}) collective-permute-start(f32[256,256]{1,0:T(8,128)S(1)} %shard_map.79.refs_1_), channel_id=1, source_target_pairs={{0,16},{4,12},{8,24},{12,4},{16,0},{20,28},{24,8},{28,20},{1,17},{... | collective-permute-start | bytes 786440 | tf_op jit(solution)/shard_map/a0/ppermute | solution.py:321
  8.6 1.6 %collective-permute-start.2 = (f32[256,256]{1,0:T(8,128)S(1)}, f32[256,256]{1,0:T(8,128)S(1)}, u32[]{:S(2)}, u32[]{:S(2)}) collective-permute-start(f32[256,256]{1,0:T(8,128)S(1)} %get-tuple-element.51.refs_1_), channel_id=1, source_target_pairs={{0,1},{1,2},{2,3},{3,0},{4,5},{5,6},{6,7},{7,4},{8,9},{9,10},{10,1... | collective-permute-start | bytes 786440 | tf_op jit(solution)/shard_map/p1/ppermute | solution.py:354
  10.2 1.4 %collective-permute-done.1.refs_3_.refs_4_ = f32[256,256]{1,0:T(8,128)S(1)} collective-permute-done((f32[256,256]{1,0:T(8,128)S(1)}, f32[256,256]{1,0:T(8,128)S(1)}, u32[]{:S(2)}, u32[]{:S(2)}) %collective-permute-start.1) | collective-permute-done | bytes 262176 | tf_op jit(solution)/shard_map/b0/ppermute | solution.py:321
  11.6 1.4 %collective-permute-done.refs_2_ = f32[256,256]{1,0:T(8,128)S(1)} collective-permute-done((f32[256,256]{1,0:T(8,128)S(1)}, f32[256,256]{1,0:T(8,128)S(1)}, u32[]{:S(2)}, u32[]{:S(2)}) %collective-permute-start) | collective-permute-done | bytes 262176 | tf_op jit(solution)/shard_map/a0/ppermute | solution.py:321
  13.0 1.3 %collective-permute-start.5 = (f32[256,256]{1,0:T(8,128)S(1)}, f32[256,256]{1,0:T(8,128)S(1)}, u32[]{:S(2)}, u32[]{:S(2)}) collective-permute-start(f32[256,256]{1,0:T(8,128)S(1)} %get-tuple-element.56.refs_2_), channel_id=1, source_target_pairs={{0,8},{4,20},{8,0},{12,28},{16,24},{20,4},{24,16},{28,12},{1,9},{5... | collective-permute-start | bytes 786440 | tf_op jit(solution)/shard_map/d0/ppermute | solution.py:321
  14.3 4.1 %collective-permute-start.4 = (f32[256,256]{1,0:T(8,128)S(1)}, f32[256,256]{1,0:T(8,128)S(1)}, u32[]{:S(2)}, u32[]{:S(2)}) collective-permute-start(f32[256,256]{1,0:T(8,128)S(1)} %get-tuple-element.52.refs_0_), channel_id=1, source_target_pairs={{0,3},{1,0},{2,1},{3,2},{4,7},{5,4},{6,5},{7,6},{8,11},{9,8},{10,9... | collective-permute-start | bytes 786440 | tf_op jit(solution)/shard_map/p2/ppermute | solution.py:354
  18.8 2.5 %collective-permute-start.6 = (f32[256,256]{1,0:T(8,128)S(1)}, f32[256,256]{1,0:T(8,128)S(1)}, u32[]{:S(2)}, u32[]{:S(2)}) collective-permute-start(f32[256,256]{1,0:T(8,128)S(1)} %get-tuple-element.55.refs_1_), channel_id=1, source_target_pairs={{0,16},{4,12},{8,24},{12,4},{16,0},{20,28},{24,8},{28,20},{1,17},{... | collective-permute-start | bytes 786440 | tf_op jit(solution)/shard_map/a1/ppermute | solution.py:321
  21.4 1.6 %collective-permute-start.7 = (f32[256,256]{1,0:T(8,128)S(1)}, f32[256,256]{1,0:T(8,128)S(1)}, u32[]{:S(2)}, u32[]{:S(2)}) collective-permute-start(f32[256,256]{1,0:T(8,128)S(1)} %get-tuple-element.55.refs_1_), channel_id=1, source_target_pairs={{0,1},{1,2},{2,3},{3,0},{4,5},{5,6},{6,7},{7,4},{8,9},{9,10},{10,1... | collective-permute-start | bytes 786440 | tf_op jit(solution)/shard_map/p3/ppermute | solution.py:354
  25.1 1.7 %collective-permute-start.9 = (f32[256,256]{1,0:T(8,128)S(1)}, f32[256,256]{1,0:T(8,128)S(1)}, u32[]{:S(2)}, u32[]{:S(2)}) collective-permute-start(f32[256,256]{1,0:T(8,128)S(1)} %get-tuple-element.63.refs_2_), channel_id=1, source_target_pairs={{0,16},{4,12},{8,24},{12,4},{16,0},{20,28},{24,8},{28,20},{1,17},{... | collective-permute-start | bytes 786440 | tf_op jit(solution)/shard_map/a2/ppermute | solution.py:321
  26.8 1.3 %collective-permute-start.10 = (f32[256,256]{1,0:T(8,128)S(1)}, f32[256,256]{1,0:T(8,128)S(1)}, u32[]{:S(2)}, u32[]{:S(2)}) collective-permute-start(f32[256,256]{1,0:T(8,128)S(1)} %get-tuple-element.57.refs_1_), channel_id=1, source_target_pairs={{0,8},{4,20},{8,0},{12,28},{16,24},{20,4},{24,16},{28,12},{1,9},{5... | collective-permute-start | bytes 786440 | tf_op jit(solution)/shard_map/b1/ppermute | solution.py:321
  28.1 4.4 %collective-permute-done.8.refs_3_.refs_2_ = f32[256,256]{1,0:T(8,128)S(1)} collective-permute-done((f32[256,256]{1,0:T(8,128)S(1)}, f32[256,256]{1,0:T(8,128)S(1)}, u32[]{:S(2)}, u32[]{:S(2)}) %collective-permute-start.8) | collective-permute-done | bytes 262176 | tf_op jit(solution)/shard_map/xy/ppermute | solution.py:321
  32.7 1.2 %collective-permute-start.12 = (f32[256,256]{1,0:T(8,128)S(1)}, f32[256,256]{1,0:T(8,128)S(1)}, u32[]{:S(2)}, u32[]{:S(2)}) collective-permute-start(f32[256,256]{1,0:T(8,128)S(1)} %get-tuple-element.61.refs_3_), channel_id=1, source_target_pairs={{0,8},{4,20},{8,0},{12,28},{16,24},{20,4},{24,16},{28,12},{1,9},{5... | collective-permute-start | bytes 786440 | tf_op jit(solution)/shard_map/d1/ppermute | solution.py:321
  35.4 2.6 %collective-permute-start.15 = (f32[256,256]{1,0:T(8,128)S(1)}, f32[256,256]{1,0:T(8,128)S(1)}, u32[]{:S(2)}, u32[]{:S(2)}) collective-permute-start(f32[256,256]{1,0:T(8,128)S(1)} %get-tuple-element.67.refs_6_), channel_id=1, source_target_pairs={{0,3},{1,0},{2,1},{3,2},{4,7},{5,4},{6,5},{7,6},{8,11},{9,8},{10,9... | collective-permute-start | bytes 786440 | tf_op jit(solution)/shard_map/d2/ppermute | solution.py:354
  38.0 2.9 %collective-permute-done.11.refs_3_ = f32[256,256]{1,0:T(8,128)S(1)} collective-permute-done((f32[256,256]{1,0:T(8,128)S(1)}, f32[256,256]{1,0:T(8,128)S(1)}, u32[]{:S(2)}, u32[]{:S(2)}) %collective-permute-start.11) | collective-permute-done | bytes 262176 | tf_op jit(solution)/shard_map/a3/ppermute | solution.py:321
  41.2 1.2 %collective-permute-start.19 = (f32[256,256]{1,0:T(8,128)S(1)}, f32[256,256]{1,0:T(8,128)S(1)}, u32[]{:S(2)}, u32[]{:S(2)}) collective-permute-start(f32[256,256]{1,0:T(8,128)S(1)} %shard_map.96.refs_2_), channel_id=1, source_target_pairs={{0,1},{1,2},{2,3},{3,0},{4,5},{5,6},{6,7},{7,4},{8,9},{9,10},{10,1... | collective-permute-start | bytes 786440 | tf_op jit(solution)/shard_map/l1/ppermute | solution.py:354
  45.4 2.6 %shard_map.90 = (bf16[2,1024,256]{2,1,0:T(8,128)(2,1)S(1)}, bf16[2,1024,256]{2,1,0:T(8,128)(2,1)S(1)}, bf16[2,1024,256]{2,1,0:T(8,128)(2,1)S(1)}, bf16[2,1024,25...) custom-call(f32[2048,256]{1,0:T(8,128)S(1)} %shard_map.89.mine, ...), custom_call_target="tpu_custom_call" | custom-call | flops 1610612736 | tf_op jit(solution)/shard_map/pallas_call | solution.py:277
  49.0 2.7 %shard_map.93 = (bf16[2,1024,256]{2,1,0:T(8,128)(2,1)S(1)}, bf16[2,1024,256]{2,1,0:T(8,128)(2,1)S(1)}, f32[1024,256]{1,0:T(8,128)S(1)}, f32[1024,256]{1,0:T(8,128)S(1)}, f32[1024,256]{1,0:T(8,128)S(1)}) custom-call(f32[1024,256]{1,0:T(8,128)S(1)} %shard_map.92.mine, ...), custom_call_target="tpu_custom_call", output_to_operand_aliasing={{2}: (6, {}), {3}: (7, {})} | custom-call | flops 2013265920 | tf_op jit(solution)/shard_map/pallas_call | solution.py:277
  52.3 3.5 %collective-permute-start.23 = (f32[256,256]{1,0:T(8,128)S(1)}, f32[256,256]{1,0:T(8,128)S(1)}, u32[]{:S(2)}, u32[]{:S(2)}) collective-permute-start(f32[256,256]{1,0:T(8,128)S(1)} %get-tuple-element.92.refs_8_), channel_id=1, source_target_pairs={{0,3},{1,0},{2,1},{3,2},{4,7},{5,4},{6,5},{7,6},{8,11},{9,8},{10,9... | collective-permute-start | bytes 786440 | tf_op jit(solution)/shard_map/l2/ppermute | solution.py:354
  55.8 10.2 %shard_map.100 = (f32[1024,128]{1,0:T(8,128)S(1)}, bf16[2,1024,256]{2,1,0:T(8,128)(2,1)S(1)}, bf16[2,1024,256]{2,1,0:T(8,128)(2,1)S(1)}) custom-call(f32[768,256]{1,0:T(8,128)S(1)} %shard_map.95.refs_0_, f32[256,256]{1,0:T(8,128)S(1)} %get-tuple-element.84.refs_1_, f32[768,256]{1,0:T(8,128)S(1)} %collective-permute-done.21.refs_2_, ...), custom_call_target="tpu_custom_call" | custom-call | flops 48318382080 | tf_op jit(solution)/shard_map/pallas_call | solution.py:277
  66.1 1.6 %shard_map.101.refs_2_.refs_13_ = f32[256,1024]{1,0:T(8,128)S(1)} custom-call(bf16[2,1024,256]{2,1,0:T(8,128)(2,1)S(1)} %get-tuple-element.68.refs_0_.refs_4_, bf16[2,1024,256]{2,1,0:T(8,128)(2,1)S(1)} %get-tuple-element.69.refs_1_.refs_2_.refs_5_, bf16[2,1024,256]{2,1,0:T(8,128)(2,1)S(1)} %get-tuple-element.77.refs_4_.refs_6_.refs_2_, ...), custom_call_target="tpu_custom_call" | custom-call | flops 1610612736 | tf_op jit(solution)/shard_map/pallas_call | solution.py:277
  69.8 1.5 %collective-permute-start.26 = (f32[256,256]{1,0:T(8,128)S(1)}, f32[256,256]{1,0:T(8,128)S(1)}, u32[]{:S(2)}, u32[]{:S(2)}) collective-permute-start(f32[256,256]{1,0:T(8,128)S(1)} %shard_map.104.own), channel_id=1, source_target_pairs={{0,16},{4,20},{8,24},{12,28},{16,0},{20,4},{24,8},{28,12},{1,17},{... | collective-permute-start | bytes 786440 | tf_op jit(solution)/shard_map/ppermute | solution.py:321
  71.3 6.8 %collective-permute-done.26.across = f32[256,256]{1,0:T(8,128)S(1)} collective-permute-done((f32[256,256]{1,0:T(8,128)S(1)}, f32[256,256]{1,0:T(8,128)S(1)}, u32[]{:S(2)}, u32[]{:S(2)}) %collective-permute-start.26) | collective-permute-done | bytes 262176 | tf_op jit(solution)/shard_map/ppermute | solution.py:321
  (66 shorter events, 13.6 us)
Async XLA Ops:
  1.9 9.7 %collective-permute-start.1 = (f32[256,256]{1,0:T(8,128)S(1)}, f32[256,256]{1,0:T(8,128)S(1)}, u32[]{:S(2)}, u32[]{:S(2)}) collective-permute-start(f32[256,256]{1,0:T(8,128)S(1)} %shard_map.79.refs_1_), channel_id=1, source_target_pairs={{0,8},{4,20},{8,0},{12,28},{16,24},{20,4},{24,16},{28,12},{1,9},{5... | collective-permute-start | bytes 786440 | tf_op jit(solution)/shard_map/b0/ppermute | solution.py:321
  5.0 8.1 %collective-permute-start = (f32[256,256]{1,0:T(8,128)S(1)}, f32[256,256]{1,0:T(8,128)S(1)}, u32[]{:S(2)}, u32[]{:S(2)}) collective-permute-start(f32[256,256]{1,0:T(8,128)S(1)} %shard_map.79.refs_1_), channel_id=1, source_target_pairs={{0,16},{4,12},{8,24},{12,4},{16,0},{20,28},{24,8},{28,20},{1,17},{... | collective-permute-start | bytes 786440 | tf_op jit(solution)/shard_map/a0/ppermute | solution.py:321
  8.0 10.8 %collective-permute-start.3 = (f32[264,256]{1,0:T(8,128)S(1)}, f32[264,256]{1,0:T(8,128)S(1)}, u32[]{:S(2)}, u32[]{:S(2)}) collective-permute-start(f32[264,256]{1,0:T(8,128)S(1)} %shard_map.82.own), channel_id=1, source_target_pairs={{0,16},{4,20},{8,24},{12,28},{16,0},{20,4},{24,8},{28,12},{1,17},{... | collective-permute-start | bytes 811016 | tf_op jit(solution)/shard_map/xx/ppermute | solution.py:321
  8.6 9.8 %collective-permute-start.2 = (f32[256,256]{1,0:T(8,128)S(1)}, f32[256,256]{1,0:T(8,128)S(1)}, u32[]{:S(2)}, u32[]{:S(2)}) collective-permute-start(f32[256,256]{1,0:T(8,128)S(1)} %get-tuple-element.51.refs_1_), channel_id=1, source_target_pairs={{0,1},{1,2},{2,3},{3,0},{4,5},{5,6},{6,7},{7,4},{8,9},{9,10},{10,1... | collective-permute-start | bytes 786440 | tf_op jit(solution)/shard_map/p1/ppermute | solution.py:354
  13.0 11.0 %collective-permute-start.5 = (f32[256,256]{1,0:T(8,128)S(1)}, f32[256,256]{1,0:T(8,128)S(1)}, u32[]{:S(2)}, u32[]{:S(2)}) collective-permute-start(f32[256,256]{1,0:T(8,128)S(1)} %get-tuple-element.56.refs_2_), channel_id=1, source_target_pairs={{0,8},{4,20},{8,0},{12,28},{16,24},{20,4},{24,16},{28,12},{1,9},{5... | collective-permute-start | bytes 786440 | tf_op jit(solution)/shard_map/d0/ppermute | solution.py:321
  14.3 10.7 %collective-permute-start.4 = (f32[256,256]{1,0:T(8,128)S(1)}, f32[256,256]{1,0:T(8,128)S(1)}, u32[]{:S(2)}, u32[]{:S(2)}) collective-permute-start(f32[256,256]{1,0:T(8,128)S(1)} %get-tuple-element.52.refs_0_), channel_id=1, source_target_pairs={{0,3},{1,0},{2,1},{3,2},{4,7},{5,4},{6,5},{7,6},{8,11},{9,8},{10,9... | collective-permute-start | bytes 786440 | tf_op jit(solution)/shard_map/p2/ppermute | solution.py:354
  18.8 13.7 %collective-permute-start.6 = (f32[256,256]{1,0:T(8,128)S(1)}, f32[256,256]{1,0:T(8,128)S(1)}, u32[]{:S(2)}, u32[]{:S(2)}) collective-permute-start(f32[256,256]{1,0:T(8,128)S(1)} %get-tuple-element.55.refs_1_), channel_id=1, source_target_pairs={{0,16},{4,12},{8,24},{12,4},{16,0},{20,28},{24,8},{28,20},{1,17},{... | collective-permute-start | bytes 786440 | tf_op jit(solution)/shard_map/a1/ppermute | solution.py:321
  21.4 11.1 %collective-permute-start.7 = (f32[256,256]{1,0:T(8,128)S(1)}, f32[256,256]{1,0:T(8,128)S(1)}, u32[]{:S(2)}, u32[]{:S(2)}) collective-permute-start(f32[256,256]{1,0:T(8,128)S(1)} %get-tuple-element.55.refs_1_), channel_id=1, source_target_pairs={{0,1},{1,2},{2,3},{3,0},{4,5},{5,6},{6,7},{7,4},{8,9},{9,10},{10,1... | collective-permute-start | bytes 786440 | tf_op jit(solution)/shard_map/p3/ppermute | solution.py:354
  23.3 9.2 %collective-permute-start.8 = (f32[256,256]{1,0:T(8,128)S(1)}, f32[256,256]{1,0:T(8,128)S(1)}, u32[]{:S(2)}, u32[]{:S(2)}) collective-permute-start(f32[256,256]{1,0:T(8,128)S(1)} %get-tuple-element.60.refs_0_), channel_id=1, source_target_pairs={{0,8},{4,12},{8,0},{12,4},{16,24},{20,28},{24,16},{28,20},{1,9},{5... | collective-permute-start | bytes 786440 | tf_op jit(solution)/shard_map/xy/ppermute | solution.py:321
  25.1 9.1 %collective-permute-start.9 = (f32[256,256]{1,0:T(8,128)S(1)}, f32[256,256]{1,0:T(8,128)S(1)}, u32[]{:S(2)}, u32[]{:S(2)}) collective-permute-start(f32[256,256]{1,0:T(8,128)S(1)} %get-tuple-element.63.refs_2_), channel_id=1, source_target_pairs={{0,16},{4,12},{8,24},{12,4},{16,0},{20,28},{24,8},{28,20},{1,17},{... | collective-permute-start | bytes 786440 | tf_op jit(solution)/shard_map/a2/ppermute | solution.py:321
  26.8 11.2 %collective-permute-start.10 = (f32[256,256]{1,0:T(8,128)S(1)}, f32[256,256]{1,0:T(8,128)S(1)}, u32[]{:S(2)}, u32[]{:S(2)}) collective-permute-start(f32[256,256]{1,0:T(8,128)S(1)} %get-tuple-element.57.refs_1_), channel_id=1, source_target_pairs={{0,8},{4,20},{8,0},{12,28},{16,24},{20,4},{24,16},{28,12},{1,9},{5... | collective-permute-start | bytes 786440 | tf_op jit(solution)/shard_map/b1/ppermute | solution.py:321
  32.5 8.3 %collective-permute-start.11 = (f32[256,256]{1,0:T(8,128)S(1)}, f32[256,256]{1,0:T(8,128)S(1)}, u32[]{:S(2)}, u32[]{:S(2)}) collective-permute-start(f32[256,256]{1,0:T(8,128)S(1)} %get-tuple-element.65.refs_2_), channel_id=1, source_target_pairs={{0,16},{4,12},{8,24},{12,4},{16,0},{20,28},{24,8},{28,20},{1,17},{... | collective-permute-start | bytes 786440 | tf_op jit(solution)/shard_map/a3/ppermute | solution.py:321
  32.7 8.1 %collective-permute-start.12 = (f32[256,256]{1,0:T(8,128)S(1)}, f32[256,256]{1,0:T(8,128)S(1)}, u32[]{:S(2)}, u32[]{:S(2)}) collective-permute-start(f32[256,256]{1,0:T(8,128)S(1)} %get-tuple-element.61.refs_3_), channel_id=1, source_target_pairs={{0,8},{4,20},{8,0},{12,28},{16,24},{20,4},{24,16},{28,12},{1,9},{5... | collective-permute-start | bytes 786440 | tf_op jit(solution)/shard_map/d1/ppermute | solution.py:321
  34.3 9.3 %collective-permute-start.14 = (f32[256,256]{1,0:T(8,128)S(1)}, f32[256,256]{1,0:T(8,128)S(1)}, u32[]{:S(2)}, u32[]{:S(2)}) collective-permute-start(f32[256,256]{1,0:T(8,128)S(1)} %get-tuple-element.70.refs_0_), channel_id=1, source_target_pairs={{0,8},{4,20},{8,0},{12,28},{16,24},{20,4},{24,16},{28,12},{1,9},{5... | collective-permute-start | bytes 786440 | tf_op jit(solution)/shard_map/b2/ppermute | solution.py:321
  35.4 9.2 %collective-permute-start.15 = (f32[256,256]{1,0:T(8,128)S(1)}, f32[256,256]{1,0:T(8,128)S(1)}, u32[]{:S(2)}, u32[]{:S(2)}) collective-permute-start(f32[256,256]{1,0:T(8,128)S(1)} %get-tuple-element.67.refs_6_), channel_id=1, source_target_pairs={{0,3},{1,0},{2,1},{3,2},{4,7},{5,4},{6,5},{7,6},{8,11},{9,8},{10,9... | collective-permute-start | bytes 786440 | tf_op jit(solution)/shard_map/d2/ppermute | solution.py:354
  41.1 4.2 %collective-permute-start.13 = (f32[2048,256]{1,0:T(8,128)S(1)}, f32[2048,256]{1,0:T(8,128)S(1)}, u32[]{:S(2)}, u32[]{:S(2)}) collective-permute-start(f32[2048,256]{1,0:T(8,128)S(1)} %shard_map.89.mine), channel_id=1, source_target_pairs={{0,4},{4,0},{8,12},{12,8},{1,5},{5,1},{9,13},{13,9},{2,6},{6,2},{1... | collective-permute-start | bytes 6291464 | tf_op jit(solution)/shard_map/t01/ppermute | solution.py:327
  41.2 10.6 %collective-permute-start.19 = (f32[256,256]{1,0:T(8,128)S(1)}, f32[256,256]{1,0:T(8,128)S(1)}, u32[]{:S(2)}, u32[]{:S(2)}) collective-permute-start(f32[256,256]{1,0:T(8,128)S(1)} %shard_map.96.refs_2_), channel_id=1, source_target_pairs={{0,1},{1,2},{2,3},{3,0},{4,5},{5,6},{6,7},{7,4},{8,9},{9,10},{10,1... | collective-permute-start | bytes 786440 | tf_op jit(solution)/shard_map/l1/ppermute | solution.py:354
  42.4 6.4 %collective-permute-start.17 = (f32[256,256]{1,0:T(8,128)S(1)}, f32[256,256]{1,0:T(8,128)S(1)}, u32[]{:S(2)}, u32[]{:S(2)}) collective-permute-start(f32[256,256]{1,0:T(8,128)S(1)} %get-tuple-element.78.refs_0_), channel_id=1, source_target_pairs={{0,8},{4,20},{8,0},{12,28},{16,24},{20,4},{24,16},{28,12},{1,9},{5... | collective-permute-start | bytes 786440 | tf_op jit(solution)/shard_map/b3/ppermute | solution.py:321
  43.6 8.1 %collective-permute-start.18 = (f32[256,256]{1,0:T(8,128)S(1)}, f32[256,256]{1,0:T(8,128)S(1)}, u32[]{:S(2)}, u32[]{:S(2)}) collective-permute-start(f32[256,256]{1,0:T(8,128)S(1)} %get-tuple-element.79.refs_1_), channel_id=1, source_target_pairs={{0,8},{4,20},{8,0},{12,28},{16,24},{20,4},{24,16},{28,12},{1,9},{5... | collective-permute-start | bytes 786440 | tf_op jit(solution)/shard_map/d3/ppermute | solution.py:321
  45.3 6.4 %collective-permute-start.20 = (f32[512,256]{1,0:T(8,128)S(1)}, f32[512,256]{1,0:T(8,128)S(1)}, u32[]{:S(2)}, u32[]{:S(2)}) collective-permute-start(f32[512,256]{1,0:T(8,128)S(1)} %shard_map.97.refs_13_), channel_id=1, source_target_pairs={{0,4},{4,0},{8,12},{12,8},{1,5},{5,1},{9,13},{13,9},{2,6},{6,2},{1... | collective-permute-start | bytes 1572872 | tf_op jit(solution)/shard_map/tx/ppermute | solution.py:327
  48.9 7.0 %collective-permute-start.21 = (f32[768,256]{1,0:T(8,128)S(1)}, f32[768,256]{1,0:T(8,128)S(1)}, u32[]{:S(2)}, u32[]{:S(2)}) collective-permute-start(f32[768,256]{1,0:T(8,128)S(1)} %shard_map.95.refs_0_), channel_id=1, source_target_pairs={{0,4},{4,0},{8,12},{12,8},{1,5},{5,1},{9,13},{13,9},{2,6},{6,2},{1... | collective-permute-start | bytes 2359304 | tf_op jit(solution)/shard_map/t3/ppermute | solution.py:327
  52.3 13.8 %collective-permute-start.23 = (f32[256,256]{1,0:T(8,128)S(1)}, f32[256,256]{1,0:T(8,128)S(1)}, u32[]{:S(2)}, u32[]{:S(2)}) collective-permute-start(f32[256,256]{1,0:T(8,128)S(1)} %get-tuple-element.92.refs_8_), channel_id=1, source_target_pairs={{0,3},{1,0},{2,1},{3,2},{4,7},{5,4},{6,5},{7,6},{8,11},{9,8},{10,9... | collective-permute-start | bytes 786440 | tf_op jit(solution)/shard_map/l2/ppermute | solution.py:354
  55.8 12.2 %collective-permute-start.24 = (f32[256,256]{1,0:T(8,128)S(1)}, f32[256,256]{1,0:T(8,128)S(1)}, u32[]{:S(2)}, u32[]{:S(2)}) collective-permute-start(f32[256,256]{1,0:T(8,128)S(1)} %get-tuple-element.93.refs_9_), channel_id=1, source_target_pairs={{0,1},{1,2},{2,3},{3,0},{4,5},{5,6},{6,7},{7,4},{8,9},{9,10},{10,1... | collective-permute-start | bytes 786440 | tf_op jit(solution)/shard_map/l3/ppermute | solution.py:354
  69.8 8.3 %collective-permute-start.26 = (f32[256,256]{1,0:T(8,128)S(1)}, f32[256,256]{1,0:T(8,128)S(1)}, u32[]{:S(2)}, u32[]{:S(2)}) collective-permute-start(f32[256,256]{1,0:T(8,128)S(1)} %shard_map.104.own), channel_id=1, source_target_pairs={{0,16},{4,20},{8,24},{12,28},{16,0},{20,4},{24,8},{28,12},{1,17},{... | collective-permute-start | bytes 786440 | tf_op jit(solution)/shard_map/ppermute | solution.py:321
  (6 other events, 16.9 us)
